TPU v7x, 32 devices: a whole 2x2x4 slice. The times are simulated.
32 devices in a mesh: row: 8 (over z, core), col: 4 (over y, x).
Axes of the slice: x: 2, y: 2, z: 4, core: 2. Of those that a mesh axis runs over, the one named last changes fastest.
Arguments:
- pair: bfloat16 [8, 384, 384, 128], P(None, 'row', 'col'), may hold values from -6 to 6
- cotangent: bfloat16 [8, 384, 384, 128], P(None, 'row', 'col'), may hold values from -6 to 6
- residue_mask: int32 [8, 384], replicated, may hold values 0 or 1
- weights: float32 [6, 128, 128], replicated, may hold values from -0.5 to 0.5
- norm_params: float32 [4, 128], replicated, may hold values from 0.1 to 1.9
- momentum: float32 [6, 128, 128], replicated, may hold values from -320 to 320
- norm_momentum: float32 [4, 128], replicated, may hold values from -320 to 320
- average: float32 [6, 128, 128], replicated, may hold values from -0.5 to 0.5
- norm_average: float32 [4, 128], replicated, may hold values from 0.1 to 1.9
Outputs:
- new_pair: bfloat16 [8, 384, 384, 128], P(None, 'row', 'col')
- pair_grad: bfloat16 [8, 384, 384, 128], P(None, 'row', 'col')
- new_weights: float32 [6, 128, 128], replicated
- new_momentum: float32 [6, 128, 128], replicated
- new_average: float32 [6, 128, 128], replicated
- new_norms: float32 [4, 128], replicated
- new_norm_momentum: float32 [4, 128], replicated
- new_norm_average: float32 [4, 128], replicated
All inputs are finite; a program needn't handle non-finite values.
Results may differ from a plain program's by a relative error of at most 0.0089.
Values may be sent and summed in bfloat16 or wider, within the bound.
No kernel may reach another device: no remote copies, remote signals or barrier semaphores. Data moves between devices by JAX's collectives and lax.ppermute only.
A program may use at most 192 MiB of HBM per device.

v0:
```python
import math

import jax
import jax.numpy as jnp
from jax import lax
from jax.sharding import PartitionSpec as P

EPS = 1e-05
MOMENT = 0.9
DECAY = 0.8


def normalize(field):
    center = field - jnp.mean(field, axis=-1, keepdims=True)
    inverse = lax.rsqrt(jnp.mean(center * center, axis=-1, keepdims=True) + EPS)
    return (center * inverse, inverse)


def norm_back(grad_hat, normed, inverse):
    first = jnp.mean(grad_hat, axis=-1, keepdims=True)
    second = jnp.mean(grad_hat * normed, axis=-1, keepdims=True)
    return inverse * (grad_hat - first - normed * second)


def contract_rows(left_mat, right_mat):
    return lax.dot_general(
        left_mat, right_mat, (((0,), (0,)), ((), ())), preferred_element_type=jnp.float32
    )


def contract_cols(left_mat, right_mat):
    return lax.dot_general(
        left_mat, right_mat, (((1,), (1,)), ((), ())), preferred_element_type=jnp.float32
    )


def shards(
    pair,
    cotangent,
    residue_mask,
    weights,
    norm_params,
    momentum,
    norm_momentum,
    average,
    norm_average,
):
    row_count = pair.shape[1]
    col_count = pair.shape[2]
    chan_width = pair.shape[3]
    length = residue_mask.shape[1]
    crop_count = pair.shape[0]
    row_start = lax.axis_index("row") * row_count
    col_start = lax.axis_index("col") * col_count
    weight_low = weights.astype(jnp.bfloat16)
    project_low = jnp.concatenate([weight_low[index] for index in range(5)], axis=1)
    output_low = weight_low[5]

    def crop_step(carry, items):
        pair_crop, cot_crop, mask_crop = items
        pair_float = pair_crop.astype(jnp.float32)
        pair_hat, inverse_in = normalize(pair_float)
        inner = (pair_hat * norm_params[0] + norm_params[1]).astype(jnp.bfloat16)
        inner_flat = inner.reshape(-1, chan_width)
        project = jnp.dot(inner_flat, project_low, preferred_element_type=jnp.float32)
        project = project.reshape(row_count, col_count, 5, chan_width)
        mask_float = mask_crop.astype(jnp.float32)
        mask_rows = lax.dynamic_slice_in_dim(mask_float, row_start, row_count, 0)
        mask_cols = lax.dynamic_slice_in_dim(mask_float, col_start, col_count, 0)
        pair_mask = (mask_rows[:, None] * mask_cols[None, :])[:, :, None]
        left_sig = jax.nn.sigmoid(project[:, :, 1])
        right_sig = jax.nn.sigmoid(project[:, :, 3])
        gate_sig = jax.nn.sigmoid(project[:, :, 4])
        left_edge = (left_sig * project[:, :, 0] * pair_mask).astype(jnp.bfloat16)
        right_edge = (right_sig * project[:, :, 2] * pair_mask).astype(jnp.bfloat16)
        edges_all = lax.all_gather(right_edge, "row", axis=0, tiled=True)
        piece = edges_all
        product_t = lax.psum_scatter(
            jnp.einsum("ikc,jkc->jic", left_edge, piece, preferred_element_type=jnp.float32).astype(
                jnp.bfloat16
            ),
            "col",
            scatter_dimension=0,
            tiled=True,
        ).astype(jnp.float32)
        product = jnp.transpose(product_t, (1, 0, 2))
        product_hat, inverse_out = normalize(product)
        mixed = (product_hat * norm_params[2] + norm_params[3]).astype(jnp.bfloat16)
        mixed_flat = mixed.reshape(-1, chan_width)
        output = jnp.dot(mixed_flat, output_low, preferred_element_type=jnp.float32)
        output = output.reshape(row_count, col_count, chan_width)
        new_crop = (pair_float + gate_sig * output).astype(jnp.bfloat16)
        grad_out = cot_crop.astype(jnp.float32)
        grad_output = (grad_out * gate_sig).astype(jnp.bfloat16)
        grad_gate = grad_out * output * gate_sig * (1.0 - gate_sig)
        grad_output_flat = grad_output.reshape(-1, chan_width)
        grad_wout = contract_rows(mixed_flat, grad_output_flat)
        grad_mixed = contract_cols(grad_output_flat, output_low).reshape(
            row_count, col_count, chan_width
        )
        gain_out = jnp.sum(grad_mixed * product_hat, axis=(0, 1))
        bias_out = jnp.sum(grad_mixed, axis=(0, 1))
        grad_product = norm_back(grad_mixed * norm_params[2], product_hat, inverse_out).astype(
            jnp.bfloat16
        )
        grad_all = lax.all_gather(grad_product, "col", axis=1, tiled=True)
        grad_left = jnp.einsum(
            "ijc,jkc->ikc", grad_all, edges_all, preferred_element_type=jnp.float32
        )
        piece = grad_all
        grad_right = lax.psum_scatter(
            jnp.einsum("ijc,ikc->jkc", piece, left_edge, preferred_element_type=jnp.float32).astype(
                jnp.bfloat16
            ),
            "row",
            scatter_dimension=0,
            tiled=True,
        ).astype(jnp.float32)
        grad_proj = (
            jnp.stack(
                [
                    grad_left * left_sig * pair_mask,
                    grad_left * project[:, :, 0] * left_sig * (1.0 - left_sig) * pair_mask,
                    grad_right * right_sig * pair_mask,
                    grad_right * project[:, :, 2] * right_sig * (1.0 - right_sig) * pair_mask,
                    grad_gate,
                ],
                axis=2,
            )
            .astype(jnp.bfloat16)
            .reshape(-1, 5 * chan_width)
        )
        grad_wproj = contract_rows(inner_flat, grad_proj)
        grad_inner = contract_cols(grad_proj, project_low).reshape(row_count, col_count, chan_width)
        gain_in = jnp.sum(grad_inner * pair_hat, axis=(0, 1))
        bias_in = jnp.sum(grad_inner, axis=(0, 1))
        grad_pair = grad_out + norm_back(grad_inner * norm_params[0], pair_hat, inverse_in)
        grad_wproj = jnp.transpose(grad_wproj.reshape(chan_width, 5, chan_width), (1, 0, 2))
        crop_wgrad = jnp.concatenate([grad_wproj, grad_wout[None]], axis=0)
        crop_ngrad = jnp.stack([gain_in, bias_in, gain_out, bias_out], axis=0)
        summed_w, summed_n = (crop_wgrad, crop_ngrad)
        new_carry = (carry[0] + summed_w, carry[1] + summed_n)
        return (new_carry, (new_crop, grad_pair.astype(jnp.bfloat16)))

    start_carry = (jnp.zeros(weights.shape, jnp.float32), jnp.zeros(norm_params.shape, jnp.float32))
    totals, stacked = lax.scan(crop_step, start_carry, (pair, cotangent, residue_mask))
    grad_weights, grad_norms = lax.psum((totals[0], totals[1]), ("row", "col"))
    rate = 0.1 / (length * math.sqrt(crop_count))
    new_momentum = MOMENT * momentum + grad_weights
    new_weights = weights - rate * (grad_weights + MOMENT * new_momentum)
    new_average = DECAY * average + (1.0 - DECAY) * new_weights
    new_norm_momentum = MOMENT * norm_momentum + grad_norms
    new_norms = norm_params - rate * (grad_norms + MOMENT * new_norm_momentum)
    new_norm_average = DECAY * norm_average + (1.0 - DECAY) * new_norms
    return (
        stacked[0],
        stacked[1],
        new_weights,
        new_momentum,
        new_average,
        new_norms,
        new_norm_momentum,
        new_norm_average,
    )


def solution(mesh):
    return jax.shard_map(
        shards,
        mesh=mesh,
        in_specs=(
            P(None, "row", "col", None),
            P(None, "row", "col", None),
            P(),
            P(),
            P(),
            P(),
            P(),
            P(),
            P(),
        ),
        out_specs=(
            P(None, "row", "col", None),
            P(None, "row", "col", None),
            P(),
            P(),
            P(),
            P(),
            P(),
            P(),
        ),
        check_vma=False,
    )
```

profile of v0, /device:TPU:0, one launch (start us, length us, event | category | flops | bytes accessed | tf_op | source)
XLA Modules:
  0.0 3862.0 jit_solution(4807032063325257577)
XLA Ops:
  9.9 3710.4 %while.19 = (s32[]{:T(128)}, f32[6,128,128]{2,1,0:T(8,128)}, f32[4,128]{1,0:T(4,128)S(1)}, bf16[8,48,96,128]{3,2,1,0:T(8,128)(2,1)}, bf16[8,48,96,128]{3,2,1,0:T...) while((s32[]{:T(128)}, f32[6,128,128]{2,1,0:T(8,128)}, ...), condition=%wide.region_15.16_spmd.clone, body=%wide.region_0.15_spmd.clone.sunk | while | flops 4156210944 | bytes 486276000 | solution.py:146
  27.2 92.5 %all-gather.3.cloned.1.call-done = bf16[384,96,128]{2,1,0:T(8,128)(2,1)} async-done(((bf16[48,96,128]{2,1,0:T(8,128)(2,1)}), bf16[384,96,128]{2,1,0:T(8,128)(2,1)}) %all-gather.3.cloned.1.call-update) | async-done | bytes 9437200 | tf_op jit(solution)/shard_map/while/body/eval_jaxpr/all_gather | solution.py:76
  119.7 15.5 copy.126
  153.0 55.6 %reduce-scatter.3.cloned.1.call-done = bf16[96,48,128]{2,1,0:T(8,128)(2,1)} async-done(((bf16[384,48,128]{2,1,0:T(8,128)(2,1)}), bf16[96,48,128]{2,1,0:T(8,128)(2,1)}) %reduce-scatter.3.cloned.1.call-update) | async-done | bytes 1179664 | tf_op jit(solution)/shard_map/while/body/eval_jaxpr/reduce_scatter | solution.py:78
  223.6 57.2 %all-gather.5.cloned.1.call-done = bf16[48,384,128]{2,0,1:T(8,128)(2,1)} async-done(((bf16[48,96,128]{2,0,1:T(8,128)(2,1)}), bf16[48,384,128]{2,0,1:T(8,128)(2,1)}) %all-gather.5.cloned.1.call-update) | async-done | bytes 4718608 | tf_op jit(solution)/shard_map/while/body/eval_jaxpr/all_gather | solution.py:106
  296.9 14.0 copy.132
  331.2 79.5 %reduce-scatter.5.cloned.1.call-done = bf16[48,96,128]{2,1,0:T(8,128)(2,1)} async-done(((bf16[384,96,128]{2,1,0:T(8,128)(2,1)}), bf16[48,96,128]{2,1,0:T(8,128)(2,1)}) %reduce-scatter.5.cloned.1.call-update) | async-done | bytes 1179664 | tf_op jit(solution)/shard_map/while/body/eval_jaxpr/reduce_scatter | solution.py:111
  432.5 10.2 copy.133
  452.5 13.4 convert_element_type.281
  494.8 88.2 %all-gather.3.cloned.1.call-done = bf16[384,96,128]{2,1,0:T(8,128)(2,1)} async-done(((bf16[48,96,128]{2,1,0:T(8,128)(2,1)}), bf16[384,96,128]{2,1,0:T(8,128)(2,1)}) %all-gather.3.cloned.1.call-update) | async-done | bytes 9437200 | tf_op jit(solution)/shard_map/while/body/eval_jaxpr/all_gather | solution.py:76
  583.0 15.5 copy.126
  616.3 55.6 %reduce-scatter.3.cloned.1.call-done = bf16[96,48,128]{2,1,0:T(8,128)(2,1)} async-done(((bf16[384,48,128]{2,1,0:T(8,128)(2,1)}), bf16[96,48,128]{2,1,0:T(8,128)(2,1)}) %reduce-scatter.3.cloned.1.call-update) | async-done | bytes 1179664 | tf_op jit(solution)/shard_map/while/body/eval_jaxpr/reduce_scatter | solution.py:78
  686.9 57.2 %all-gather.5.cloned.1.call-done = bf16[48,384,128]{2,0,1:T(8,128)(2,1)} async-done(((bf16[48,96,128]{2,0,1:T(8,128)(2,1)}), bf16[48,384,128]{2,0,1:T(8,128)(2,1)}) %all-gather.5.cloned.1.call-update) | async-done | bytes 4718608 | tf_op jit(solution)/shard_map/while/body/eval_jaxpr/all_gather | solution.py:106
  760.2 14.0 copy.132
  794.5 79.5 %reduce-scatter.5.cloned.1.call-done = bf16[48,96,128]{2,1,0:T(8,128)(2,1)} async-done(((bf16[384,96,128]{2,1,0:T(8,128)(2,1)}), bf16[48,96,128]{2,1,0:T(8,128)(2,1)}) %reduce-scatter.5.cloned.1.call-update) | async-done | bytes 1179664 | tf_op jit(solution)/shard_map/while/body/eval_jaxpr/reduce_scatter | solution.py:111
  895.8 10.2 copy.133
  915.7 13.4 convert_element_type.281
  958.0 88.2 %all-gather.3.cloned.1.call-done = bf16[384,96,128]{2,1,0:T(8,128)(2,1)} async-done(((bf16[48,96,128]{2,1,0:T(8,128)(2,1)}), bf16[384,96,128]{2,1,0:T(8,128)(2,1)}) %all-gather.3.cloned.1.call-update) | async-done | bytes 9437200 | tf_op jit(solution)/shard_map/while/body/eval_jaxpr/all_gather | solution.py:76
  1046.2 15.5 copy.126
  1079.6 55.6 %reduce-scatter.3.cloned.1.call-done = bf16[96,48,128]{2,1,0:T(8,128)(2,1)} async-done(((bf16[384,48,128]{2,1,0:T(8,128)(2,1)}), bf16[96,48,128]{2,1,0:T(8,128)(2,1)}) %reduce-scatter.3.cloned.1.call-update) | async-done | bytes 1179664 | tf_op jit(solution)/shard_map/while/body/eval_jaxpr/reduce_scatter | solution.py:78
  1150.2 57.2 %all-gather.5.cloned.1.call-done = bf16[48,384,128]{2,0,1:T(8,128)(2,1)} async-done(((bf16[48,96,128]{2,0,1:T(8,128)(2,1)}), bf16[48,384,128]{2,0,1:T(8,128)(2,1)}) %all-gather.5.cloned.1.call-update) | async-done | bytes 4718608 | tf_op jit(solution)/shard_map/while/body/eval_jaxpr/all_gather | solution.py:106
  1223.5 14.0 copy.132
  1257.7 79.5 %reduce-scatter.5.cloned.1.call-done = bf16[48,96,128]{2,1,0:T(8,128)(2,1)} async-done(((bf16[384,96,128]{2,1,0:T(8,128)(2,1)}), bf16[48,96,128]{2,1,0:T(8,128)(2,1)}) %reduce-scatter.5.cloned.1.call-update) | async-done | bytes 1179664 | tf_op jit(solution)/shard_map/while/body/eval_jaxpr/reduce_scatter | solution.py:111
  1379.0 13.4 convert_element_type.281
  1421.3 88.2 %all-gather.3.cloned.1.call-done = bf16[384,96,128]{2,1,0:T(8,128)(2,1)} async-done(((bf16[48,96,128]{2,1,0:T(8,128)(2,1)}), bf16[384,96,128]{2,1,0:T(8,128)(2,1)}) %all-gather.3.cloned.1.call-update) | async-done | bytes 9437200 | tf_op jit(solution)/shard_map/while/body/eval_jaxpr/all_gather | solution.py:76
  1509.5 15.5 copy.126
  1542.8 55.6 %reduce-scatter.3.cloned.1.call-done = bf16[96,48,128]{2,1,0:T(8,128)(2,1)} async-done(((bf16[384,48,128]{2,1,0:T(8,128)(2,1)}), bf16[96,48,128]{2,1,0:T(8,128)(2,1)}) %reduce-scatter.3.cloned.1.call-update) | async-done | bytes 1179664 | tf_op jit(solution)/shard_map/while/body/eval_jaxpr/reduce_scatter | solution.py:78
  1613.4 57.2 %all-gather.5.cloned.1.call-done = bf16[48,384,128]{2,0,1:T(8,128)(2,1)} async-done(((bf16[48,96,128]{2,0,1:T(8,128)(2,1)}), bf16[48,384,128]{2,0,1:T(8,128)(2,1)}) %all-gather.5.cloned.1.call-update) | async-done | bytes 4718608 | tf_op jit(solution)/shard_map/while/body/eval_jaxpr/all_gather | solution.py:106
  1686.7 14.0 copy.132
  1721.0 79.5 %reduce-scatter.5.cloned.1.call-done = bf16[48,96,128]{2,1,0:T(8,128)(2,1)} async-done(((bf16[384,96,128]{2,1,0:T(8,128)(2,1)}), bf16[48,96,128]{2,1,0:T(8,128)(2,1)}) %reduce-scatter.5.cloned.1.call-update) | async-done | bytes 1179664 | tf_op jit(solution)/shard_map/while/body/eval_jaxpr/reduce_scatter | solution.py:111
  1822.3 10.2 copy.133
  1842.2 13.4 convert_element_type.281
  1884.6 88.2 %all-gather.3.cloned.1.call-done = bf16[384,96,128]{2,1,0:T(8,128)(2,1)} async-done(((bf16[48,96,128]{2,1,0:T(8,128)(2,1)}), bf16[384,96,128]{2,1,0:T(8,128)(2,1)}) %all-gather.3.cloned.1.call-update) | async-done | bytes 9437200 | tf_op jit(solution)/shard_map/while/body/eval_jaxpr/all_gather | solution.py:76
  1972.7 15.5 copy.126
  2006.1 55.6 %reduce-scatter.3.cloned.1.call-done = bf16[96,48,128]{2,1,0:T(8,128)(2,1)} async-done(((bf16[384,48,128]{2,1,0:T(8,128)(2,1)}), bf16[96,48,128]{2,1,0:T(8,128)(2,1)}) %reduce-scatter.3.cloned.1.call-update) | async-done | bytes 1179664 | tf_op jit(solution)/shard_map/while/body/eval_jaxpr/reduce_scatter | solution.py:78
  2076.7 57.2 %all-gather.5.cloned.1.call-done = bf16[48,384,128]{2,0,1:T(8,128)(2,1)} async-done(((bf16[48,96,128]{2,0,1:T(8,128)(2,1)}), bf16[48,384,128]{2,0,1:T(8,128)(2,1)}) %all-gather.5.cloned.1.call-update) | async-done | bytes 4718608 | tf_op jit(solution)/shard_map/while/body/eval_jaxpr/all_gather | solution.py:106
  2150.0 14.0 copy.132
  2184.2 79.5 %reduce-scatter.5.cloned.1.call-done = bf16[48,96,128]{2,1,0:T(8,128)(2,1)} async-done(((bf16[384,96,128]{2,1,0:T(8,128)(2,1)}), bf16[48,96,128]{2,1,0:T(8,128)(2,1)}) %reduce-scatter.5.cloned.1.call-update) | async-done | bytes 1179664 | tf_op jit(solution)/shard_map/while/body/eval_jaxpr/reduce_scatter | solution.py:111
  2285.6 10.2 copy.133
  2305.5 13.4 convert_element_type.281
  2347.8 88.2 %all-gather.3.cloned.1.call-done = bf16[384,96,128]{2,1,0:T(8,128)(2,1)} async-done(((bf16[48,96,128]{2,1,0:T(8,128)(2,1)}), bf16[384,96,128]{2,1,0:T(8,128)(2,1)}) %all-gather.3.cloned.1.call-update) | async-done | bytes 9437200 | tf_op jit(solution)/shard_map/while/body/eval_jaxpr/all_gather | solution.py:76
  2436.0 15.5 copy.126
  2469.3 55.6 %reduce-scatter.3.cloned.1.call-done = bf16[96,48,128]{2,1,0:T(8,128)(2,1)} async-done(((bf16[384,48,128]{2,1,0:T(8,128)(2,1)}), bf16[96,48,128]{2,1,0:T(8,128)(2,1)}) %reduce-scatter.3.cloned.1.call-update) | async-done | bytes 1179664 | tf_op jit(solution)/shard_map/while/body/eval_jaxpr/reduce_scatter | solution.py:78
  2539.9 57.2 %all-gather.5.cloned.1.call-done = bf16[48,384,128]{2,0,1:T(8,128)(2,1)} async-done(((bf16[48,96,128]{2,0,1:T(8,128)(2,1)}), bf16[48,384,128]{2,0,1:T(8,128)(2,1)}) %all-gather.5.cloned.1.call-update) | async-done | bytes 4718608 | tf_op jit(solution)/shard_map/while/body/eval_jaxpr/all_gather | solution.py:106
  2613.3 14.0 copy.132
  2647.5 79.5 %reduce-scatter.5.cloned.1.call-done = bf16[48,96,128]{2,1,0:T(8,128)(2,1)} async-done(((bf16[384,96,128]{2,1,0:T(8,128)(2,1)}), bf16[48,96,128]{2,1,0:T(8,128)(2,1)}) %reduce-scatter.5.cloned.1.call-update) | async-done | bytes 1179664 | tf_op jit(solution)/shard_map/while/body/eval_jaxpr/reduce_scatter | solution.py:111
  2768.8 13.4 convert_element_type.281
  2811.1 88.2 %all-gather.3.cloned.1.call-done = bf16[384,96,128]{2,1,0:T(8,128)(2,1)} async-done(((bf16[48,96,128]{2,1,0:T(8,128)(2,1)}), bf16[384,96,128]{2,1,0:T(8,128)(2,1)}) %all-gather.3.cloned.1.call-update) | async-done | bytes 9437200 | tf_op jit(solution)/shard_map/while/body/eval_jaxpr/all_gather | solution.py:76
  2899.3 15.5 copy.126
  2932.6 55.6 %reduce-scatter.3.cloned.1.call-done = bf16[96,48,128]{2,1,0:T(8,128)(2,1)} async-done(((bf16[384,48,128]{2,1,0:T(8,128)(2,1)}), bf16[96,48,128]{2,1,0:T(8,128)(2,1)}) %reduce-scatter.3.cloned.1.call-update) | async-done | bytes 1179664 | tf_op jit(solution)/shard_map/while/body/eval_jaxpr/reduce_scatter | solution.py:78
  3003.2 57.2 %all-gather.5.cloned.1.call-done = bf16[48,384,128]{2,0,1:T(8,128)(2,1)} async-done(((bf16[48,96,128]{2,0,1:T(8,128)(2,1)}), bf16[48,384,128]{2,0,1:T(8,128)(2,1)}) %all-gather.5.cloned.1.call-update) | async-done | bytes 4718608 | tf_op jit(solution)/shard_map/while/body/eval_jaxpr/all_gather | solution.py:106
  3076.5 14.0 copy.132
  3110.7 79.5 %reduce-scatter.5.cloned.1.call-done = bf16[48,96,128]{2,1,0:T(8,128)(2,1)} async-done(((bf16[384,96,128]{2,1,0:T(8,128)(2,1)}), bf16[48,96,128]{2,1,0:T(8,128)(2,1)}) %reduce-scatter.5.cloned.1.call-update) | async-done | bytes 1179664 | tf_op jit(solution)/shard_map/while/body/eval_jaxpr/reduce_scatter | solution.py:111
  3212.1 10.2 copy.133
  3232.0 13.4 convert_element_type.281
  3274.3 88.2 %all-gather.3.cloned.1.call-done = bf16[384,96,128]{2,1,0:T(8,128)(2,1)} async-done(((bf16[48,96,128]{2,1,0:T(8,128)(2,1)}), bf16[384,96,128]{2,1,0:T(8,128)(2,1)}) %all-gather.3.cloned.1.call-update) | async-done | bytes 9437200 | tf_op jit(solution)/shard_map/while/body/eval_jaxpr/all_gather | solution.py:76
  3362.5 15.5 copy.126
  3395.8 55.6 %reduce-scatter.3.cloned.1.call-done = bf16[96,48,128]{2,1,0:T(8,128)(2,1)} async-done(((bf16[384,48,128]{2,1,0:T(8,128)(2,1)}), bf16[96,48,128]{2,1,0:T(8,128)(2,1)}) %reduce-scatter.3.cloned.1.call-update) | async-done | bytes 1179664 | tf_op jit(solution)/shard_map/while/body/eval_jaxpr/reduce_scatter | solution.py:78
  3466.5 57.2 %all-gather.5.cloned.1.call-done = bf16[48,384,128]{2,0,1:T(8,128)(2,1)} async-done(((bf16[48,96,128]{2,0,1:T(8,128)(2,1)}), bf16[48,384,128]{2,0,1:T(8,128)(2,1)}) %all-gather.5.cloned.1.call-update) | async-done | bytes 4718608 | tf_op jit(solution)/shard_map/while/body/eval_jaxpr/all_gather | solution.py:106
  3539.8 14.0 copy.132
  3574.0 79.5 %reduce-scatter.5.cloned.1.call-done = bf16[48,96,128]{2,1,0:T(8,128)(2,1)} async-done(((bf16[384,96,128]{2,1,0:T(8,128)(2,1)}), bf16[48,96,128]{2,1,0:T(8,128)(2,1)}) %reduce-scatter.5.cloned.1.call-update) | async-done | bytes 1179664 | tf_op jit(solution)/shard_map/while/body/eval_jaxpr/reduce_scatter | solution.py:111
  3695.3 13.4 convert_element_type.281
  3720.9 38.0 psum.15
  3760.2 92.3 %all-reduce.2.cloned.1.call-done = f32[6,128,128]{2,1,0:T(8,128)} async-done(((f32[6,128,128]{2,1,0:T(8,128)}), f32[6,128,128]{2,1,0:T(8,128)}) %all-reduce.2.cloned.1.call-update) | async-done | bytes 393232 | tf_op jit(solution)/shard_map/psum | solution.py:147
  (875 shorter events, 1070.6 us)
Async XLA Ops:
  9.9 109.7 %all-gather.3.cloned.1.call-start = ((), (), s32[]{:S(2)}) async-start(), calls=%async_computation.3 | async-start | bytes 10616832 | tf_op jit(solution)/shard_map/while/body/eval_jaxpr/all_gather | solution.py:76
  26.1 182.6 %reduce-scatter.3.cloned.1.call-start = ((), (), s32[]{:S(2)}) async-start(), calls=%async_computation.4 | async-start | bytes 5898240 | tf_op jit(solution)/shard_map/while/body/eval_jaxpr/reduce_scatter | solution.py:78
  153.0 127.8 %all-gather.5.cloned.1.call-start = ((), (), s32[]{:S(2)}) async-start(), calls=%async_computation.5 | async-start | bytes 5898240 | tf_op jit(solution)/shard_map/while/body/eval_jaxpr/all_gather | solution.py:106
  210.9 100.1 %copy-start.20 = (f32[48,96]{1,0:T(8,128)}, f32[48,96]{1,0:T(8,128)S(1)}, u32[]{:S(2)}) copy-start(f32[48,96]{1,0:T(8,128)S(1)} %broadcast_multiply_fusion.15) | copy-start | bytes 55300 | tf_op jit(solution)/shard_map/while
  213.7 97.3 %copy-start.22 = (f32[48,96]{1,0:T(8,128)}, f32[48,96]{1,0:T(8,128)S(1)}, u32[]{:S(2)}) copy-start(f32[48,96]{1,0:T(8,128)S(1)} %add_rsqrt_fusion.5) | copy-start | bytes 55300 | tf_op jit(solution)/shard_map/while
  223.6 187.1 %reduce-scatter.5.cloned.1.call-start = ((), (), s32[]{:S(2)}) async-start(), calls=%async_computation.6 | async-start | bytes 10616832 | tf_op jit(solution)/shard_map/while/body/eval_jaxpr/reduce_scatter | solution.py:111
  432.5 10.2 copy-start.18
  452.5 13.4 copy-start.4
  477.6 105.4 %all-gather.3.cloned.1.call-start = ((), (), s32[]{:S(2)}) async-start(), calls=%async_computation.3 | async-start | bytes 10616832 | tf_op jit(solution)/shard_map/while/body/eval_jaxpr/all_gather | solution.py:76
  493.7 178.2 %reduce-scatter.3.cloned.1.call-start = ((), (), s32[]{:S(2)}) async-start(), calls=%async_computation.4 | async-start | bytes 5898240 | tf_op jit(solution)/shard_map/while/body/eval_jaxpr/reduce_scatter | solution.py:78
  616.2 127.8 %all-gather.5.cloned.1.call-start = ((), (), s32[]{:S(2)}) async-start(), calls=%async_computation.5 | async-start | bytes 5898240 | tf_op jit(solution)/shard_map/while/body/eval_jaxpr/all_gather | solution.py:106
  674.2 100.1 %copy-start.20 = (f32[48,96]{1,0:T(8,128)}, f32[48,96]{1,0:T(8,128)S(1)}, u32[]{:S(2)}) copy-start(f32[48,96]{1,0:T(8,128)S(1)} %broadcast_multiply_fusion.15) | copy-start | bytes 55300 | tf_op jit(solution)/shard_map/while
  677.0 97.3 %copy-start.22 = (f32[48,96]{1,0:T(8,128)}, f32[48,96]{1,0:T(8,128)S(1)}, u32[]{:S(2)}) copy-start(f32[48,96]{1,0:T(8,128)S(1)} %add_rsqrt_fusion.5) | copy-start | bytes 55300 | tf_op jit(solution)/shard_map/while
  686.8 187.1 %reduce-scatter.5.cloned.1.call-start = ((), (), s32[]{:S(2)}) async-start(), calls=%async_computation.6 | async-start | bytes 10616832 | tf_op jit(solution)/shard_map/while/body/eval_jaxpr/reduce_scatter | solution.py:111
  895.8 10.2 copy-start.18
  915.7 13.4 copy-start.4
  940.8 105.4 %all-gather.3.cloned.1.call-start = ((), (), s32[]{:S(2)}) async-start(), calls=%async_computation.3 | async-start | bytes 10616832 | tf_op jit(solution)/shard_map/while/body/eval_jaxpr/all_gather | solution.py:76
  957.0 178.2 %reduce-scatter.3.cloned.1.call-start = ((), (), s32[]{:S(2)}) async-start(), calls=%async_computation.4 | async-start | bytes 5898240 | tf_op jit(solution)/shard_map/while/body/eval_jaxpr/reduce_scatter | solution.py:78
  1079.5 127.8 %all-gather.5.cloned.1.call-start = ((), (), s32[]{:S(2)}) async-start(), calls=%async_computation.5 | async-start | bytes 5898240 | tf_op jit(solution)/shard_map/while/body/eval_jaxpr/all_gather | solution.py:106
  1137.5 100.1 %copy-start.20 = (f32[48,96]{1,0:T(8,128)}, f32[48,96]{1,0:T(8,128)S(1)}, u32[]{:S(2)}) copy-start(f32[48,96]{1,0:T(8,128)S(1)} %broadcast_multiply_fusion.15) | copy-start | bytes 55300 | tf_op jit(solution)/shard_map/while
  1140.2 97.3 %copy-start.22 = (f32[48,96]{1,0:T(8,128)}, f32[48,96]{1,0:T(8,128)S(1)}, u32[]{:S(2)}) copy-start(f32[48,96]{1,0:T(8,128)S(1)} %add_rsqrt_fusion.5) | copy-start | bytes 55300 | tf_op jit(solution)/shard_map/while
  1150.1 187.1 %reduce-scatter.5.cloned.1.call-start = ((), (), s32[]{:S(2)}) async-start(), calls=%async_computation.6 | async-start | bytes 10616832 | tf_op jit(solution)/shard_map/while/body/eval_jaxpr/reduce_scatter | solution.py:111
  1359.0 10.2 copy-start.18
  1379.0 13.4 copy-start.4
  1404.1 105.4 %all-gather.3.cloned.1.call-start = ((), (), s32[]{:S(2)}) async-start(), calls=%async_computation.3 | async-start | bytes 10616832 | tf_op jit(solution)/shard_map/while/body/eval_jaxpr/all_gather | solution.py:76
  1420.2 178.2 %reduce-scatter.3.cloned.1.call-start = ((), (), s32[]{:S(2)}) async-start(), calls=%async_computation.4 | async-start | bytes 5898240 | tf_op jit(solution)/shard_map/while/body/eval_jaxpr/reduce_scatter | solution.py:78
  1542.8 127.8 %all-gather.5.cloned.1.call-start = ((), (), s32[]{:S(2)}) async-start(), calls=%async_computation.5 | async-start | bytes 5898240 | tf_op jit(solution)/shard_map/while/body/eval_jaxpr/all_gather | solution.py:106
  1600.7 100.1 %copy-start.20 = (f32[48,96]{1,0:T(8,128)}, f32[48,96]{1,0:T(8,128)S(1)}, u32[]{:S(2)}) copy-start(f32[48,96]{1,0:T(8,128)S(1)} %broadcast_multiply_fusion.15) | copy-start | bytes 55300 | tf_op jit(solution)/shard_map/while
  1603.5 97.3 %copy-start.22 = (f32[48,96]{1,0:T(8,128)}, f32[48,96]{1,0:T(8,128)S(1)}, u32[]{:S(2)}) copy-start(f32[48,96]{1,0:T(8,128)S(1)} %add_rsqrt_fusion.5) | copy-start | bytes 55300 | tf_op jit(solution)/shard_map/while
  1613.4 187.1 %reduce-scatter.5.cloned.1.call-start = ((), (), s32[]{:S(2)}) async-start(), calls=%async_computation.6 | async-start | bytes 10616832 | tf_op jit(solution)/shard_map/while/body/eval_jaxpr/reduce_scatter | solution.py:111
  1822.3 10.2 copy-start.18
  1842.2 13.4 copy-start.4
  1867.3 105.4 %all-gather.3.cloned.1.call-start = ((), (), s32[]{:S(2)}) async-start(), calls=%async_computation.3 | async-start | bytes 10616832 | tf_op jit(solution)/shard_map/while/body/eval_jaxpr/all_gather | solution.py:76
  1883.5 178.2 %reduce-scatter.3.cloned.1.call-start = ((), (), s32[]{:S(2)}) async-start(), calls=%async_computation.4 | async-start | bytes 5898240 | tf_op jit(solution)/shard_map/while/body/eval_jaxpr/reduce_scatter | solution.py:78
  2006.0 127.8 %all-gather.5.cloned.1.call-start = ((), (), s32[]{:S(2)}) async-start(), calls=%async_computation.5 | async-start | bytes 5898240 | tf_op jit(solution)/shard_map/while/body/eval_jaxpr/all_gather | solution.py:106
  2064.0 100.1 %copy-start.20 = (f32[48,96]{1,0:T(8,128)}, f32[48,96]{1,0:T(8,128)S(1)}, u32[]{:S(2)}) copy-start(f32[48,96]{1,0:T(8,128)S(1)} %broadcast_multiply_fusion.15) | copy-start | bytes 55300 | tf_op jit(solution)/shard_map/while
  2066.7 97.3 %copy-start.22 = (f32[48,96]{1,0:T(8,128)}, f32[48,96]{1,0:T(8,128)S(1)}, u32[]{:S(2)}) copy-start(f32[48,96]{1,0:T(8,128)S(1)} %add_rsqrt_fusion.5) | copy-start | bytes 55300 | tf_op jit(solution)/shard_map/while
  2076.6 187.1 %reduce-scatter.5.cloned.1.call-start = ((), (), s32[]{:S(2)}) async-start(), calls=%async_computation.6 | async-start | bytes 10616832 | tf_op jit(solution)/shard_map/while/body/eval_jaxpr/reduce_scatter | solution.py:111
  2285.6 10.2 copy-start.18
  2305.5 13.4 copy-start.4
  2330.6 105.4 %all-gather.3.cloned.1.call-start = ((), (), s32[]{:S(2)}) async-start(), calls=%async_computation.3 | async-start | bytes 10616832 | tf_op jit(solution)/shard_map/while/body/eval_jaxpr/all_gather | solution.py:76
  2346.7 178.2 %reduce-scatter.3.cloned.1.call-start = ((), (), s32[]{:S(2)}) async-start(), calls=%async_computation.4 | async-start | bytes 5898240 | tf_op jit(solution)/shard_map/while/body/eval_jaxpr/reduce_scatter | solution.py:78
  2469.3 127.8 %all-gather.5.cloned.1.call-start = ((), (), s32[]{:S(2)}) async-start(), calls=%async_computation.5 | async-start | bytes 5898240 | tf_op jit(solution)/shard_map/while/body/eval_jaxpr/all_gather | solution.py:106
  2527.2 100.1 %copy-start.20 = (f32[48,96]{1,0:T(8,128)}, f32[48,96]{1,0:T(8,128)S(1)}, u32[]{:S(2)}) copy-start(f32[48,96]{1,0:T(8,128)S(1)} %broadcast_multiply_fusion.15) | copy-start | bytes 55300 | tf_op jit(solution)/shard_map/while
  2530.0 97.3 %copy-start.22 = (f32[48,96]{1,0:T(8,128)}, f32[48,96]{1,0:T(8,128)S(1)}, u32[]{:S(2)}) copy-start(f32[48,96]{1,0:T(8,128)S(1)} %add_rsqrt_fusion.5) | copy-start | bytes 55300 | tf_op jit(solution)/shard_map/while
  2539.9 187.1 %reduce-scatter.5.cloned.1.call-start = ((), (), s32[]{:S(2)}) async-start(), calls=%async_computation.6 | async-start | bytes 10616832 | tf_op jit(solution)/shard_map/while/body/eval_jaxpr/reduce_scatter | solution.py:111
  2748.8 10.2 copy-start.18
  2768.8 13.4 copy-start.4
  2793.8 105.4 %all-gather.3.cloned.1.call-start = ((), (), s32[]{:S(2)}) async-start(), calls=%async_computation.3 | async-start | bytes 10616832 | tf_op jit(solution)/shard_map/while/body/eval_jaxpr/all_gather | solution.py:76
  2810.0 178.2 %reduce-scatter.3.cloned.1.call-start = ((), (), s32[]{:S(2)}) async-start(), calls=%async_computation.4 | async-start | bytes 5898240 | tf_op jit(solution)/shard_map/while/body/eval_jaxpr/reduce_scatter | solution.py:78
  2932.5 127.8 %all-gather.5.cloned.1.call-start = ((), (), s32[]{:S(2)}) async-start(), calls=%async_computation.5 | async-start | bytes 5898240 | tf_op jit(solution)/shard_map/while/body/eval_jaxpr/all_gather | solution.py:106
  2990.5 100.1 %copy-start.20 = (f32[48,96]{1,0:T(8,128)}, f32[48,96]{1,0:T(8,128)S(1)}, u32[]{:S(2)}) copy-start(f32[48,96]{1,0:T(8,128)S(1)} %broadcast_multiply_fusion.15) | copy-start | bytes 55300 | tf_op jit(solution)/shard_map/while
  2993.3 97.3 %copy-start.22 = (f32[48,96]{1,0:T(8,128)}, f32[48,96]{1,0:T(8,128)S(1)}, u32[]{:S(2)}) copy-start(f32[48,96]{1,0:T(8,128)S(1)} %add_rsqrt_fusion.5) | copy-start | bytes 55300 | tf_op jit(solution)/shard_map/while
  3003.1 187.1 %reduce-scatter.5.cloned.1.call-start = ((), (), s32[]{:S(2)}) async-start(), calls=%async_computation.6 | async-start | bytes 10616832 | tf_op jit(solution)/shard_map/while/body/eval_jaxpr/reduce_scatter | solution.py:111
  3212.1 10.2 copy-start.18
  3232.0 13.4 copy-start.4
  3257.1 105.4 %all-gather.3.cloned.1.call-start = ((), (), s32[]{:S(2)}) async-start(), calls=%async_computation.3 | async-start | bytes 10616832 | tf_op jit(solution)/shard_map/while/body/eval_jaxpr/all_gather | solution.py:76
  3273.3 178.2 %reduce-scatter.3.cloned.1.call-start = ((), (), s32[]{:S(2)}) async-start(), calls=%async_computation.4 | async-start | bytes 5898240 | tf_op jit(solution)/shard_map/while/body/eval_jaxpr/reduce_scatter | solution.py:78
  3395.8 127.8 %all-gather.5.cloned.1.call-start = ((), (), s32[]{:S(2)}) async-start(), calls=%async_computation.5 | async-start | bytes 5898240 | tf_op jit(solution)/shard_map/while/body/eval_jaxpr/all_gather | solution.py:106
  3453.8 100.1 %copy-start.20 = (f32[48,96]{1,0:T(8,128)}, f32[48,96]{1,0:T(8,128)S(1)}, u32[]{:S(2)}) copy-start(f32[48,96]{1,0:T(8,128)S(1)} %broadcast_multiply_fusion.15) | copy-start | bytes 55300 | tf_op jit(solution)/shard_map/while
  3456.5 97.3 %copy-start.22 = (f32[48,96]{1,0:T(8,128)}, f32[48,96]{1,0:T(8,128)S(1)}, u32[]{:S(2)}) copy-start(f32[48,96]{1,0:T(8,128)S(1)} %add_rsqrt_fusion.5) | copy-start | bytes 55300 | tf_op jit(solution)/shard_map/while
  3466.4 187.1 %reduce-scatter.5.cloned.1.call-start = ((), (), s32[]{:S(2)}) async-start(), calls=%async_computation.6 | async-start | bytes 10616832 | tf_op jit(solution)/shard_map/while/body/eval_jaxpr/reduce_scatter | solution.py:111
  3695.3 13.4 copy-start.4
  3720.3 132.1 %all-reduce.2.cloned.1.call-start = ((), (), s32[]{:S(2)}) async-start(), calls=%async_computation.2 | async-start | bytes 786432 | tf_op jit(solution)/shard_map/psum | solution.py:147
  (201 other events, 974.3 us)
Sparse Core Ops, SparseCore 0:
  26.2 93.4 all-gather.2
  153.1 55.5 reduce-scatter.2
  223.7 57.0 all-gather.4
  311.1 99.5 reduce-scatter.4
  493.8 89.0 all-gather.2
  616.4 55.5 reduce-scatter.2
  687.0 57.0 all-gather.4
  774.4 99.5 reduce-scatter.4
  957.1 89.0 all-gather.2
  1079.6 55.5 reduce-scatter.2
  1150.2 57.0 all-gather.4
  1237.6 99.5 reduce-scatter.4
  1420.3 89.0 all-gather.2
  1542.9 55.5 reduce-scatter.2
  1613.5 57.0 all-gather.4
  1700.9 99.5 reduce-scatter.4
  1883.6 89.0 all-gather.2
  2006.1 55.5 reduce-scatter.2
  2076.7 57.0 all-gather.4
  2164.1 99.5 reduce-scatter.4
  2346.9 89.0 all-gather.2
  2469.4 55.5 reduce-scatter.2
  2540.0 57.0 all-gather.4
  2627.4 99.5 reduce-scatter.4
  2810.1 89.0 all-gather.2
  2932.7 55.5 reduce-scatter.2
  3003.3 57.0 all-gather.4
  3090.7 99.5 reduce-scatter.4
  3273.4 89.0 all-gather.2
  3395.9 55.5 reduce-scatter.2
  3466.5 57.0 all-gather.4
  3553.9 99.5 reduce-scatter.4
Sparse Core Ops, SparseCore 1:
  3726.7 125.7 all-reduce.1
where the time goes:
time: 3880 us; the launch traced here: 3860 us
  waiting for transfers between devices  2340 us (60%)
  local copies, waits for them, and re-layouts  682 us (18%)
  matrix products  424 us (11%)
  other arithmetic  357 us (9%)
    all_gather x8, waiting for transfers between devices, crop_step(): edges_all = lax.all_gather(right_edge, 'row', axis=0, tiled=True)  710 us
    reduce_scatter x8, waiting for transfers between devices, crop_step(): lax.psum_scatter(jnp.einsum('ijc,ikc->jkc', piece, left_edge, preferred_e...  636 us
    all_gather x8, waiting for transfers between devices, crop_step(): grad_all = lax.all_gather(grad_product, 'col', axis=1, tiled=True)  457 us
    reduce_scatter x8, waiting for transfers between devices, crop_step(): lax.psum_scatter(jnp.einsum('ikc,jkc->jic', left_edge, piece, preferred_e...  445 us
    convert_element_type x24, local copies, waits for them, and re-layouts, crop_step(): grad_proj = jnp.stack([grad_left * left_sig * pair_mask, grad_left * proj...  267 us
    all_gather x8, local copies, waits for them, and re-layouts, crop_step(): edges_all = lax.all_gather(right_edge, 'row', axis=0, tiled=True)  124 us
    while x32, other arithmetic  117 us
    dot_general x8, local copies, waits for them, and re-layouts, crop_step(): jnp.einsum('ijc,ikc->jkc', piece, left_edge, preferred_element_type=jnp.f...  112 us
  transfers between devices with their start and end apart: 33, of which 33 were waited for; matrix products, arithmetic and copies ran while one was open for 4% of the time, Pallas kernels for 0%

commit v1 on v0

v1 whole, which is shorter than its diff:
```python
import math

import jax
import jax.numpy as jnp
from jax import lax
from jax.experimental import pallas as pl
from jax.experimental.pallas import tpu as pltpu
from jax.sharding import PartitionSpec as P

EPS = 1e-05
MOMENT = 0.9
DECAY = 0.8
LOW = jnp.bfloat16
F32 = jnp.float32
MIB = 1 << 20
COST = 1.0


def sds(shape, dtype):
    return jax.ShapeDtypeStruct(shape, dtype)


def params(mib):
    return pltpu.CompilerParams(vmem_limit_bytes=mib * MIB)


def cost(flops, moved):
    return pl.CostEstimate(flops=int(flops * COST), bytes_accessed=int(moved * COST),
                           transcendentals=0)


def sigmoid(v):
    return 0.5 * jnp.tanh(0.5 * v) + 0.5


def normalize(v):
    center = v - jnp.mean(v, axis=-1, keepdims=True)
    inverse = lax.rsqrt(jnp.mean(center * center, axis=-1, keepdims=True) + EPS)
    return center * inverse, inverse


def norm_back(grad_hat, normed, inverse):
    first = jnp.mean(grad_hat, axis=-1, keepdims=True)
    second = jnp.mean(grad_hat * normed, axis=-1, keepdims=True)
    return inverse * (grad_hat - first - normed * second)


def dot(a, b, ca=1, cb=0):
    return lax.dot_general(a, b, (((ca,), (cb,)), ((), ())), preferred_element_type=F32)


def eights(v):
    return jnp.sum(v.reshape(-1, 8, v.shape[-1]), axis=0)


def to_major(v):
    return jnp.swapaxes(jnp.swapaxes(v, 1, 2), 0, 1)


def to_minor(v):
    return jnp.swapaxes(jnp.swapaxes(v, 0, 1), 1, 2)


def row_mask(rowm, colm, start, count):
    m = rowm[pl.ds(start, count)][:, None, :] * colm[...][None]
    return m.reshape(-1, m.shape[-1])


def pick_rows(nrow):
    return 16 if nrow % 16 == 0 else 8


def fold(nblocks, refs, dst):
    for d in range(nblocks):
        @pl.when(pl.program_id(0) == d)
        def _(d=d):
            dst[...] = refs[d][...]


def clamp_map(d, steps):
    def index(g, r, *_):
        return (jnp.where(g == d, r, jnp.where(g < d, 0, steps - 1)), 0, 0)
    return index


def edges_kernel(nblocks, sub, *refs):
    zs, (norms, proj, rowm, colm, left, right, tile) = refs[:nblocks], refs[nblocks:]
    rows, nk, chan = tile.shape
    fold(nblocks, zs, tile)
    base = (pl.program_id(0) * pl.num_programs(1) + pl.program_id(1)) * rows

    def step(t, _):
        at = t * sub
        z = tile[pl.ds(at, sub)].astype(F32).reshape(-1, chan)
        hat, _ = normalize(z)
        u = (hat * norms[0:1] + norms[1:2]).astype(LOW)
        p = dot(u, proj[...])
        m = row_mask(rowm, colm, base + at, sub)
        lv = sigmoid(p[:, chan:2 * chan]) * p[:, :chan] * m
        rv = sigmoid(p[:, 3 * chan:]) * p[:, 2 * chan:3 * chan] * m
        left[pl.ds(at, sub)] = lv.astype(LOW).reshape(sub, nk, chan)
        right[pl.ds(at, sub)] = rv.astype(LOW).reshape(sub, nk, chan)
        return 0

    lax.fori_loop(0, rows // sub, step, 0)


def edges_call(zs, norms, proj, rowm, colm):
    nblocks = len(zs)
    nrow, nk, chan = zs[0].shape
    rows = pick_rows(nrow)
    steps = nrow // rows
    whole = lambda shape: pl.BlockSpec(shape, lambda g, r: (0,) * len(shape))
    flat = pl.BlockSpec((rows, nk, chan), lambda g, r: (g * steps + r, 0, 0))
    cells = nblocks * nrow * nk
    return pl.pallas_call(
        lambda *refs: edges_kernel(nblocks, 4, *refs),
        grid=(nblocks, steps),
        in_specs=[pl.BlockSpec((rows, nk, chan), clamp_map(d, steps)) for d in range(nblocks)]
        + [whole(norms.shape), whole(proj.shape), whole(rowm.shape), whole(colm.shape)],
        out_specs=[flat, flat],
        out_shape=[sds((nblocks * nrow, nk, chan), LOW)] * 2,
        scratch_shapes=[pltpu.VMEM((rows, nk, chan), LOW)],
        compiler_params=params(32),
        cost_estimate=cost(cells * chan * chan * 8, cells * chan * 6),
        name="edges",
    )(*zs, norms, proj, rowm, colm)


def product_kernel(nparts, unroll, sc, left, own, other, *refs):
    outs, (lt, rt, xt) = refs[:nparts], refs[nparts:]
    s = pl.program_id(0)
    rows, nk, chan = left.shape
    chunk = pick_rows(rows)
    half = nparts * rows
    core = sc[0]

    @pl.when(s < nparts)
    def _():
        def move(t, _):
            at = pl.multiple_of(t * chunk, chunk)
            to = s * rows + at
            lt[:, pl.ds(pl.multiple_of(to, chunk), chunk), :] = to_major(left[pl.ds(at, chunk)])
            rt[:, pl.ds(pl.multiple_of(core * half + to, chunk), chunk), :] = to_major(
                own[0, pl.ds(at, chunk)])
            rt[:, pl.ds(pl.multiple_of((1 - core) * half + to, chunk), chunk), :] = to_major(
                other[0, pl.ds(at, chunk)])
            return 0
        lax.fori_loop(0, rows // chunk, move, 0)

    @pl.when(s == nparts)
    def _():
        def multiply(c, _):
            xt[c] = dot(lt[c], rt[c], 1, 1).astype(LOW)
            return 0
        lax.fori_loop(0, chan, multiply, 0, unroll=unroll)

    @pl.when(s >= nparts)
    def _():
        def move(t, _):
            at = pl.multiple_of(t * chunk, chunk)
            x = to_minor(xt[:, pl.ds(pl.multiple_of((s - nparts) * rows + at, chunk), chunk), :])
            for e in range(nparts):
                for core in range(2):
                    start = core * half + e * rows
                    outs[e][pl.ds(at, chunk), core * rows:(core + 1) * rows] = (
                        x[:, start:start + rows])
            return 0
        lax.fori_loop(0, rows // chunk, move, 0)


def product_call(scal, left, own, other):
    nparts, rows, nk, chan = own.shape
    ni, nj = nparts * rows, 2 * nparts * rows
    last = nparts - 1
    edge = pl.BlockSpec((1, rows, nk, chan),
                        lambda s, sc: (sc[1 + jnp.minimum(s, last)], 0, 0, 0))
    return pl.pallas_call(
        lambda *refs: product_kernel(nparts, 4, *refs),
        grid_spec=pltpu.PrefetchScalarGridSpec(
            num_scalar_prefetch=1,
            grid=(2 * nparts,),
            in_specs=[pl.BlockSpec((rows, nk, chan), lambda s, sc: (jnp.minimum(s, last), 0, 0)),
                      edge, edge],
            out_specs=[pl.BlockSpec((rows, 2 * rows, chan),
                                    lambda s, sc: (jnp.maximum(s - nparts, 0), 0, 0))] * nparts,
            scratch_shapes=[pltpu.VMEM((chan, ni, nk), LOW), pltpu.VMEM((chan, nj, nk), LOW),
                            pltpu.VMEM((chan, ni, nj), LOW)],
        ),
        out_shape=[sds((ni, 2 * rows, chan), LOW)] * nparts,
        compiler_params=params(60),
        cost_estimate=cost(2 * ni * nj * nk * chan * 8, 14 * ni * nk * chan),
        name="product",
    )(scal, left, own, other)


def middle_kernel(nblocks, nparts, sub, *refs):
    zs, refs = refs[:nblocks], refs[nblocks:]
    gs, refs = refs[:nblocks], refs[nblocks:]
    xs, refs = refs[:nparts], refs[nparts:]
    (norms, gate_w, out_w), refs = refs[:3], refs[3:]
    news, refs = refs[:nblocks], refs[nblocks:]
    gx, gate_grad, wout, nout, ztile, gtile, ntile, ylow, glow = refs
    rows, nk, chan = ztile.shape
    fold(nblocks, zs, ztile)
    fold(nblocks, gs, gtile)

    @pl.when((pl.program_id(0) == 0) & (pl.program_id(1) == 0))
    def _():
        wout[...] = jnp.zeros_like(wout)
        nout[...] = jnp.zeros_like(nout)

    def step(t, _):
        rng = pl.ds(t * sub, sub)
        flat = pl.ds(pl.multiple_of(t * sub * nk, sub * nk), sub * nk)
        z = ztile[rng].astype(F32).reshape(-1, chan)
        zhat, _ = normalize(z)
        u = (zhat * norms[0:1] + norms[1:2]).astype(LOW)
        gate = sigmoid(dot(u, gate_w[...]))
        x = xs[0][rng].astype(F32)
        for other in xs[1:]:
            x = x + other[rng].astype(F32)
        hat, inverse = normalize(x.reshape(-1, chan))
        y = (hat * norms[2:3] + norms[3:4]).astype(LOW)
        out = dot(y, out_w[...])
        so = gate * out
        ntile[rng] = (z + so).astype(LOW).reshape(sub, nk, chan)
        g = gtile[rng].astype(F32).reshape(-1, chan)
        go = (g * gate).astype(LOW)
        gate_grad[rng] = (g * so * (1.0 - gate)).astype(LOW).reshape(sub, nk, chan)
        ylow[flat] = y
        glow[flat] = go
        gy = dot(go, out_w[...], 1, 1)
        nout[0] += eights(gy * hat)
        nout[1] += eights(gy)
        gx[rng] = norm_back(gy * norms[2:3], hat, inverse).astype(LOW).reshape(sub, nk, chan)
        return 0

    lax.fori_loop(0, rows // sub, step, 0)
    wout[...] += dot(ylow[...], glow[...], 0, 0)
    for d in range(nblocks):
        @pl.when(pl.program_id(0) == d)
        def _(d=d):
            news[d][...] = ntile[...]


def middle_call(zs, gs, xs, norms, gate_w, out_w):
    nblocks, nparts = len(zs), len(xs)
    nrow, nk, chan = zs[0].shape
    rows = pick_rows(nrow)
    steps = nrow // rows
    whole = lambda shape: pl.BlockSpec(shape, lambda g, r: (0,) * len(shape))
    flat = pl.BlockSpec((rows, nk, chan), lambda g, r: (g * steps + r, 0, 0))
    block = [pl.BlockSpec((rows, nk, chan), clamp_map(d, steps)) for d in range(nblocks)]
    cells = nblocks * nrow * nk
    tile = pltpu.VMEM((rows, nk, chan), LOW)
    low = pltpu.VMEM((rows * nk, chan), LOW)
    return pl.pallas_call(
        lambda *refs: middle_kernel(nblocks, nparts, 4, *refs),
        grid=(nblocks, steps),
        in_specs=block + block + [flat] * nparts
        + [whole(norms.shape), whole(gate_w.shape), whole(out_w.shape)],
        out_specs=block + [flat, flat, whole((chan, chan)), whole((2, 8, chan))],
        out_shape=[sds((nrow, nk, chan), LOW)] * nblocks
        + [sds((nblocks * nrow, nk, chan), LOW)] * 2
        + [sds((chan, chan), F32), sds((2, 8, chan), F32)],
        scratch_shapes=[tile, tile, tile, low, low],
        compiler_params=params(40),
        cost_estimate=cost(cells * chan * chan * 8, cells * chan * 18),
        name="middle",
    )(*zs, *gs, *xs, norms, gate_w, out_w)


def edge_grad_kernel(nparts, unroll, sc, left, own, other, *refs):
    gxs, (gleft, keep, send, lt, rt, gt) = refs[:nparts], refs[nparts:]
    s = pl.program_id(0)
    rows, nk, chan = left.shape
    chunk = pick_rows(rows)
    half = nparts * rows
    core = sc[0]

    @pl.when(s < nparts)
    def _():
        def move(t, _):
            at = pl.multiple_of(t * chunk, chunk)
            to = s * rows + at
            to_l = pl.multiple_of(to, chunk)
            lt[:, pl.ds(to_l, chunk), :] = to_major(left[pl.ds(at, chunk)])
            rt[:, pl.ds(pl.multiple_of(core * half + to, chunk), chunk), :] = to_major(
                own[0, pl.ds(at, chunk)])
            rt[:, pl.ds(pl.multiple_of((1 - core) * half + to, chunk), chunk), :] = to_major(
                other[0, pl.ds(at, chunk)])
            g = jnp.concatenate([
                gxs[e][pl.ds(at, chunk), c * rows:(c + 1) * rows]
                for c in range(2) for e in range(nparts)
            ], axis=1)
            gt[:, pl.ds(to_l, chunk), :] = to_major(g)
            return 0
        lax.fori_loop(0, rows // chunk, move, 0)

    @pl.when(s == nparts)
    def _():
        def multiply(c, _):
            lc, rc, gc = lt[c], rt[c], gt[c]
            lt[c] = dot(gc, rc, 1, 0).astype(LOW)
            rt[c] = dot(gc, lc, 0, 0).astype(LOW)
            return 0
        lax.fori_loop(0, chan, multiply, 0, unroll=unroll)

    @pl.when(s >= nparts)
    def _():
        def move(t, _):
            at = pl.multiple_of(t * chunk, chunk)
            to = (s - nparts) * rows + at
            gleft[pl.ds(at, chunk)] = to_minor(lt[:, pl.ds(pl.multiple_of(to, chunk), chunk), :])
            keep[0, pl.ds(at, chunk)] = to_minor(
                rt[:, pl.ds(pl.multiple_of(core * half + to, chunk), chunk), :])
            send[0, pl.ds(at, chunk)] = to_minor(
                rt[:, pl.ds(pl.multiple_of((1 - core) * half + to, chunk), chunk), :])
            return 0
        lax.fori_loop(0, rows // chunk, move, 0)


def edge_grad_call(scal, left, own, other, gxs):
    nparts, rows, nk, chan = own.shape
    ni, nj = nparts * rows, 2 * nparts * rows
    last = nparts - 1
    edge = pl.BlockSpec((1, rows, nk, chan),
                        lambda s, sc: (sc[1 + jnp.minimum(s, last)], 0, 0, 0))
    back = pl.BlockSpec((1, rows, nk, chan),
                        lambda s, sc: (sc[1 + jnp.maximum(s - nparts, 0)], 0, 0, 0))
    first = lambda s, sc: (jnp.minimum(s, last), 0, 0)
    return pl.pallas_call(
        lambda *refs: edge_grad_kernel(nparts, 4, *refs),
        grid_spec=pltpu.PrefetchScalarGridSpec(
            num_scalar_prefetch=1,
            grid=(2 * nparts,),
            in_specs=[pl.BlockSpec((rows, nk, chan), first), edge, edge]
            + [pl.BlockSpec((rows, 2 * rows, chan), first)] * nparts,
            out_specs=[pl.BlockSpec((rows, nk, chan),
                                    lambda s, sc: (jnp.maximum(s - nparts, 0), 0, 0)), back, back],
            scratch_shapes=[pltpu.VMEM((chan, ni, nk), LOW), pltpu.VMEM((chan, nj, nk), LOW),
                            pltpu.VMEM((chan, ni, nj), LOW)],
        ),
        out_shape=[sds((ni, nk, chan), LOW), sds((nparts, rows, nk, chan), LOW),
                   sds((nparts, rows, nk, chan), LOW)],
        compiler_params=params(62),
        cost_estimate=cost(4 * ni * nj * nk * chan * 8, 14 * ni * nk * chan),
        name="edge_grad",
    )(scal, left, own, other, *gxs)


def input_kernel(nblocks, sub, *refs):
    zs, refs = refs[:nblocks], refs[nblocks:]
    gs, refs = refs[:nblocks], refs[nblocks:]
    (gleft, keep, got, gate_grad, norms, proj, rowm, colm), refs = refs[:8], refs[8:]
    outs, refs = refs[:nblocks], refs[nblocks:]
    wproj, nin, ztile, gtile, otile, ulow, plow = refs
    rows, nk, chan = ztile.shape
    fold(nblocks, zs, ztile)
    fold(nblocks, gs, gtile)
    base = (pl.program_id(0) * pl.num_programs(1) + pl.program_id(1)) * rows

    @pl.when((pl.program_id(0) == 0) & (pl.program_id(1) == 0))
    def _():
        wproj[...] = jnp.zeros_like(wproj)
        nin[...] = jnp.zeros_like(nin)

    def step(t, _):
        at = t * sub
        rng = pl.ds(at, sub)
        flat = pl.ds(pl.multiple_of(at * nk, sub * nk), sub * nk)
        z = ztile[rng].astype(F32).reshape(-1, chan)
        hat, inverse = normalize(z)
        u = (hat * norms[0:1] + norms[1:2]).astype(LOW)
        ulow[flat] = u
        p = dot(u, proj[:, :4 * chan])
        m = row_mask(rowm, colm, base + at, sub)
        gl = gleft[rng].astype(F32).reshape(-1, chan) * m
        gr = (keep[rng].astype(F32) + got[rng].astype(F32)).reshape(-1, chan) * m
        for n, grad in ((0, gl), (2, gr)):
            sig = sigmoid(p[:, (n + 1) * chan:(n + 2) * chan])
            first = grad * sig
            plow[flat, n * chan:(n + 1) * chan] = first.astype(LOW)
            second = first * (p[:, n * chan:(n + 1) * chan] * (1.0 - sig))
            plow[flat, (n + 1) * chan:(n + 2) * chan] = second.astype(LOW)
        plow[flat, 4 * chan:] = gate_grad[rng].reshape(-1, chan)
        gu = dot(plow[flat], proj[...], 1, 1)
        nin[0] += eights(gu * hat)
        nin[1] += eights(gu)
        g = gtile[rng].astype(F32).reshape(-1, chan)
        grad_z = g + norm_back(gu * norms[0:1], hat, inverse)
        otile[rng] = grad_z.astype(LOW).reshape(sub, nk, chan)
        return 0

    lax.fori_loop(0, rows // sub, step, 0)
    wproj[...] += dot(ulow[...], plow[...], 0, 0)
    for d in range(nblocks):
        @pl.when(pl.program_id(0) == d)
        def _(d=d):
            outs[d][...] = otile[...]


def input_call(zs, gs, gleft, keep, got, gate_grad, norms, proj, rowm, colm):
    nblocks = len(zs)
    nrow, nk, chan = zs[0].shape
    rows = pick_rows(nrow)
    steps = nrow // rows
    whole = lambda shape: pl.BlockSpec(shape, lambda g, r: (0,) * len(shape))
    flat = pl.BlockSpec((rows, nk, chan), lambda g, r: (g * steps + r, 0, 0))
    block = [pl.BlockSpec((rows, nk, chan), clamp_map(d, steps)) for d in range(nblocks)]
    cells = nblocks * nrow * nk
    width = proj.shape[1]
    tile = pltpu.VMEM((rows, nk, chan), LOW)
    return pl.pallas_call(
        lambda *refs: input_kernel(nblocks, 4, *refs),
        grid=(nblocks, steps),
        in_specs=block + block + [flat] * 4
        + [whole(norms.shape), whole(proj.shape), whole(rowm.shape), whole(colm.shape)],
        out_specs=block + [whole((chan, width)), whole((2, 8, chan))],
        out_shape=[sds((nrow, nk, chan), LOW)] * nblocks
        + [sds((chan, width), F32), sds((2, 8, chan), F32)],
        scratch_shapes=[tile, tile, tile, pltpu.VMEM((rows * nk, chan), LOW),
                        pltpu.VMEM((rows * nk, width), LOW)],
        compiler_params=params(40),
        cost_estimate=cost(cells * chan * chan * 28, cells * chan * 14),
        name="input_grad",
    )(*zs, *gs, gleft, keep, got, gate_grad, norms, proj, rowm, colm)


def place_call(scal, pieces, whole=None, shape=None):
    count = len(pieces)
    fresh = whole is None
    nrow, nk, chan = pieces[0].shape
    rows = pick_rows(nrow)
    steps = nrow // rows

    def kernel(*refs):
        blocks, out = refs[1:1 + count], refs[-1]
        for n in range(count):
            @pl.when(pl.program_id(0) == n)
            def _(n=n):
                out[0] = blocks[n][...]

    args = [scal, *pieces] + ([] if fresh else [whole])
    return pl.pallas_call(
        kernel,
        grid_spec=pltpu.PrefetchScalarGridSpec(
            num_scalar_prefetch=1,
            grid=(count, steps),
            in_specs=[pl.BlockSpec((rows, nk, chan), clamp_map(n, steps)) for n in range(count)]
            + [pl.BlockSpec(memory_space=pl.ANY)] * (0 if fresh else 1),
            out_specs=pl.BlockSpec((1, rows, nk, chan), lambda g, r, sc: (sc[g], r, 0, 0)),
        ),
        out_shape=sds(shape if fresh else whole.shape, LOW),
        input_output_aliases={} if fresh else {len(args) - 1: 0},
        compiler_params=params(32),
        cost_estimate=cost(0, 4 * count * nrow * nk * chan),
        name="place",
    )(*args)


def shards(rows, cols, pair, cotangent, residue_mask, weights, norm_params, momentum,
           norm_momentum, average, norm_average):
    zeds = rows // 2
    crops, nrow, ncol, chan = pair.shape
    batches = crops // zeds
    length = residue_mask.shape[1]
    row = lax.axis_index("row")
    col = lax.axis_index("col")
    zed, core = row // 2, row % 2
    weight_low = weights.astype(LOW)
    project_low = jnp.concatenate([weight_low[n] for n in range(5)], axis=1)
    mask_float = residue_mask.astype(F32)
    scal = jnp.stack([core] + [zed ^ col ^ e for e in range(cols)]).astype(jnp.int32)

    def zswap(block, d):
        if d == 0:
            return block
        return lax.ppermute(block, "row", [(r, r ^ (2 * d)) for r in range(rows)])

    def cswap(block, e):
        if e == 0:
            return block
        return lax.ppermute(block, "col", [(q, q ^ e) for q in range(cols)])

    def coreswap(block):
        return lax.ppermute(block, "row", [(r, r ^ 1) for r in range(rows)])

    def fetch(whole, b):
        return [
            zswap(lax.dynamic_index_in_dim(whole, (zed ^ d) * batches + b, 0, keepdims=False), d)
            for d in range(zeds)
        ]

    def blocked(v):
        return v.reshape(zeds, nrow, ncol, chan)

    masks = []
    for b in range(batches):
        crop_mask = lax.dynamic_index_in_dim(mask_float, zed * batches + b, 0, keepdims=False)
        rowm = jnp.concatenate([
            lax.dynamic_slice_in_dim(crop_mask, ((zed ^ d) * 2 + core) * nrow, nrow, 0)
            for d in range(zeds)
        ])
        colm = lax.dynamic_slice_in_dim(crop_mask, col * ncol, ncol, 0)
        masks.append((jnp.broadcast_to(rowm[:, None], (zeds * nrow, chan)),
                      jnp.broadcast_to(colm[:, None], (ncol, chan))))

    pairs = [fetch(pair, b) for b in range(batches)]
    cots = [fetch(cotangent, b) for b in range(batches)]
    lefts, owns, others, parts = [], [], [], []
    for b in range(batches):
        left, right = edges_call(pairs[b], norm_params, project_low[:, :4 * chan], *masks[b])
        own = blocked(right)
        other = coreswap(own)
        part = product_call(scal, left, own, other)
        lefts.append(left)
        owns.append(own)
        others.append(other)
        parts.append([cswap(part[e], e) for e in range(cols)])
    news, grads, gates, sums = [], [], [], []
    for b in range(batches):
        out = middle_call(pairs[b], cots[b], parts[b], norm_params, weight_low[4], weight_low[5])
        new, (gx, gate_grad, wout, nout) = out[:zeds], out[zeds:]
        news.append([zswap(new[d], d) for d in range(zeds)])
        grads.append([cswap(gx, e) for e in range(cols)])
        gates.append(gate_grad)
        sums.append((wout, nout))
    backs, flats = [], []
    for b in range(batches):
        gleft, keep, send = edge_grad_call(scal, lefts[b], owns[b], others[b], grads[b])
        got = coreswap(send)
        joined = (zeds * nrow, ncol, chan)
        out = input_call(pairs[b], cots[b], gleft, keep.reshape(joined), got.reshape(joined),
                         gates[b], norm_params, project_low, *masks[b])
        back, (wproj, nin) = out[:zeds], out[zeds:]
        backs.append([zswap(back[d], d) for d in range(zeds)])
        wout, nout = sums[b]
        wproj = jnp.transpose(wproj.reshape(chan, 5, chan), (1, 0, 2)).reshape(5 * chan, chan)
        flats.append(jnp.concatenate(
            [wproj, wout, jnp.sum(nin, axis=1), jnp.sum(nout, axis=1)], axis=0))

    def collect(pieces):
        whole = None
        for b in range(batches):
            where = jnp.stack([(zed ^ d) * batches + b for d in range(zeds)]).astype(jnp.int32)
            whole = place_call(where, pieces[b], whole, pair.shape)
        return whole

    new_pair = collect(news)
    pair_grad = collect(backs)
    flat = lax.psum(sum(flats), ("row", "col"))
    grad_weights = flat[: 6 * chan].reshape(weights.shape)
    grad_norms = flat[6 * chan:]
    rate = 0.1 / (length * math.sqrt(crops))
    new_momentum = MOMENT * momentum + grad_weights
    new_weights = weights - rate * (grad_weights + MOMENT * new_momentum)
    new_average = DECAY * average + (1.0 - DECAY) * new_weights
    new_norm_momentum = MOMENT * norm_momentum + grad_norms
    new_norms = norm_params - rate * (grad_norms + MOMENT * new_norm_momentum)
    new_norm_average = DECAY * norm_average + (1.0 - DECAY) * new_norms
    return (new_pair, pair_grad, new_weights, new_momentum, new_average, new_norms,
            new_norm_momentum, new_norm_average)


def solution(mesh):
    rows, cols = mesh.shape["row"], mesh.shape["col"]
    tiled = P(None, "row", "col", None)

    def body(*args):
        return shards(rows, cols, *args)

    return jax.shard_map(
        body,
        mesh=mesh,
        in_specs=(tiled, tiled) + (P(),) * 7,
        out_specs=(tiled, tiled) + (P(),) * 6,
        check_vma=False,
    )
```

time: 3880 us -> 1650 us (0.43)
  waiting for transfers between devices: 2340 us -> 949 us
  local copies, waits for them, and re-layouts: 682 us -> 49 us
  Pallas kernels: 0 us -> 439 us
  matrix products: 424 us -> 0 us
  other arithmetic: 357 us -> 8.6 us
  starting transfers between devices: 1.43 us -> 187 us
    all_gather x16 -> x0, waiting for transfers between devices: 1170 us -> none  [the longest x8 710 us: crop_step(): edges_all = lax.all_gather(right_edge, 'row', axis=0, tiled=True)]
    reduce_scatter x16 -> x0, waiting for transfers between devices: 1080 us -> none  [the longest x8 636 us: crop_step(): lax.psum_scatter(jnp.einsum('ijc,ikc->jkc', piece, left_edge, preferred_e...]
    ppermute x0 -> x40, waiting for transfers between devices: none -> 807 us  [the longest x12 493 us: cswap(): return lax.ppermute(block, 'col', [(q, q ^ e) for q in range(cols)])]
    pallas_call x0 -> x14, Pallas kernels: none -> 439 us  [the longest x2 108 us: input_call(): pl.pallas_call(lambda *refs: input_kernel(nblocks, 4, *refs), grid=(nbloc...]
    dot_general x72 -> x0, matrix products: 424 us -> none  [the longest x16 109 us: contract_cols(): lax.dot_general(left_mat, right_mat, (((1,), (1,)), ((), ())), preferred_...]
    convert_element_type x48 -> x0, local copies, waits for them, and re-layouts: 348 us -> none  [the longest x24 267 us: crop_step(): grad_proj = jnp.stack([grad_left * left_sig * pair_mask, grad_left * proj...]
    ppermute x0 -> x40, starting transfers between devices: none -> 187 us  [the longest x24 169 us: zswap(): return lax.ppermute(block, 'row', [(r, r ^ 2 * d) for r in range(rows)])]
    all_gather x16 -> x0, local copies, waits for them, and re-layouts: 185 us -> none  [the longest x8 124 us: crop_step(): edges_all = lax.all_gather(right_edge, 'row', axis=0, tiled=True)]
  transfers between devices with their start and end apart: 33 -> 41, of which waited for: 33 -> 18; matrix products, arithmetic and copies ran while one was open for 4% -> 2% of each run, Pallas kernels for 0% -> 24%
where the time goes in v1:
time: 1650 us
  waiting for transfers between devices  949 us (58%)
  Pallas kernels  439 us (27%)
  starting transfers between devices  187 us (11%)
  local copies, waits for them, and re-layouts  49 us (3%)
    ppermute x12, waiting for transfers between devices, cswap(): return lax.ppermute(block, 'col', [(q, q ^ e) for q in range(cols)])  493 us
    ppermute x24, waiting for transfers between devices, zswap(): return lax.ppermute(block, 'row', [(r, r ^ 2 * d) for r in range(rows)])  314 us
    ppermute x24, starting transfers between devices, zswap(): return lax.ppermute(block, 'row', [(r, r ^ 2 * d) for r in range(rows)])  169 us
    psum x1, waiting for transfers between devices, shards(): flat = lax.psum(sum(flats), ('row', 'col'))  142 us
    pallas_call x2, Pallas kernels, input_call(): pl.pallas_call(lambda *refs: input_kernel(nblocks, 4, *refs), grid=(nbloc...  108 us
    pallas_call x2, Pallas kernels, edge_grad_call(): pl.pallas_call(lambda *refs: edge_grad_kernel(nparts, 4, *refs), grid_spe...  99.9 us
    pallas_call x2, Pallas kernels, middle_call(): pl.pallas_call(lambda *refs: middle_kernel(nblocks, nparts, 4, *refs), gr...  80.1 us
    pallas_call x2, Pallas kernels, product_call(): pl.pallas_call(lambda *refs: product_kernel(nparts, 4, *refs), grid_spec=...  66.2 us
  transfers between devices with their start and end apart: 41, of which 18 were waited for; matrix products, arithmetic and copies ran while one was open for 2% of the time, Pallas kernels for 24%

profile of v1, /device:TPU:0, one launch (start us, length us, event | category | flops | bytes accessed | tf_op | source)
XLA Modules:
  0.0 1647.2 jit_solution(1924189891695596747)
XLA Ops:
  7.3 7.6 dynamic-slice_bitcast_fusion.4
  15.0 3.1 collective-permute-start.13
  18.1 2.6 collective-permute-start.14
  21.0 47.8 %collective-permute-done.13.refs_1_ = bf16[48,96,128]{2,1,0:T(8,128)(2,1)} collective-permute-done((bf16[48,96,128]{2,1,0:T(8,128)(2,1)}, bf16[48,96,128]{2,1,0:T(8,128)(2,1)}, u32[]{:S(2)}, u32[]{:S(2)}) %collective-permute-start.13) | collective-permute-done | bytes 1179680 | tf_op jit(solution)/shard_map/ppermute | solution.py:480
  68.9 29.9 %collective-permute-done.14.refs_2_ = bf16[48,96,128]{2,1,0:T(8,128)(2,1)} collective-permute-done((bf16[48,96,128]{2,1,0:T(8,128)(2,1)}, bf16[48,96,128]{2,1,0:T(8,128)(2,1)}, u32[]{:S(2)}, u32[]{:S(2)}) %collective-permute-start.14) | collective-permute-done | bytes 1179680 | tf_op jit(solution)/shard_map/ppermute | solution.py:480
  98.9 28.3 %edges.3 = (bf16[192,96,128]{2,1,0:T(8,128)(2,1)S(1)}, bf16[192,96,128]{2,1,0:T(8,128)(2,1)}) custom-call(bf16[48,96,128]{2,1,0:T(8,128)(2,1)S(1)} %get-tuple-element.116.refs_0_, bf16[48,96,128]{2,1,0:T(8,128)(2,1)} %collective-permute-done.13.refs_1_, bf16[48,96,128]{2,1,0:T(8,128)(2,1)} %collective-permute-done.14.refs_2_, ...), custom_call_target="tpu_custom_call" | custom-call | flops 2415919104 | bytes 14155776 | tf_op jit(solution)/shard_map/edges/pallas_call | solution.py:116
  127.3 2.2 copy-done.52
  129.5 24.4 %collective-permute-start = (bf16[48,96,128]{2,1,0:T(8,128)(2,1)S(1)}, bf16[48,96,128]{2,1,0:T(8,128)(2,1)S(1)}, u32[]{:S(2)}, u32[]{:S(2)}) collective-permute-start(bf16[48,96,128]{2,1,0:T(8,128)(2,1)S(1)} %copy-done.57), channel_id=1, source_target_pairs={{0,8},{4,12},{8,0},{12,4},{16,24},{20,28},{24,16},{28,20},{1,9},{5... | collective-permute-start | bytes 3538952 | tf_op jit(solution)/shard_map/ppermute | solution.py:480
  155.0 1.5 collective-permute-start.2
  156.5 48.9 %collective-permute-done.refs_1_ = bf16[48,96,128]{2,1,0:T(8,128)(2,1)S(1)} collective-permute-done((bf16[48,96,128]{2,1,0:T(8,128)(2,1)S(1)}, bf16[48,96,128]{2,1,0:T(8,128)(2,1)S(1)}, u32[]{:S(2)}, u32[]{:S(2)}) %collective-permute-start) | collective-permute-done | bytes 1179680 | tf_op jit(solution)/shard_map/ppermute | solution.py:480
  205.4 28.8 %collective-permute-done.1.refs_2_ = bf16[48,96,128]{2,1,0:T(8,128)(2,1)S(1)} collective-permute-done((bf16[48,96,128]{2,1,0:T(8,128)(2,1)S(1)}, bf16[48,96,128]{2,1,0:T(8,128)(2,1)S(1)}, u32[]{:S(2)}, u32[]{:S(2)}) %collective-permute-start.1) | collective-permute-done | bytes 1179680 | tf_op jit(solution)/shard_map/ppermute | solution.py:480
  234.4 26.3 %edges.2 = (bf16[192,96,128]{2,1,0:T(8,128)(2,1)S(1)}, bf16[192,96,128]{2,1,0:T(8,128)(2,1)}) custom-call(bf16[48,96,128]{2,1,0:T(8,128)(2,1)S(1)} %get-tuple-element.120.refs_0_, bf16[48,96,128]{2,1,0:T(8,128)(2,1)S(1)} %collective-permute-done.refs_1_, bf16[48,96,128]{2,1,0:T(8,128)(2,1)S(1)} %collective-permute-done.1.refs_2_, ...), custom_call_target="tpu_custom_call" | custom-call | flops 2415919104 | bytes 14155776 | tf_op jit(solution)/shard_map/edges/pallas_call | solution.py:116
  260.7 2.2 copy-done.53
  263.5 33.1 %product.3 = (bf16[192,96,128]{2,1,0:T(8,128)(2,1)}, bf16[192,96,128]{2,1,0:T(8,128)(2,1)}, bf16[192,96,128]{2,1,0:T(8,128)(2,1)}, bf16[192,96,128]{2,1,0:T(8,128)(2,1)}) custom-call(s32[5]{0:T(128)} %stack.68.refs_0_, bf16[192,96,128]{2,1,0:T(8,128)(2,1)} %copy-done.52, bf16[4,48,96,128]{3,2,1,0:T(8,128)(2,1)} %bitcast.46.refs_2_, ...), custom_call_target="tpu_custom_call" | custom-call | flops 14495514624 | bytes 33030144 | tf_op jit(solution)/shard_map/product/pallas_call | solution.py:178
  296.6 1.5 collective-permute-start.20
  298.1 1.5 collective-permute-start.21
  300.1 8.0 dynamic-slice_bitcast_fusion
  308.1 25.1 %collective-permute-start.16 = (bf16[48,96,128]{2,1,0:T(8,128)(2,1)}, bf16[48,96,128]{2,1,0:T(8,128)(2,1)}, u32[]{:S(2)}, u32[]{:S(2)}) collective-permute-start(bf16[48,96,128]{2,1,0:T(8,128)(2,1)} %get-tuple-element.107), channel_id=1, source_target_pairs={{0,8},{4,12},{8,0},{12,4},{16,24},{20,28},{24,16},{28,20},{1,9},{5... | collective-permute-start | bytes 3538952 | tf_op jit(solution)/shard_map/ppermute | solution.py:480
  334.3 33.1 %product.2 = (bf16[192,96,128]{2,1,0:T(8,128)(2,1)}, bf16[192,96,128]{2,1,0:T(8,128)(2,1)}, bf16[192,96,128]{2,1,0:T(8,128)(2,1)}, bf16[192,96,128]{2,1,0:T(8,128)(2,1)}) custom-call(s32[5]{0:T(128)} %stack.68.refs_0_, bf16[192,96,128]{2,1,0:T(8,128)(2,1)} %copy-done.53, bf16[4,48,96,128]{3,2,1,0:T(8,128)(2,1)} %bitcast.26.refs_2_, ...), custom_call_target="tpu_custom_call" | custom-call | flops 14495514624 | bytes 33030144 | tf_op jit(solution)/shard_map/product/pallas_call | solution.py:178
  367.4 17.1 %collective-permute-done.16.refs_5_ = bf16[48,96,128]{2,1,0:T(8,128)(2,1)} collective-permute-done((bf16[48,96,128]{2,1,0:T(8,128)(2,1)}, bf16[48,96,128]{2,1,0:T(8,128)(2,1)}, u32[]{:S(2)}, u32[]{:S(2)}) %collective-permute-start.16) | collective-permute-done | bytes 1179680 | tf_op jit(solution)/shard_map/ppermute | solution.py:480
  384.5 1.5 collective-permute-start.7
  387.0 2.5 collective-permute-start.18
  389.5 25.3 %collective-permute-done.18.refs_7_ = bf16[48,96,128]{2,1,0:T(8,128)(2,1)S(1)} collective-permute-done((bf16[48,96,128]{2,1,0:T(8,128)(2,1)}, bf16[48,96,128]{2,1,0:T(8,128)(2,1)S(1)}, u32[]{:S(2)}, u32[]{:S(2)}) %collective-permute-start.18) | collective-permute-done | bytes 1179680 | tf_op jit(solution)/shard_map/ppermute | solution.py:480
  414.8 24.8 %collective-permute-start.3 = (bf16[48,96,128]{2,1,0:T(8,128)(2,1)}, bf16[48,96,128]{2,1,0:T(8,128)(2,1)S(1)}, u32[]{:S(2)}, u32[]{:S(2)}) collective-permute-start(bf16[48,96,128]{2,1,0:T(8,128)(2,1)} %get-tuple-element.111), channel_id=1, source_target_pairs={{0,8},{4,12},{8,0},{12,4},{16,24},{20,28},{24,16},{28,20},{1,9},{5... | collective-permute-start | bytes 3538952 | tf_op jit(solution)/shard_map/ppermute | solution.py:480
  439.5 63.8 %collective-permute-done.21.refs_10_ = bf16[192,96,128]{2,1,0:T(8,128)(2,1)} collective-permute-done((bf16[192,96,128]{2,1,0:T(8,128)(2,1)}, bf16[192,96,128]{2,1,0:T(8,128)(2,1)}, u32[]{:S(2)}, u32[]{:S(2)}) %collective-permute-start.21) | collective-permute-done | bytes 4718624 | tf_op jit(solution)/shard_map/ppermute | solution.py:485
  503.3 1.7 collective-permute-start.8
  506.4 40.9 %middle.3 = (bf16[48,96,128]{2,1,0:T(8,128)(2,1)S(1)}, bf16[48,96,128]{2,1,0:T(8,128)(2,1)S(1)}, bf16[48,96,128]{2,1,0:T(8,128)(2,1)S(1)}, bf16[48,96,128]{2,1,0...) custom-call(bf16[48,96,128]{2,1,0:T(8,128)(2,1)S(1)} %get-tuple-elem, ...), custom_call_target="tpu_custom_call" | custom-call | flops 2415919104 | bytes 42467328 | tf_op jit(solution)/shard_map/middle/pallas_call | solution.py:258
  549.0 1.7 collective-permute-start.33
  550.7 2.5 collective-permute-start.5
  553.3 25.8 %collective-permute-done.5.refs_7_ = bf16[48,96,128]{2,1,0:T(8,128)(2,1)S(1)} collective-permute-done((bf16[48,96,128]{2,1,0:T(8,128)(2,1)S(1)}, bf16[48,96,128]{2,1,0:T(8,128)(2,1)S(1)}, u32[]{:S(2)}, u32[]{:S(2)}) %collective-permute-start.5) | collective-permute-done | bytes 1179680 | tf_op jit(solution)/shard_map/ppermute | solution.py:480
  579.1 1.7 collective-permute-start.34
  580.8 23.0 %collective-permute-done.7.refs_9_ = bf16[192,96,128]{2,1,0:T(8,128)(2,1)} collective-permute-done((bf16[192,96,128]{2,1,0:T(8,128)(2,1)}, bf16[192,96,128]{2,1,0:T(8,128)(2,1)}, u32[]{:S(2)}, u32[]{:S(2)}) %collective-permute-start.7) | collective-permute-done | bytes 4718624 | tf_op jit(solution)/shard_map/ppermute | solution.py:485
  603.8 2.4 collective-permute-start.35
  606.3 103.2 %collective-permute-done.8.refs_10_ = bf16[192,96,128]{2,1,0:T(8,128)(2,1)} collective-permute-done((bf16[192,96,128]{2,1,0:T(8,128)(2,1)}, bf16[192,96,128]{2,1,0:T(8,128)(2,1)}, u32[]{:S(2)}, u32[]{:S(2)}) %collective-permute-start.8) | collective-permute-done | bytes 4718624 | tf_op jit(solution)/shard_map/ppermute | solution.py:485
  709.5 39.3 %middle.2 = (bf16[48,96,128]{2,1,0:T(8,128)(2,1)S(1)}, bf16[48,96,128]{2,1,0:T(8,128)(2,1)S(1)}, bf16[48,96,128]{2,1,0:T(8,128)(2,1)S(1)}, bf16[48,96,128]{2,1,0...) custom-call(bf16[48,96,128]{2,1,0:T(8,128)(2,1)S(1)} %get-tuple-elem, ...), custom_call_target="tpu_custom_call" | custom-call | flops 2415919104 | bytes 42467328 | tf_op jit(solution)/shard_map/middle/pallas_call | solution.py:258
  754.6 2.0 collective-permute-start.27
  756.6 49.5 %collective-permute-done.33.refs_5_ = bf16[192,96,128]{2,1,0:T(8,128)(2,1)} collective-permute-done((bf16[192,96,128]{2,1,0:T(8,128)(2,1)}, bf16[192,96,128]{2,1,0:T(8,128)(2,1)}, u32[]{:S(2)}, u32[]{:S(2)}) %collective-permute-start.33) | collective-permute-done | bytes 4718624 | tf_op jit(solution)/shard_map/ppermute | solution.py:485
  806.1 2.4 collective-permute-start.28
  808.5 103.2 %collective-permute-done.34.refs_6_ = bf16[192,96,128]{2,1,0:T(8,128)(2,1)} collective-permute-done((bf16[192,96,128]{2,1,0:T(8,128)(2,1)}, bf16[192,96,128]{2,1,0:T(8,128)(2,1)}, u32[]{:S(2)}, u32[]{:S(2)}) %collective-permute-start.34) | collective-permute-done | bytes 4718624 | tf_op jit(solution)/shard_map/ppermute | solution.py:485
  911.7 50.0 %edge_grad.3 = (bf16[192,96,128]{2,1,0:T(8,128)(2,1)}, bf16[4,48,96,128]{3,2,1,0:T(8,128)(2,1)}, bf16[4,48,96,128]{3,2,1,0:T(8,128)(2,1)}) custom-call(s32[5]{0:T(128)} %stack.68.refs_0_, bf16[192,96,128]{2,1,0:T(8,128)(2,1)} %copy-done.52, bf16[4,48,96,128]{3,2,1,0:T(8,128)(2,1)} %bitcast.46.refs_2_, ...), custom_call_target="tpu_custom_call" | custom-call | flops 28991029248 | bytes 33030144 | tf_op jit(solution)/shard_map/edge_grad/pallas_call | solution.py:333
  961.8 46.6 %collective-permute-done.26.refs_5_ = bf16[192,96,128]{2,1,0:T(8,128)(2,1)} collective-permute-done((bf16[192,96,128]{2,1,0:T(8,128)(2,1)}, bf16[192,96,128]{2,1,0:T(8,128)(2,1)}, u32[]{:S(2)}, u32[]{:S(2)}) %collective-permute-start.26) | collective-permute-done | bytes 4718624 | tf_op jit(solution)/shard_map/ppermute | solution.py:485
  1008.4 103.9 %collective-permute-done.27.refs_6_ = bf16[192,96,128]{2,1,0:T(8,128)(2,1)} collective-permute-done((bf16[192,96,128]{2,1,0:T(8,128)(2,1)}, bf16[192,96,128]{2,1,0:T(8,128)(2,1)}, u32[]{:S(2)}, u32[]{:S(2)}) %collective-permute-start.27) | collective-permute-done | bytes 4718624 | tf_op jit(solution)/shard_map/ppermute | solution.py:485
  1112.3 49.9 %edge_grad.2 = (bf16[192,96,128]{2,1,0:T(8,128)(2,1)}, bf16[4,48,96,128]{3,2,1,0:T(8,128)(2,1)}, bf16[4,48,96,128]{3,2,1,0:T(8,128)(2,1)}) custom-call(s32[5]{0:T(128)} %stack.68.refs_0_, bf16[192,96,128]{2,1,0:T(8,128)(2,1)} %copy-done.53, bf16[4,48,96,128]{3,2,1,0:T(8,128)(2,1)} %bitcast.26.refs_2_, ...), custom_call_target="tpu_custom_call" | custom-call | flops 28991029248 | bytes 33030144 | tf_op jit(solution)/shard_map/edge_grad/pallas_call | solution.py:333
  1162.2 25.1 %collective-permute-start.23 = (bf16[48,96,128]{2,1,0:T(8,128)(2,1)}, bf16[48,96,128]{2,1,0:T(8,128)(2,1)}, u32[]{:S(2)}, u32[]{:S(2)}) collective-permute-start(bf16[48,96,128]{2,1,0:T(8,128)(2,1)} %copy-done.50), channel_id=1, source_target_pairs={{0,8},{4,12},{8,0},{12,4},{16,24},{20,28},{24,16},{28,20},{1,9},{5... | collective-permute-start | bytes 3538952 | tf_op jit(solution)/shard_map/ppermute | solution.py:480
  1188.6 1.5 collective-permute-start.25
  1193.6 54.5 %input_grad.3 = (bf16[48,96,128]{2,1,0:T(8,128)(2,1)S(1)}, bf16[48,96,128]{2,1,0:T(8,128)(2,1)}, bf16[48,96,128]{2,1,0:T(8,128)(2,1)}, bf16[48,96,128]{2,1,0:T(8...) custom-call(bf16[48,96,128]{2,1,0:T(8,128)(2,1)S(1)} %copy-done.1, ...), custom_call_target="tpu_custom_call" | custom-call | flops 8455716864 | bytes 33030144 | tf_op jit(solution)/shard_map/input_grad/pallas_call | solution.py:415
  1249.8 2.1 collective-permute-start.11
  1251.9 16.2 collective-permute-done.24.refs_3_
  1268.0 2.6 collective-permute-start.12
  1270.7 53.5 %input_grad.2 = (bf16[48,96,128]{2,1,0:T(8,128)(2,1)S(1)}, bf16[48,96,128]{2,1,0:T(8,128)(2,1)}, bf16[48,96,128]{2,1,0:T(8,128)(2,1)}, bf16[48,96,128]{2,1,0:T(8...) custom-call(bf16[48,96,128]{2,1,0:T(8,128)(2,1)S(1)} %get-tuple-element.120.refs_0_, ...), custom_call_target="tpu_custom_call" | custom-call | flops 8455716864 | bytes 33030144 | tf_op jit(solution)/shard_map/input_grad/pallas_call | solution.py:415
  1326.5 19.0 %collective-permute-start.38 = (bf16[48,96,128]{2,1,0:T(8,128)(2,1)}, bf16[48,96,128]{2,1,0:T(8,128)(2,1)}, u32[]{:S(2)}, u32[]{:S(2)}) collective-permute-start(bf16[48,96,128]{2,1,0:T(8,128)(2,1)} %get-tuple-element.90), channel_id=1, source_target_pairs={{0,16},{4,20},{8,24},{12,28},{16,0},{20,4},{24,8},{28,12},{1,17},{... | collective-permute-start | bytes 3538952 | tf_op jit(solution)/shard_map/ppermute | solution.py:480
  1346.8 72.8 %collective-permute-done.11.refs_3_ = bf16[48,96,128]{2,1,0:T(8,128)(2,1)S(1)} collective-permute-done((bf16[48,96,128]{2,1,0:T(8,128)(2,1)}, bf16[48,96,128]{2,1,0:T(8,128)(2,1)S(1)}, u32[]{:S(2)}, u32[]{:S(2)}) %collective-permute-start.11) | collective-permute-done | bytes 1179680 | tf_op jit(solution)/shard_map/ppermute | solution.py:480
  1421.7 25.9 %collective-permute-start.31 = (bf16[48,96,128]{2,1,0:T(8,128)(2,1)}, bf16[48,96,128]{2,1,0:T(8,128)(2,1)S(1)}, u32[]{:S(2)}, u32[]{:S(2)}) collective-permute-start(bf16[48,96,128]{2,1,0:T(8,128)(2,1)} %get-tuple-element.81), channel_id=1, source_target_pairs={{0,16},{4,20},{8,24},{12,28},{16,0},{20,4},{24,8},{28,12},{1,17},{... | collective-permute-start | bytes 3538952 | tf_op jit(solution)/shard_map/ppermute | solution.py:480
  1451.2 1.9 copy.23
  1453.0 1.9 copy.24
  1455.5 1.9 copy.25
  1457.4 1.9 copy.26
  1459.8 2.0 maximum_add_fusion
  1463.3 9.1 place.4.refs_5_
  1472.4 5.4 place.5
  1477.8 142.4 %all-reduce.2.cloned.1.call-done = f32[772,128]{1,0:T(8,128)} async-done(((f32[772,128]{1,0:T(8,128)}), f32[772,128]{1,0:T(8,128)}) %all-reduce.2.cloned.1.call-update) | async-done | bytes 395280 | tf_op jit(solution)/shard_map/psum | solution.py:553
  1622.5 2.5 multiply_add_fusion
  1625.0 8.0 place.6.refs_5_
  1633.1 7.3 place.7
  (189 shorter events, 34.6 us)
Async XLA Ops:
  7.2 1613.0 %all-reduce.2.cloned.1.call-start = ((), (), s32[]{:S(2)}) async-start(), calls=%async_computation | async-start | bytes 794624 | tf_op jit(solution)/shard_map/psum | solution.py:553
  15.0 490.2 %copy-start = (bf16[48,96,128]{2,1,0:T(8,128)(2,1)}, bf16[48,96,128]{2,1,0:T(8,128)(2,1)S(1)}, u32[]{:S(2)}) copy-start(bf16[48,96,128]{2,1,0:T(8,128)(2,1)S(1)} %get-tuple-element.116.refs_0_) | copy-start | bytes 3538948
  15.0 83.9 %copy-start.39 = (f32[4,128]{1,0:T(4,128)S(1)}, f32[4,128]{1,0:T(4,128)}, u32[]{:S(2)}) copy-start(f32[4,128]{1,0:T(4,128)} %refs_12_.7) | copy-start | bytes 6148
  15.0 53.9 %collective-permute-start.13 = (bf16[48,96,128]{2,1,0:T(8,128)(2,1)}, bf16[48,96,128]{2,1,0:T(8,128)(2,1)}, u32[]{:S(2)}, u32[]{:S(2)}) collective-permute-start(bf16[48,96,128]{2,1,0:T(8,128)(2,1)} %get-tuple-element.115), channel_id=1, source_target_pairs={{0,8},{4,12},{8,0},{12,4},{16,24},{20,28},{24,16},{28,20},{1,9},{5... | collective-permute-start | bytes 3538952 | tf_op jit(solution)/shard_map/ppermute | solution.py:480
  18.1 80.7 %collective-permute-start.14 = (bf16[48,96,128]{2,1,0:T(8,128)(2,1)}, bf16[48,96,128]{2,1,0:T(8,128)(2,1)}, u32[]{:S(2)}, u32[]{:S(2)}) collective-permute-start(bf16[48,96,128]{2,1,0:T(8,128)(2,1)} %get-tuple-element.121), channel_id=1, source_target_pairs={{0,16},{4,20},{8,24},{12,28},{16,0},{20,4},{24,8},{28,12},{1,17},{... | collective-permute-start | bytes 3538952 | tf_op jit(solution)/shard_map/ppermute | solution.py:480
  20.7 78.1 %collective-permute-start.15 = (bf16[48,96,128]{2,1,0:T(8,128)(2,1)}, bf16[48,96,128]{2,1,0:T(8,128)(2,1)}, u32[]{:S(2)}, u32[]{:S(2)}) collective-permute-start(bf16[48,96,128]{2,1,0:T(8,128)(2,1)} %get-tuple-element.114), channel_id=1, source_target_pairs={{0,24},{4,28},{8,16},{12,20},{16,8},{20,12},{24,0},{28,4},{1,25},{... | collective-permute-start | bytes 3538952 | tf_op jit(solution)/shard_map/ppermute | solution.py:480
  98.9 56.1 %copy-start.55 = (bf16[48,96,128]{2,1,0:T(8,128)(2,1)S(1)}, bf16[48,96,128]{2,1,0:T(8,128)(2,1)}, u32[]{:S(2)}) copy-start(bf16[48,96,128]{2,1,0:T(8,128)(2,1)} %get-tuple-element.117) | copy-start | bytes 3538948
  129.5 134.0 %collective-permute-start.19 = (bf16[4,48,96,128]{3,2,1,0:T(8,128)(2,1)}, bf16[4,48,96,128]{3,2,1,0:T(8,128)(2,1)}, u32[]{:S(2)}, u32[]{:S(2)}) collective-permute-start(bf16[4,48,96,128]{3,2,1,0:T(8,128)(2,1)} %bitcast.46.refs_2_), channel_id=1, source_target_pairs={{0,4},{4,0},{8,12},{12,8},{16,20},{20,16},{24,28},{28,24},{1,5},{5... | collective-permute-start | bytes 14155784 | tf_op jit(solution)/shard_map/ppermute | solution.py:488
  129.5 75.9 %collective-permute-start = (bf16[48,96,128]{2,1,0:T(8,128)(2,1)S(1)}, bf16[48,96,128]{2,1,0:T(8,128)(2,1)S(1)}, u32[]{:S(2)}, u32[]{:S(2)}) collective-permute-start(bf16[48,96,128]{2,1,0:T(8,128)(2,1)S(1)} %copy-done.57), channel_id=1, source_target_pairs={{0,8},{4,12},{8,0},{12,4},{16,24},{20,28},{24,16},{28,20},{1,9},{5... | collective-permute-start | bytes 3538952 | tf_op jit(solution)/shard_map/ppermute | solution.py:480
  153.9 80.3 %collective-permute-start.1 = (bf16[48,96,128]{2,1,0:T(8,128)(2,1)S(1)}, bf16[48,96,128]{2,1,0:T(8,128)(2,1)S(1)}, u32[]{:S(2)}, u32[]{:S(2)}) collective-permute-start(bf16[48,96,128]{2,1,0:T(8,128)(2,1)S(1)} %copy-done.56), channel_id=1, source_target_pairs={{0,16},{4,20},{8,24},{12,28},{16,0},{20,4},{24,8},{28,12},{1,17},{... | collective-permute-start | bytes 3538952 | tf_op jit(solution)/shard_map/ppermute | solution.py:480
  155.0 79.2 %collective-permute-start.2 = (bf16[48,96,128]{2,1,0:T(8,128)(2,1)S(1)}, bf16[48,96,128]{2,1,0:T(8,128)(2,1)S(1)}, u32[]{:S(2)}, u32[]{:S(2)}) collective-permute-start(bf16[48,96,128]{2,1,0:T(8,128)(2,1)S(1)} %copy-done.55), channel_id=1, source_target_pairs={{0,24},{4,28},{8,16},{12,20},{16,8},{20,12},{24,0},{28,4},{1,25},{... | collective-permute-start | bytes 3538952 | tf_op jit(solution)/shard_map/ppermute | solution.py:480
  205.4 55.3 %copy-start.6 = (bf16[48,96,128]{2,1,0:T(8,128)(2,1)}, bf16[48,96,128]{2,1,0:T(8,128)(2,1)S(1)}, u32[]{:S(2)}) copy-start(bf16[48,96,128]{2,1,0:T(8,128)(2,1)S(1)} %collective-permute-done.refs_1_) | copy-start | bytes 3538948
  262.9 70.3 %collective-permute-start.6 = (bf16[4,48,96,128]{3,2,1,0:T(8,128)(2,1)}, bf16[4,48,96,128]{3,2,1,0:T(8,128)(2,1)}, u32[]{:S(2)}, u32[]{:S(2)}) collective-permute-start(bf16[4,48,96,128]{3,2,1,0:T(8,128)(2,1)} %bitcast.26.refs_2_), channel_id=1, source_target_pairs={{0,4},{4,0},{8,12},{12,8},{16,20},{20,16},{24,28},{28,24},{1,5},{5... | collective-permute-start | bytes 14155784 | tf_op jit(solution)/shard_map/ppermute | solution.py:488
  296.6 142.9 %collective-permute-start.20 = (bf16[192,96,128]{2,1,0:T(8,128)(2,1)}, bf16[192,96,128]{2,1,0:T(8,128)(2,1)}, u32[]{:S(2)}, u32[]{:S(2)}) collective-permute-start(bf16[192,96,128]{2,1,0:T(8,128)(2,1)} %get-tuple-element.67), channel_id=1, source_target_pairs={{0,1},{1,0},{2,3},{3,2},{4,5},{5,4},{6,7},{7,6},{8,9},{9,8},{10,11... | collective-permute-start | bytes 14155784 | tf_op jit(solution)/shard_map/ppermute | solution.py:485
  298.1 205.2 %collective-permute-start.21 = (bf16[192,96,128]{2,1,0:T(8,128)(2,1)}, bf16[192,96,128]{2,1,0:T(8,128)(2,1)}, u32[]{:S(2)}, u32[]{:S(2)}) collective-permute-start(bf16[192,96,128]{2,1,0:T(8,128)(2,1)} %get-tuple-element.68), channel_id=1, source_target_pairs={{0,2},{1,3},{2,0},{3,1},{4,6},{5,7},{6,4},{7,5},{8,10},{9,11},{10,... | collective-permute-start | bytes 14155784 | tf_op jit(solution)/shard_map/ppermute | solution.py:485
  299.6 205.4 %collective-permute-start.22 = (bf16[192,96,128]{2,1,0:T(8,128)(2,1)}, bf16[192,96,128]{2,1,0:T(8,128)(2,1)}, u32[]{:S(2)}, u32[]{:S(2)}) collective-permute-start(bf16[192,96,128]{2,1,0:T(8,128)(2,1)} %get-tuple-element.69), channel_id=1, source_target_pairs={{0,3},{1,2},{2,1},{3,0},{4,7},{5,6},{6,5},{7,4},{8,11},{9,10},{10,... | collective-permute-start | bytes 14155784 | tf_op jit(solution)/shard_map/ppermute | solution.py:485
  308.1 76.4 %collective-permute-start.16 = (bf16[48,96,128]{2,1,0:T(8,128)(2,1)}, bf16[48,96,128]{2,1,0:T(8,128)(2,1)}, u32[]{:S(2)}, u32[]{:S(2)}) collective-permute-start(bf16[48,96,128]{2,1,0:T(8,128)(2,1)} %get-tuple-element.107), channel_id=1, source_target_pairs={{0,8},{4,12},{8,0},{12,4},{16,24},{20,28},{24,16},{28,20},{1,9},{5... | collective-permute-start | bytes 3538952 | tf_op jit(solution)/shard_map/ppermute | solution.py:480
  333.2 53.8 %collective-permute-start.17 = (bf16[48,96,128]{2,1,0:T(8,128)(2,1)}, bf16[48,96,128]{2,1,0:T(8,128)(2,1)}, u32[]{:S(2)}, u32[]{:S(2)}) collective-permute-start(bf16[48,96,128]{2,1,0:T(8,128)(2,1)} %get-tuple-element.113), channel_id=1, source_target_pairs={{0,16},{4,20},{8,24},{12,28},{16,0},{20,4},{24,8},{28,12},{1,17},{... | collective-permute-start | bytes 3538952 | tf_op jit(solution)/shard_map/ppermute | solution.py:480
  384.5 219.4 %collective-permute-start.7 = (bf16[192,96,128]{2,1,0:T(8,128)(2,1)}, bf16[192,96,128]{2,1,0:T(8,128)(2,1)}, u32[]{:S(2)}, u32[]{:S(2)}) collective-permute-start(bf16[192,96,128]{2,1,0:T(8,128)(2,1)} %get-tuple-element.57), channel_id=1, source_target_pairs={{0,1},{1,0},{2,3},{3,2},{4,5},{5,4},{6,7},{7,6},{8,9},{9,8},{10,11... | collective-permute-start | bytes 14155784 | tf_op jit(solution)/shard_map/ppermute | solution.py:485
  387.0 27.8 %collective-permute-start.18 = (bf16[48,96,128]{2,1,0:T(8,128)(2,1)}, bf16[48,96,128]{2,1,0:T(8,128)(2,1)S(1)}, u32[]{:S(2)}, u32[]{:S(2)}) collective-permute-start(bf16[48,96,128]{2,1,0:T(8,128)(2,1)} %get-tuple-element.106), channel_id=1, source_target_pairs={{0,24},{4,28},{8,16},{12,20},{16,8},{20,12},{24,0},{28,4},{1,25},{... | collective-permute-start | bytes 3538952 | tf_op jit(solution)/shard_map/ppermute | solution.py:480
  414.8 132.5 %copy-start.19 = (bf16[48,96,128]{2,1,0:T(8,128)(2,1)}, bf16[48,96,128]{2,1,0:T(8,128)(2,1)S(1)}, u32[]{:S(2)}) copy-start(bf16[48,96,128]{2,1,0:T(8,128)(2,1)S(1)} %collective-permute-done.18.refs_7_) | copy-start | bytes 3538948
  414.8 134.2 %collective-permute-start.3 = (bf16[48,96,128]{2,1,0:T(8,128)(2,1)}, bf16[48,96,128]{2,1,0:T(8,128)(2,1)S(1)}, u32[]{:S(2)}, u32[]{:S(2)}) collective-permute-start(bf16[48,96,128]{2,1,0:T(8,128)(2,1)} %get-tuple-element.111), channel_id=1, source_target_pairs={{0,8},{4,12},{8,0},{12,4},{16,24},{20,28},{24,16},{28,20},{1,9},{5... | collective-permute-start | bytes 3538952 | tf_op jit(solution)/shard_map/ppermute | solution.py:480
  439.5 111.2 %collective-permute-start.4 = (bf16[48,96,128]{2,1,0:T(8,128)(2,1)}, bf16[48,96,128]{2,1,0:T(8,128)(2,1)S(1)}, u32[]{:S(2)}, u32[]{:S(2)}) collective-permute-start(bf16[48,96,128]{2,1,0:T(8,128)(2,1)} %get-tuple-element.110), channel_id=1, source_target_pairs={{0,16},{4,20},{8,24},{12,28},{16,0},{20,4},{24,8},{28,12},{1,17},{... | collective-permute-start | bytes 3538952 | tf_op jit(solution)/shard_map/ppermute | solution.py:480
  503.3 206.2 %collective-permute-start.8 = (bf16[192,96,128]{2,1,0:T(8,128)(2,1)}, bf16[192,96,128]{2,1,0:T(8,128)(2,1)}, u32[]{:S(2)}, u32[]{:S(2)}) collective-permute-start(bf16[192,96,128]{2,1,0:T(8,128)(2,1)} %get-tuple-element.58), channel_id=1, source_target_pairs={{0,2},{1,3},{2,0},{3,1},{4,6},{5,7},{6,4},{7,5},{8,10},{9,11},{10,... | collective-permute-start | bytes 14155784 | tf_op jit(solution)/shard_map/ppermute | solution.py:485
  505.0 204.5 %collective-permute-start.9 = (bf16[192,96,128]{2,1,0:T(8,128)(2,1)}, bf16[192,96,128]{2,1,0:T(8,128)(2,1)}, u32[]{:S(2)}, u32[]{:S(2)}) collective-permute-start(bf16[192,96,128]{2,1,0:T(8,128)(2,1)} %get-tuple-element.59), channel_id=1, source_target_pairs={{0,3},{1,2},{2,1},{3,0},{4,7},{5,6},{6,5},{7,4},{8,11},{9,10},{10,... | collective-permute-start | bytes 14155784 | tf_op jit(solution)/shard_map/ppermute | solution.py:485
  506.4 203.1 %copy-start.2 = (bf16[48,96,128]{2,1,0:T(8,128)(2,1)S(1)}, bf16[48,96,128]{2,1,0:T(8,128)(2,1)}, u32[]{:S(2)}) copy-start(bf16[48,96,128]{2,1,0:T(8,128)(2,1)} %get-tuple-element.112.refs_4_) | copy-start | bytes 3538948
  506.4 203.1 %copy-start.7 = (bf16[48,96,128]{2,1,0:T(8,128)(2,1)S(1)}, bf16[48,96,128]{2,1,0:T(8,128)(2,1)}, u32[]{:S(2)}) copy-start(bf16[48,96,128]{2,1,0:T(8,128)(2,1)} %copy-done.6) | copy-start | bytes 3538948
  506.4 203.1 %copy-start.10 = (bf16[48,96,128]{2,1,0:T(8,128)(2,1)S(1)}, bf16[48,96,128]{2,1,0:T(8,128)(2,1)}, u32[]{:S(2)}) copy-start(bf16[48,96,128]{2,1,0:T(8,128)(2,1)} %copy-done.9) | copy-start | bytes 3538948
  506.4 203.1 %copy-start.13 = (bf16[48,96,128]{2,1,0:T(8,128)(2,1)S(1)}, bf16[48,96,128]{2,1,0:T(8,128)(2,1)}, u32[]{:S(2)}) copy-start(bf16[48,96,128]{2,1,0:T(8,128)(2,1)} %copy-done.12) | copy-start | bytes 3538948
  549.0 199.9 %copy-start.45 = (bf16[48,96,128]{2,1,0:T(8,128)(2,1)}, bf16[48,96,128]{2,1,0:T(8,128)(2,1)S(1)}, u32[]{:S(2)}) copy-start(bf16[48,96,128]{2,1,0:T(8,128)(2,1)S(1)} %get-tuple-element.73) | copy-start | bytes 3538948
  549.0 199.9 %copy-start.48 = (bf16[48,96,128]{2,1,0:T(8,128)(2,1)}, bf16[48,96,128]{2,1,0:T(8,128)(2,1)S(1)}, u32[]{:S(2)}) copy-start(bf16[48,96,128]{2,1,0:T(8,128)(2,1)S(1)} %get-tuple-element.72) | copy-start | bytes 3538948
  549.0 199.9 %copy-start.50 = (bf16[48,96,128]{2,1,0:T(8,128)(2,1)}, bf16[48,96,128]{2,1,0:T(8,128)(2,1)S(1)}, u32[]{:S(2)}) copy-start(bf16[48,96,128]{2,1,0:T(8,128)(2,1)S(1)} %get-tuple-element.71) | copy-start | bytes 3538948
  549.0 199.9 %copy-start.15 = (bf16[48,96,128]{2,1,0:T(8,128)(2,1)}, bf16[48,96,128]{2,1,0:T(8,128)(2,1)S(1)}, u32[]{:S(2)}) copy-start(bf16[48,96,128]{2,1,0:T(8,128)(2,1)S(1)} %collective-permute-done.3.refs_5_) | copy-start | bytes 3538948
  549.0 257.1 %collective-permute-start.33 = (bf16[192,96,128]{2,1,0:T(8,128)(2,1)}, bf16[192,96,128]{2,1,0:T(8,128)(2,1)}, u32[]{:S(2)}, u32[]{:S(2)}) collective-permute-start(bf16[192,96,128]{2,1,0:T(8,128)(2,1)} %get-tuple-element.83.refs_4_), channel_id=1, source_target_pairs={{0,1},{1,0},{2,3},{3,2},{4,5},{5,4},{6,7},{7,6},{8,9},{9,8},{10,11... | collective-permute-start | bytes 14155784 | tf_op jit(solution)/shard_map/ppermute | solution.py:485
  550.7 198.1 %copy-start.17 = (bf16[48,96,128]{2,1,0:T(8,128)(2,1)}, bf16[48,96,128]{2,1,0:T(8,128)(2,1)S(1)}, u32[]{:S(2)}) copy-start(bf16[48,96,128]{2,1,0:T(8,128)(2,1)S(1)} %collective-permute-done.4.refs_6_) | copy-start | bytes 3538948
  550.7 28.4 %collective-permute-start.5 = (bf16[48,96,128]{2,1,0:T(8,128)(2,1)S(1)}, bf16[48,96,128]{2,1,0:T(8,128)(2,1)S(1)}, u32[]{:S(2)}, u32[]{:S(2)}) collective-permute-start(bf16[48,96,128]{2,1,0:T(8,128)(2,1)S(1)} %copy-done.58), channel_id=1, source_target_pairs={{0,24},{4,28},{8,16},{12,20},{16,8},{20,12},{24,0},{28,4},{1,25},{... | collective-permute-start | bytes 3538952 | tf_op jit(solution)/shard_map/ppermute | solution.py:480
  579.1 169.8 %copy-start.20 = (bf16[48,96,128]{2,1,0:T(8,128)(2,1)}, bf16[48,96,128]{2,1,0:T(8,128)(2,1)S(1)}, u32[]{:S(2)}) copy-start(bf16[48,96,128]{2,1,0:T(8,128)(2,1)S(1)} %collective-permute-done.5.refs_7_) | copy-start | bytes 3538948
  579.1 332.6 %collective-permute-start.34 = (bf16[192,96,128]{2,1,0:T(8,128)(2,1)}, bf16[192,96,128]{2,1,0:T(8,128)(2,1)}, u32[]{:S(2)}, u32[]{:S(2)}) collective-permute-start(bf16[192,96,128]{2,1,0:T(8,128)(2,1)} %get-tuple-element.83.refs_4_), channel_id=1, source_target_pairs={{0,2},{1,3},{2,0},{3,1},{4,6},{5,7},{6,4},{7,5},{8,10},{9,11},{10,... | collective-permute-start | bytes 14155784 | tf_op jit(solution)/shard_map/ppermute | solution.py:485
  603.8 307.9 %collective-permute-start.35 = (bf16[192,96,128]{2,1,0:T(8,128)(2,1)}, bf16[192,96,128]{2,1,0:T(8,128)(2,1)}, u32[]{:S(2)}, u32[]{:S(2)}) collective-permute-start(bf16[192,96,128]{2,1,0:T(8,128)(2,1)} %get-tuple-element.83.refs_4_), channel_id=1, source_target_pairs={{0,3},{1,2},{2,1},{3,0},{4,7},{5,6},{6,5},{7,4},{8,11},{9,10},{10,... | collective-permute-start | bytes 14155784 | tf_op jit(solution)/shard_map/ppermute | solution.py:485
  754.2 254.1 %collective-permute-start.26 = (bf16[192,96,128]{2,1,0:T(8,128)(2,1)}, bf16[192,96,128]{2,1,0:T(8,128)(2,1)}, u32[]{:S(2)}, u32[]{:S(2)}) collective-permute-start(bf16[192,96,128]{2,1,0:T(8,128)(2,1)} %get-tuple-element.74.refs_4_), channel_id=1, source_target_pairs={{0,1},{1,0},{2,3},{3,2},{4,5},{5,4},{6,7},{7,6},{8,9},{9,8},{10,11... | collective-permute-start | bytes 14155784 | tf_op jit(solution)/shard_map/ppermute | solution.py:485
  754.6 357.7 %collective-permute-start.27 = (bf16[192,96,128]{2,1,0:T(8,128)(2,1)}, bf16[192,96,128]{2,1,0:T(8,128)(2,1)}, u32[]{:S(2)}, u32[]{:S(2)}) collective-permute-start(bf16[192,96,128]{2,1,0:T(8,128)(2,1)} %get-tuple-element.74.refs_4_), channel_id=1, source_target_pairs={{0,2},{1,3},{2,0},{3,1},{4,6},{5,7},{6,4},{7,5},{8,10},{9,11},{10,... | collective-permute-start | bytes 14155784 | tf_op jit(solution)/shard_map/ppermute | solution.py:485
  806.1 306.2 %collective-permute-start.28 = (bf16[192,96,128]{2,1,0:T(8,128)(2,1)}, bf16[192,96,128]{2,1,0:T(8,128)(2,1)}, u32[]{:S(2)}, u32[]{:S(2)}) collective-permute-start(bf16[192,96,128]{2,1,0:T(8,128)(2,1)} %get-tuple-element.74.refs_4_), channel_id=1, source_target_pairs={{0,3},{1,2},{2,1},{3,0},{4,7},{5,6},{6,5},{7,4},{8,11},{9,10},{10,... | collective-permute-start | bytes 14155784 | tf_op jit(solution)/shard_map/ppermute | solution.py:485
  961.8 228.3 %collective-permute-start.36 = (bf16[4,48,96,128]{3,2,1,0:T(8,128)(2,1)}, bf16[4,48,96,128]{3,2,1,0:T(8,128)(2,1)}, u32[]{:S(2)}, u32[]{:S(2)}) collective-permute-start(bf16[4,48,96,128]{3,2,1,0:T(8,128)(2,1)} %get-tuple-element.86), channel_id=1, source_target_pairs={{0,4},{4,0},{8,12},{12,8},{16,20},{20,16},{24,28},{28,24},{1,5},{5... | collective-permute-start | bytes 14155784 | tf_op jit(solution)/shard_map/ppermute | solution.py:488
  1162.2 108.5 %collective-permute-start.29 = (bf16[4,48,96,128]{3,2,1,0:T(8,128)(2,1)}, bf16[4,48,96,128]{3,2,1,0:T(8,128)(2,1)}, u32[]{:S(2)}, u32[]{:S(2)}) collective-permute-start(bf16[4,48,96,128]{3,2,1,0:T(8,128)(2,1)} %get-tuple-element.77), channel_id=1, source_target_pairs={{0,4},{4,0},{8,12},{12,8},{16,20},{20,16},{24,28},{28,24},{1,5},{5... | collective-permute-start | bytes 14155784 | tf_op jit(solution)/shard_map/ppermute | solution.py:488
  1162.2 87.5 %collective-permute-start.23 = (bf16[48,96,128]{2,1,0:T(8,128)(2,1)}, bf16[48,96,128]{2,1,0:T(8,128)(2,1)}, u32[]{:S(2)}, u32[]{:S(2)}) collective-permute-start(bf16[48,96,128]{2,1,0:T(8,128)(2,1)} %copy-done.50), channel_id=1, source_target_pairs={{0,8},{4,12},{8,0},{12,4},{16,24},{20,28},{24,16},{28,20},{1,9},{5... | collective-permute-start | bytes 3538952 | tf_op jit(solution)/shard_map/ppermute | solution.py:480
  1187.4 80.7 %collective-permute-start.24 = (bf16[48,96,128]{2,1,0:T(8,128)(2,1)}, bf16[48,96,128]{2,1,0:T(8,128)(2,1)}, u32[]{:S(2)}, u32[]{:S(2)}) collective-permute-start(bf16[48,96,128]{2,1,0:T(8,128)(2,1)} %copy-done.48), channel_id=1, source_target_pairs={{0,16},{4,20},{8,24},{12,28},{16,0},{20,4},{24,8},{28,12},{1,17},{... | collective-permute-start | bytes 3538952 | tf_op jit(solution)/shard_map/ppermute | solution.py:480
  1188.6 137.9 %collective-permute-start.25 = (bf16[48,96,128]{2,1,0:T(8,128)(2,1)}, bf16[48,96,128]{2,1,0:T(8,128)(2,1)}, u32[]{:S(2)}, u32[]{:S(2)}) collective-permute-start(bf16[48,96,128]{2,1,0:T(8,128)(2,1)} %copy-done.45), channel_id=1, source_target_pairs={{0,24},{4,28},{8,16},{12,20},{16,8},{20,12},{24,0},{28,4},{1,25},{... | collective-permute-start | bytes 3538952 | tf_op jit(solution)/shard_map/ppermute | solution.py:480
  1190.1 155.5 %collective-permute-start.10 = (bf16[48,96,128]{2,1,0:T(8,128)(2,1)}, bf16[48,96,128]{2,1,0:T(8,128)(2,1)S(1)}, u32[]{:S(2)}, u32[]{:S(2)}) collective-permute-start(bf16[48,96,128]{2,1,0:T(8,128)(2,1)} %copy-done.51), channel_id=1, source_target_pairs={{0,8},{4,12},{8,0},{12,4},{16,24},{20,28},{24,16},{28,20},{1,9},{5... | collective-permute-start | bytes 3538952 | tf_op jit(solution)/shard_map/ppermute | solution.py:480
  1193.5 74.5 %copy-start.47 = (bf16[48,96,128]{2,1,0:T(8,128)(2,1)S(1)}, bf16[48,96,128]{2,1,0:T(8,128)(2,1)}, u32[]{:S(2)}) copy-start(bf16[48,96,128]{2,1,0:T(8,128)(2,1)} %copy-done.46) | copy-start | bytes 3538948
  1193.5 77.1 %copy-start.3 = (bf16[48,96,128]{2,1,0:T(8,128)(2,1)S(1)}, bf16[48,96,128]{2,1,0:T(8,128)(2,1)}, u32[]{:S(2)}) copy-start(bf16[48,96,128]{2,1,0:T(8,128)(2,1)} %get-tuple-element.112.refs_4_) | copy-start | bytes 3538948
  1193.5 77.1 %copy-start.8 = (bf16[48,96,128]{2,1,0:T(8,128)(2,1)S(1)}, bf16[48,96,128]{2,1,0:T(8,128)(2,1)}, u32[]{:S(2)}) copy-start(bf16[48,96,128]{2,1,0:T(8,128)(2,1)} %copy-done.6) | copy-start | bytes 3538948
  1193.5 77.2 %copy-start.11 = (bf16[48,96,128]{2,1,0:T(8,128)(2,1)S(1)}, bf16[48,96,128]{2,1,0:T(8,128)(2,1)}, u32[]{:S(2)}) copy-start(bf16[48,96,128]{2,1,0:T(8,128)(2,1)} %copy-done.9) | copy-start | bytes 3538948
  1193.5 77.2 %copy-start.14 = (bf16[48,96,128]{2,1,0:T(8,128)(2,1)S(1)}, bf16[48,96,128]{2,1,0:T(8,128)(2,1)}, u32[]{:S(2)}) copy-start(bf16[48,96,128]{2,1,0:T(8,128)(2,1)} %copy-done.12) | copy-start | bytes 3538948
  1193.5 77.2 %copy-start.16 = (bf16[48,96,128]{2,1,0:T(8,128)(2,1)S(1)}, bf16[48,96,128]{2,1,0:T(8,128)(2,1)}, u32[]{:S(2)}) copy-start(bf16[48,96,128]{2,1,0:T(8,128)(2,1)} %copy-done.15) | copy-start | bytes 3538948
  1193.5 77.2 %copy-start.18 = (bf16[48,96,128]{2,1,0:T(8,128)(2,1)S(1)}, bf16[48,96,128]{2,1,0:T(8,128)(2,1)}, u32[]{:S(2)}) copy-start(bf16[48,96,128]{2,1,0:T(8,128)(2,1)} %copy-done.17) | copy-start | bytes 3538948
  1249.8 169.8 %collective-permute-start.11 = (bf16[48,96,128]{2,1,0:T(8,128)(2,1)}, bf16[48,96,128]{2,1,0:T(8,128)(2,1)S(1)}, u32[]{:S(2)}, u32[]{:S(2)}) collective-permute-start(bf16[48,96,128]{2,1,0:T(8,128)(2,1)} %copy-done.49), channel_id=1, source_target_pairs={{0,16},{4,20},{8,24},{12,28},{16,0},{20,4},{24,8},{28,12},{1,17},{... | collective-permute-start | bytes 3538952 | tf_op jit(solution)/shard_map/ppermute | solution.py:480
  1268.0 152.6 %collective-permute-start.12 = (bf16[48,96,128]{2,1,0:T(8,128)(2,1)S(1)}, bf16[48,96,128]{2,1,0:T(8,128)(2,1)S(1)}, u32[]{:S(2)}, u32[]{:S(2)}) collective-permute-start(bf16[48,96,128]{2,1,0:T(8,128)(2,1)S(1)} %copy-done.47), channel_id=1, source_target_pairs={{0,24},{4,28},{8,16},{12,20},{16,8},{20,12},{24,0},{28,4},{1,25},{... | collective-permute-start | bytes 3538952 | tf_op jit(solution)/shard_map/ppermute | solution.py:480
  1270.6 177.0 %collective-permute-start.37 = (bf16[48,96,128]{2,1,0:T(8,128)(2,1)}, bf16[48,96,128]{2,1,0:T(8,128)(2,1)S(1)}, u32[]{:S(2)}, u32[]{:S(2)}) collective-permute-start(bf16[48,96,128]{2,1,0:T(8,128)(2,1)} %get-tuple-element.89), channel_id=1, source_target_pairs={{0,8},{4,12},{8,0},{12,4},{16,24},{20,28},{24,16},{28,20},{1,9},{5... | collective-permute-start | bytes 3538952 | tf_op jit(solution)/shard_map/ppermute | solution.py:480
  1326.5 298.5 %collective-permute-start.38 = (bf16[48,96,128]{2,1,0:T(8,128)(2,1)}, bf16[48,96,128]{2,1,0:T(8,128)(2,1)}, u32[]{:S(2)}, u32[]{:S(2)}) collective-permute-start(bf16[48,96,128]{2,1,0:T(8,128)(2,1)} %get-tuple-element.90), channel_id=1, source_target_pairs={{0,16},{4,20},{8,24},{12,28},{16,0},{20,4},{24,8},{28,12},{1,17},{... | collective-permute-start | bytes 3538952 | tf_op jit(solution)/shard_map/ppermute | solution.py:480
  1345.6 279.4 %collective-permute-start.39 = (bf16[48,96,128]{2,1,0:T(8,128)(2,1)}, bf16[48,96,128]{2,1,0:T(8,128)(2,1)}, u32[]{:S(2)}, u32[]{:S(2)}) collective-permute-start(bf16[48,96,128]{2,1,0:T(8,128)(2,1)} %get-tuple-element.91), channel_id=1, source_target_pairs={{0,24},{4,28},{8,16},{12,20},{16,8},{20,12},{24,0},{28,4},{1,25},{... | collective-permute-start | bytes 3538952 | tf_op jit(solution)/shard_map/ppermute | solution.py:480
  1420.6 212.4 %collective-permute-start.30 = (bf16[48,96,128]{2,1,0:T(8,128)(2,1)}, bf16[48,96,128]{2,1,0:T(8,128)(2,1)S(1)}, u32[]{:S(2)}, u32[]{:S(2)}) collective-permute-start(bf16[48,96,128]{2,1,0:T(8,128)(2,1)} %get-tuple-element.80), channel_id=1, source_target_pairs={{0,8},{4,12},{8,0},{12,4},{16,24},{20,28},{24,16},{28,20},{1,9},{5... | collective-permute-start | bytes 3538952 | tf_op jit(solution)/shard_map/ppermute | solution.py:480
  1421.7 211.4 %collective-permute-start.31 = (bf16[48,96,128]{2,1,0:T(8,128)(2,1)}, bf16[48,96,128]{2,1,0:T(8,128)(2,1)S(1)}, u32[]{:S(2)}, u32[]{:S(2)}) collective-permute-start(bf16[48,96,128]{2,1,0:T(8,128)(2,1)} %get-tuple-element.81), channel_id=1, source_target_pairs={{0,16},{4,20},{8,24},{12,28},{16,0},{20,4},{24,8},{28,12},{1,17},{... | collective-permute-start | bytes 3538952 | tf_op jit(solution)/shard_map/ppermute | solution.py:480
  1448.6 184.4 %collective-permute-start.32 = (bf16[48,96,128]{2,1,0:T(8,128)(2,1)}, bf16[48,96,128]{2,1,0:T(8,128)(2,1)}, u32[]{:S(2)}, u32[]{:S(2)}) collective-permute-start(bf16[48,96,128]{2,1,0:T(8,128)(2,1)} %get-tuple-element.82), channel_id=1, source_target_pairs={{0,24},{4,28},{8,16},{12,20},{16,8},{20,12},{24,0},{28,4},{1,25},{... | collective-permute-start | bytes 3538952 | tf_op jit(solution)/shard_map/ppermute | solution.py:480
  1472.4 148.8 %copy-start.60 = (f32[4,128]{1,0:T(4,128)S(1)}, f32[4,128]{1,0:T(4,128)}, u32[]{:S(2)}) copy-start(f32[4,128]{1,0:T(4,128)} %param.17) | copy-start | bytes 6148
  (38 other events, 303.2 us)
Sparse Core Ops, SparseCore 0:
  1461.9 158.1 all-reduce.1

commit v2 on v1

v2 whole, which is shorter than its diff:
```python
import math

import jax
import jax.numpy as jnp
from jax import lax
from jax.experimental import pallas as pl
from jax.experimental.pallas import tpu as pltpu
from jax.sharding import PartitionSpec as P

EPS = 1e-05
MOMENT = 0.9
DECAY = 0.8
LOW = jnp.bfloat16
F32 = jnp.float32
MIB = 1 << 20
SHARE = 600_000_000


def sds(shape, dtype):
    return jax.ShapeDtypeStruct(shape, dtype)


def params(mib):
    return pltpu.CompilerParams(vmem_limit_bytes=mib * MIB)


def cost(micros):
    return pl.CostEstimate(flops=int(micros * SHARE), bytes_accessed=0, transcendentals=0)


def sigmoid(v):
    return 0.5 * jnp.tanh(0.5 * v) + 0.5


def normalize(v):
    center = v - jnp.mean(v, axis=-1, keepdims=True)
    inverse = lax.rsqrt(jnp.mean(center * center, axis=-1, keepdims=True) + EPS)
    return center * inverse, inverse


def norm_back(grad_hat, normed, inverse):
    first = jnp.mean(grad_hat, axis=-1, keepdims=True)
    second = jnp.mean(grad_hat * normed, axis=-1, keepdims=True)
    return inverse * (grad_hat - first - normed * second)


def dot(a, b, ca=1, cb=0):
    return lax.dot_general(a, b, (((ca,), (cb,)), ((), ())), preferred_element_type=F32)


def eights(v):
    return jnp.sum(v.reshape(-1, 8, v.shape[-1]), axis=0)


def to_major(v):
    return jnp.swapaxes(jnp.swapaxes(v, 1, 2), 0, 1)


def to_minor(v):
    return jnp.swapaxes(jnp.swapaxes(v, 0, 1), 1, 2)


def row_mask(rowm, colm, start, count):
    m = rowm[pl.ds(start, count)][:, None, :] * colm[...][None]
    return m.reshape(-1, m.shape[-1])


def pick_rows(nrow):
    return 16 if nrow % 16 == 0 else 8


def whole_spec(array):
    return pl.BlockSpec(array.shape, lambda s: (0,) * len(array.shape))


def edges_kernel(sub, z_ref, norms, proj, rowm, colm, left, right):
    rows, nk, chan = z_ref.shape
    base = pl.program_id(0) * rows

    def step(t, _):
        at = t * sub
        z = z_ref[pl.ds(at, sub)].astype(F32).reshape(-1, chan)
        hat, _ = normalize(z)
        u = (hat * norms[0:1] + norms[1:2]).astype(LOW)
        p = dot(u, proj[...])
        m = row_mask(rowm, colm, base + at, sub)
        lv = sigmoid(p[:, chan:2 * chan]) * p[:, :chan] * m
        rv = sigmoid(p[:, 3 * chan:]) * p[:, 2 * chan:3 * chan] * m
        left[pl.ds(at, sub)] = lv.astype(LOW).reshape(sub, nk, chan)
        right[pl.ds(at, sub)] = rv.astype(LOW).reshape(sub, nk, chan)
        return 0

    lax.fori_loop(0, rows // sub, step, 0)


def edges_call(z, norms, proj, rowm, colm):
    ni, nk, chan = z.shape
    rows = 16
    flat = pl.BlockSpec((rows, nk, chan), lambda s: (s, 0, 0))
    return pl.pallas_call(
        lambda *refs: edges_kernel(4, *refs),
        grid=(ni // rows,),
        in_specs=[flat] + [whole_spec(v) for v in (norms, proj, rowm, colm)],
        out_specs=[flat, flat],
        out_shape=[sds(z.shape, LOW)] * 2,
        compiler_params=params(32),
        cost_estimate=cost(27),
        name="edges",
    )(z, norms, proj, rowm, colm)


def product_kernel(nparts, unroll, sc, left, own, other, out, lt, rt, xt):
    s = pl.program_id(0)
    steps = pl.num_programs(0) // 2
    rows, nk, chan = left.shape
    nrow = out.shape[2] // 2
    half = nparts * nrow
    core = sc[0]

    @pl.when(s < steps)
    def _():
        at = pl.multiple_of(s * rows, rows)
        lt[:, pl.ds(at, rows), :] = to_major(left[...])
        rt[:, pl.ds(pl.multiple_of(core * half + at, rows), rows), :] = to_major(own[...])
        rt[:, pl.ds(pl.multiple_of((1 - core) * half + at, rows), rows), :] = to_major(other[...])

    @pl.when(s == steps)
    def _():
        def multiply(c, _):
            xt[c] = dot(lt[c], rt[c], 1, 1).astype(LOW)
            return 0
        lax.fori_loop(0, chan, multiply, 0, unroll=unroll)

    @pl.when(s >= steps)
    def _():
        x = to_minor(xt[:, pl.ds(pl.multiple_of((s - steps) * rows, rows), rows), :])
        for q in range(nparts):
            for c in range(2):
                start = c * half + q * nrow
                out[q, :, c * nrow:(c + 1) * nrow] = x[:, start:start + nrow]


def phases(ni, rows):
    steps = ni // rows
    inward = lambda s: jnp.minimum(s, steps - 1)
    outward = lambda s: jnp.maximum(s - steps, 0)
    return steps, inward, outward


def product_call(scal, left, own, other, nparts):
    ni, nk, chan = left.shape
    nrow = ni // nparts
    nj = 2 * ni
    rows = pick_rows(nrow)
    steps, inward, outward = phases(ni, rows)
    edge = pl.BlockSpec((rows, nk, chan), lambda s, sc: (inward(s), 0, 0))
    return pl.pallas_call(
        lambda *refs: product_kernel(nparts, 4, *refs),
        grid_spec=pltpu.PrefetchScalarGridSpec(
            num_scalar_prefetch=1,
            grid=(2 * steps,),
            in_specs=[edge] * 3,
            out_specs=pl.BlockSpec((nparts, rows, 2 * nrow, chan),
                                   lambda s, sc: (0, outward(s), 0, 0)),
            scratch_shapes=[pltpu.VMEM((chan, ni, nk), LOW), pltpu.VMEM((chan, nj, nk), LOW),
                            pltpu.VMEM((chan, ni, nj), LOW)],
        ),
        out_shape=sds((nparts, ni, 2 * nrow, chan), LOW),
        compiler_params=params(56),
        cost_estimate=cost(33),
        name="product",
    )(scal, left, own, other)


def middle_kernel(sub, z_ref, g_ref, x_ref, norms, gate_w, out_w, new, gx, gate_grad, wout, nout,
                  ylow, glow):
    rows, nk, chan = z_ref.shape

    @pl.when(pl.program_id(0) == 0)
    def _():
        wout[...] = jnp.zeros_like(wout)
        nout[...] = jnp.zeros_like(nout)

    def step(t, _):
        rng = pl.ds(t * sub, sub)
        flat = pl.ds(pl.multiple_of(t * sub * nk, sub * nk), sub * nk)
        z = z_ref[rng].astype(F32).reshape(-1, chan)
        zhat, _ = normalize(z)
        u = (zhat * norms[0:1] + norms[1:2]).astype(LOW)
        gate = sigmoid(dot(u, gate_w[...]))
        hat, inverse = normalize(x_ref[rng].astype(F32).reshape(-1, chan))
        y = (hat * norms[2:3] + norms[3:4]).astype(LOW)
        out = dot(y, out_w[...])
        so = gate * out
        new[rng] = (z + so).astype(LOW).reshape(sub, nk, chan)
        g = g_ref[rng].astype(F32).reshape(-1, chan)
        go = (g * gate).astype(LOW)
        gate_grad[rng] = (g * so * (1.0 - gate)).astype(LOW).reshape(sub, nk, chan)
        ylow[flat] = y
        glow[flat] = go
        gy = dot(go, out_w[...], 1, 1)
        nout[0] += eights(gy * hat)
        nout[1] += eights(gy)
        gx[rng] = norm_back(gy * norms[2:3], hat, inverse).astype(LOW).reshape(sub, nk, chan)
        return 0

    lax.fori_loop(0, rows // sub, step, 0)
    wout[...] += dot(ylow[...], glow[...], 0, 0)


def middle_call(z, g, x, norms, gate_w, out_w):
    ni, nk, chan = z.shape
    rows = 16
    flat = pl.BlockSpec((rows, nk, chan), lambda s: (s, 0, 0))
    low = pltpu.VMEM((rows * nk, chan), LOW)
    sums = [sds((chan, chan), F32), sds((2, 8, chan), F32)]
    return pl.pallas_call(
        lambda *refs: middle_kernel(4, *refs),
        grid=(ni // rows,),
        in_specs=[flat] * 3 + [whole_spec(v) for v in (norms, gate_w, out_w)],
        out_specs=[flat] * 3 + [whole_spec(v) for v in sums],
        out_shape=[sds(z.shape, LOW)] * 3 + sums,
        scratch_shapes=[low, low],
        compiler_params=params(40),
        cost_estimate=cost(40),
        name="middle",
    )(z, g, x, norms, gate_w, out_w)


def edge_grad_kernel(nparts, unroll, sc, left, own, other, gx, gleft, keep, send, lt, rt, gt):
    s = pl.program_id(0)
    steps = pl.num_programs(0) // 2
    rows, nk, chan = left.shape
    nrow = gx.shape[2] // 2
    half = nparts * nrow
    core = sc[0]

    @pl.when(s < steps)
    def _():
        at = pl.multiple_of(s * rows, rows)
        lt[:, pl.ds(at, rows), :] = to_major(left[...])
        rt[:, pl.ds(pl.multiple_of(core * half + at, rows), rows), :] = to_major(own[...])
        rt[:, pl.ds(pl.multiple_of((1 - core) * half + at, rows), rows), :] = to_major(other[...])
        g = jnp.concatenate([
            gx[q, :, c * nrow:(c + 1) * nrow] for c in range(2) for q in range(nparts)
        ], axis=1)
        gt[:, pl.ds(at, rows), :] = to_major(g)

    @pl.when(s == steps)
    def _():
        def multiply(c, _):
            lc, rc, gc = lt[c], rt[c], gt[c]
            lt[c] = dot(gc, rc, 1, 0).astype(LOW)
            rt[c] = dot(gc, lc, 0, 0).astype(LOW)
            return 0
        lax.fori_loop(0, chan, multiply, 0, unroll=unroll)

    @pl.when(s >= steps)
    def _():
        at = pl.multiple_of((s - steps) * rows, rows)
        gleft[...] = to_minor(lt[:, pl.ds(at, rows), :])
        keep[...] = to_minor(rt[:, pl.ds(pl.multiple_of(core * half + at, rows), rows), :])
        send[...] = to_minor(rt[:, pl.ds(pl.multiple_of((1 - core) * half + at, rows), rows), :])


def edge_grad_call(scal, left, own, other, gx):
    nparts = gx.shape[0]
    ni, nk, chan = left.shape
    nrow = ni // nparts
    nj = 2 * ni
    rows = pick_rows(nrow)
    steps, inward, outward = phases(ni, rows)
    edge = pl.BlockSpec((rows, nk, chan), lambda s, sc: (inward(s), 0, 0))
    back = pl.BlockSpec((rows, nk, chan), lambda s, sc: (outward(s), 0, 0))
    return pl.pallas_call(
        lambda *refs: edge_grad_kernel(nparts, 4, *refs),
        grid_spec=pltpu.PrefetchScalarGridSpec(
            num_scalar_prefetch=1,
            grid=(2 * steps,),
            in_specs=[edge] * 3 + [pl.BlockSpec((nparts, rows, 2 * nrow, chan),
                                                lambda s, sc: (0, inward(s), 0, 0))],
            out_specs=[back] * 3,
            scratch_shapes=[pltpu.VMEM((chan, ni, nk), LOW), pltpu.VMEM((chan, nj, nk), LOW),
                            pltpu.VMEM((chan, ni, nj), LOW)],
        ),
        out_shape=[sds(left.shape, LOW)] * 3,
        compiler_params=params(58),
        cost_estimate=cost(50),
        name="edge_grad",
    )(scal, left, own, other, gx)


def input_kernel(sub, z_ref, g_ref, gleft, keep, got, gate_grad, norms, proj, rowm, colm,
                 out, wproj, nin, ulow, plow):
    rows, nk, chan = z_ref.shape
    base = pl.program_id(0) * rows

    @pl.when(pl.program_id(0) == 0)
    def _():
        wproj[...] = jnp.zeros_like(wproj)
        nin[...] = jnp.zeros_like(nin)

    def step(t, _):
        at = t * sub
        rng = pl.ds(at, sub)
        flat = pl.ds(pl.multiple_of(at * nk, sub * nk), sub * nk)
        z = z_ref[rng].astype(F32).reshape(-1, chan)
        hat, inverse = normalize(z)
        u = (hat * norms[0:1] + norms[1:2]).astype(LOW)
        ulow[flat] = u
        p = dot(u, proj[:, :4 * chan])
        m = row_mask(rowm, colm, base + at, sub)
        gl = gleft[rng].astype(F32).reshape(-1, chan) * m
        gr = (keep[rng].astype(F32) + got[rng].astype(F32)).reshape(-1, chan) * m
        for n, grad in ((0, gl), (2, gr)):
            sig = sigmoid(p[:, (n + 1) * chan:(n + 2) * chan])
            first = grad * sig
            plow[flat, n * chan:(n + 1) * chan] = first.astype(LOW)
            second = first * (p[:, n * chan:(n + 1) * chan] * (1.0 - sig))
            plow[flat, (n + 1) * chan:(n + 2) * chan] = second.astype(LOW)
        plow[flat, 4 * chan:] = gate_grad[rng].reshape(-1, chan)
        gu = dot(plow[flat], proj[...], 1, 1)
        nin[0] += eights(gu * hat)
        nin[1] += eights(gu)
        g = g_ref[rng].astype(F32).reshape(-1, chan)
        grad_z = g + norm_back(gu * norms[0:1], hat, inverse)
        out[rng] = grad_z.astype(LOW).reshape(sub, nk, chan)
        return 0

    lax.fori_loop(0, rows // sub, step, 0)
    wproj[...] += dot(ulow[...], plow[...], 0, 0)


def input_call(z, g, gleft, keep, got, gate_grad, norms, proj, rowm, colm):
    ni, nk, chan = z.shape
    rows = 16
    flat = pl.BlockSpec((rows, nk, chan), lambda s: (s, 0, 0))
    width = proj.shape[1]
    sums = [sds((chan, width), F32), sds((2, 8, chan), F32)]
    return pl.pallas_call(
        lambda *refs: input_kernel(4, *refs),
        grid=(ni // rows,),
        in_specs=[flat] * 6 + [whole_spec(v) for v in (norms, proj, rowm, colm)],
        out_specs=[flat] + [whole_spec(v) for v in sums],
        out_shape=[sds(z.shape, LOW)] + sums,
        scratch_shapes=[pltpu.VMEM((rows * nk, chan), LOW), pltpu.VMEM((rows * nk, width), LOW)],
        compiler_params=params(40),
        cost_estimate=cost(54),
        name="input_grad",
    )(z, g, gleft, keep, got, gate_grad, norms, proj, rowm, colm)


def place_call(blocks, b, batches, whole=None):
    count, nrow, nk, chan = blocks.shape
    half = nrow // 2

    def kernel(*refs):
        refs[-1][...] = refs[0][...]

    args = [blocks] + ([] if whole is None else [whole])
    return pl.pallas_call(
        kernel,
        grid=(count, 2),
        in_specs=[pl.BlockSpec((1, half, nk, chan), lambda g, r: (g, r, 0, 0))]
        + [pl.BlockSpec(memory_space=pl.ANY)] * (len(args) - 1),
        out_specs=pl.BlockSpec((1, half, nk, chan), lambda g, r: (g * batches + b, r, 0, 0)),
        out_shape=sds((count * batches, nrow, nk, chan), LOW),
        input_output_aliases={} if whole is None else {1: 0},
        compiler_params=params(16),
        cost_estimate=cost(5),
        name="place",
    )(*args)


def shards(rows, cols, pair, cotangent, residue_mask, weights, norm_params, momentum,
           norm_momentum, average, norm_average):
    zeds = rows // 2
    crops, nrow, ncol, chan = pair.shape
    batches = crops // zeds
    length = residue_mask.shape[1]
    ni = zeds * nrow
    row = lax.axis_index("row")
    col = lax.axis_index("col")
    zed, core = row // 2, row % 2
    weight_low = weights.astype(LOW)
    project_low = jnp.concatenate([weight_low[n] for n in range(5)], axis=1)
    mask_float = residue_mask.astype(F32)
    scal = jnp.stack([core]).astype(jnp.int32)
    same_core = [[2 * q + c for q in range(zeds)] for c in range(2)]

    def zswap(blocks):
        return lax.all_to_all(blocks, "row", 0, 0, tiled=True, axis_index_groups=same_core)

    def coreswap(block):
        return lax.ppermute(block, "row", [(r, r ^ 1) for r in range(rows)])

    def after(values, *others):
        return lax.optimization_barrier((values, others))[0]

    def flat(v):
        return v.reshape(ni, ncol, chan)

    def blocked(v):
        return v.reshape(zeds, nrow, ncol, chan)

    def sum_all(term):
        count = term.shape[0] // 2
        mine = lax.dynamic_slice_in_dim(term, core * count, count, 0)
        mine = mine + coreswap(lax.dynamic_slice_in_dim(term, (1 - core) * count, count, 0))
        step = 1
        while step < cols:
            mine = mine + lax.ppermute(mine, "col", [(q, q ^ step) for q in range(cols)])
            step *= 2
        step = 2
        while step < rows:
            mine = mine + lax.ppermute(mine, "row", [(r, r ^ step) for r in range(rows)])
            step *= 2
        got = coreswap(mine)
        return jnp.concatenate([jnp.where(core == 0, mine, got), jnp.where(core == 0, got, mine)])

    masks = []
    for b in range(batches):
        crop_mask = lax.dynamic_index_in_dim(mask_float, zed * batches + b, 0, keepdims=False)
        by_block = crop_mask.reshape(zeds, 2, nrow)
        rowm = lax.dynamic_index_in_dim(by_block, core, 1, keepdims=False).reshape(-1)
        colm = lax.dynamic_slice_in_dim(crop_mask, col * ncol, ncol, 0)
        masks.append((jnp.broadcast_to(rowm[:, None], (ni, chan)),
                      jnp.broadcast_to(colm[:, None], (ncol, chan))))

    def take(whole, b):
        return whole.reshape(zeds, batches, nrow, ncol, chan)[:, b]

    def edges(b):
        left, right = edges_call(pairs[b], norm_params, project_low[:, :4 * chan], *masks[b])
        return left, right, coreswap(right)

    pairs, cots, kept, reduced = [], [], [], []
    for b in range(batches):
        block = zswap(after(take(pair, b), pairs[b - 1]) if b else take(pair, b))
        pairs.append(flat(block))
    for b in range(batches):
        block = zswap(after(take(cotangent, b), cots[b - 1] if b else pairs[-1]))
        cots.append(flat(block))
    for b in range(batches):
        if b:
            pairs[b] = after(pairs[b], part)
        kept.append(edges(b))
        part = product_call(scal, *kept[b], cols)
        if b:
            part = after(part, reduced[b - 1])
        reduced.append(flat(lax.psum_scatter(part, "col", scatter_dimension=0, tiled=True)))
    gathered, news, gates, sums = [], [], [], []
    for b in range(batches):
        new, gx, gate_grad, wout, nout = middle_call(
            pairs[b], cots[b], reduced[b], norm_params, weight_low[4], weight_low[5])
        news.append(zswap(blocked(new)))
        gx = after(gx, gathered[b - 1] if b else reduced[-1])
        gathered.append(lax.all_gather(gx, "col", axis=0))
        gates.append(gate_grad)
        sums.append((wout, nout))
    backs, flats = [], []
    for b in range(batches):
        gx = after(gathered[b], out) if b else gathered[b]
        gleft, keep, send = edge_grad_call(scal, *kept[b], gx)
        got = coreswap(send)
        out = input_call(pairs[b], cots[b], gleft, keep, got, gates[b], norm_params, project_low,
                         *masks[b])
        back, wproj, nin = out
        backs.append(zswap(blocked(back)))
        wout, nout = sums[b]
        wproj = jnp.transpose(wproj.reshape(chan, 5, chan), (1, 0, 2)).reshape(5 * chan, chan)
        flats.append(jnp.concatenate(
            [wproj, wout, jnp.sum(nin, axis=1), jnp.sum(nout, axis=1)], axis=0))

    def collect(pieces):
        whole = None
        for b in range(batches):
            whole = place_call(pieces[b], b, batches, whole)
        return whole

    new_pair = collect(news)
    pair_grad = collect(backs)
    grads = sum_all(sum(flats))
    grad_weights = grads[: 6 * chan].reshape(weights.shape)
    grad_norms = grads[6 * chan:]
    rate = 0.1 / (length * math.sqrt(crops))
    new_momentum = MOMENT * momentum + grad_weights
    new_weights = weights - rate * (grad_weights + MOMENT * new_momentum)
    new_average = DECAY * average + (1.0 - DECAY) * new_weights
    new_norm_momentum = MOMENT * norm_momentum + grad_norms
    new_norms = norm_params - rate * (grad_norms + MOMENT * new_norm_momentum)
    new_norm_average = DECAY * norm_average + (1.0 - DECAY) * new_norms
    return (new_pair, pair_grad, new_weights, new_momentum, new_average, new_norms,
            new_norm_momentum, new_norm_average)


def solution(mesh):
    rows, cols = mesh.shape["row"], mesh.shape["col"]
    tiled = P(None, "row", "col", None)

    def body(*args):
        return shards(rows, cols, *args)

    return jax.shard_map(
        body,
        mesh=mesh,
        in_specs=(tiled, tiled) + (P(),) * 7,
        out_specs=(tiled, tiled) + (P(),) * 6,
        check_vma=False,
    )
```

time: 1650 us -> 1210 us (0.73)
  waiting for transfers between devices: 949 us -> 465 us
  blocking collectives: 0 us -> 219 us
  starting transfers between devices: 187 us -> 41.7 us
    ppermute x36 -> x4, waiting for transfers between devices: 807 us -> 87.1 us  [the longest x2 76.7 us: sum_all(): lax.ppermute(mine, 'row', [(r, r ^ step) for r in range(rows)])]
    all_to_all x0 -> x6, waiting for transfers between devices: none -> 312 us  [zswap(): lax.all_to_all(blocks, 'row', 0, 0, tiled=True, axis_index_groups=same_core)]
    all_to_all x0 -> x2, blocking collectives: none -> 219 us  [zswap(): lax.all_to_all(blocks, 'row', 0, 0, tiled=True, axis_index_groups=same_core)]
    ppermute x36 -> x4, starting transfers between devices: 187 us -> 9.74 us  [the longest x2 6.68 us: sum_all(): lax.ppermute(mine, 'row', [(r, r ^ step) for r in range(rows)])]
    psum x1 -> x0, waiting for transfers between devices: 142 us -> none  [shards(): flat = lax.psum(sum(flats), ('row', 'col'))]
    all_gather x0 -> x2, waiting for transfers between devices: none -> 34.5 us  [shards(): gathered.append(lax.all_gather(gx, 'col', axis=0))]
    all_to_all x0 -> x6, starting transfers between devices: none -> 31.7 us  [zswap(): lax.all_to_all(blocks, 'row', 0, 0, tiled=True, axis_index_groups=same_core)]
    ppermute x4 -> x6, waiting for transfers between devices: 0.01 us -> 20.3 us  [coreswap(): return lax.ppermute(block, 'row', [(r, r ^ 1) for r in range(rows)])]
  transfers between devices with their start and end apart: 41 -> 20, of which waited for: 18 -> 15; matrix products, arithmetic and copies ran while one was open for 2% -> 1% of each run, Pallas kernels for 24% -> 29%
where the time goes in v2:
time: 1210 us
  waiting for transfers between devices  465 us (38%)
  Pallas kernels  426 us (35%)
  blocking collectives  219 us (18%)
  local copies, waits for them, and re-layouts  44.1 us (4%)
  starting transfers between devices  41.7 us (3%)
  between operations  14.3 us (1%)
    all_to_all x6, waiting for transfers between devices, zswap(): lax.all_to_all(blocks, 'row', 0, 0, tiled=True, axis_index_groups=same_core)  312 us
    all_to_all x2, blocking collectives, zswap(): lax.all_to_all(blocks, 'row', 0, 0, tiled=True, axis_index_groups=same_core)  219 us
    pallas_call x2, Pallas kernels, edge_grad_call(): pl.pallas_call(lambda *refs: edge_grad_kernel(nparts, 4, *refs), grid_spe...  102 us
    pallas_call x2, Pallas kernels, input_call(): pl.pallas_call(lambda *refs: input_kernel(4, *refs), grid=(ni // rows,),...  101 us
    ppermute x2, waiting for transfers between devices, sum_all(): lax.ppermute(mine, 'row', [(r, r ^ step) for r in range(rows)])  76.7 us
    pallas_call x2, Pallas kernels, middle_call(): pl.pallas_call(lambda *refs: middle_kernel(4, *refs), grid=(ni // rows,),...  72.9 us
    pallas_call x2, Pallas kernels, product_call(): pl.pallas_call(lambda *refs: product_kernel(nparts, 4, *refs), grid_spec=...  71.8 us
    pallas_call x2, Pallas kernels, edges_call(): pl.pallas_call(lambda *refs: edges_kernel(4, *refs), grid=(ni // rows,),...  51.8 us
  transfers between devices with their start and end apart: 20, of which 15 were waited for; matrix products, arithmetic and copies ran while one was open for 1% of the time, Pallas kernels for 29%

profile of v2, /device:TPU:0, one launch (start us, length us, event | category | flops | bytes accessed | tf_op | source)
XLA Modules:
  0.0 1212.5 jit_solution(2070237034464162063)
XLA Ops:
  7.2 9.1 slice_bitcast_fusion.2
  16.3 6.5 all-to-all-start
  22.8 0.1 reshape.90
  22.9 0.1 broadcast_in_dim.30
  23.2 104.3 %all-to-all-done = bf16[4,48,96,128]{3,2,1,0:T(8,128)(2,1)} async-done(((bf16[4,48,96,128]{3,2,1,0:T(8,128)(2,1)}), bf16[4,48,96,128]{3,2,1,0:T(8,128)(2,1)}, u32[]{:S(2)}, u32[]{:S(2)}) %all-to-all-start) | async-done | bytes 4718624 | tf_op jit(solution)/shard_map/all_to_all | solution.py:392
  127.7 25.9 %edges.2 = (bf16[192,96,128]{2,1,0:T(8,128)(2,1)S(1)}, bf16[192,96,128]{2,1,0:T(8,128)(2,1)S(1)}) custom-call(bf16[192,96,128]{2,1,0:T(8,128)(2,1)} %bitcast.3.refs_0_, f32[4,128]{1,0:T(4,128)S(1)} %copy-done.14, bf16[128,512]{1,0:T(8,128)(2,1)S(1)} %pad_maximum_fusion.1.refs_2_, f32[192,128]{1,0:T(8,128)S(1)} %broadcast_in_dim.31.refs_3_.refs_8_, ...), custom_call_target="tpu_custom_call" | custom-call | flops 16199999488 | tf_op jit(solution)/shard_map/edges/pallas_call | solution.py:100
  153.7 2.1 copy-done.18
  155.8 7.9 collective-permute-done.refs_3_
  163.7 2.2 copy-done.31
  165.9 35.8 %product.2 = bf16[4,192,96,128]{3,2,1,0:T(8,128)(2,1)} custom-call(s32[1]{0:T(128)} %bitcast.5.refs_0_, bf16[192,96,128]{2,1,0:T(8,128)(2,1)} %copy-done.18, bf16[192,96,128]{2,1,0:T(8,128)(2,1)} %copy-done.16, bf16[192,96,128]{2,1,0:T(8,128)(2,1)} %copy-done.31), custom_call_target="tpu_custom_call" | custom-call | flops 19800000512 | tf_op jit(solution)/shard_map/product/pallas_call | solution.py:157
  201.7 5.0 all-to-all-start.1
  206.7 0.1 reshape.94
  206.9 104.8 %all-to-all-done.1 = bf16[4,48,96,128]{3,2,1,0:T(8,128)(2,1)} async-done(((bf16[4,48,96,128]{3,2,1,0:T(8,128)(2,1)}), bf16[4,48,96,128]{3,2,1,0:T(8,128)(2,1)}, u32[]{:S(2)}, u32[]{:S(2)}) %all-to-all-start.1) | async-done | bytes 4718624 | tf_op jit(solution)/shard_map/all_to_all | solution.py:392
  311.8 25.9 %edges.3 = (bf16[192,96,128]{2,1,0:T(8,128)(2,1)S(1)}, bf16[192,96,128]{2,1,0:T(8,128)(2,1)S(1)}) custom-call(bf16[192,96,128]{2,1,0:T(8,128)(2,1)} %bitcast.4.refs_0_, f32[4,128]{1,0:T(4,128)S(1)} %copy-done.14, bf16[128,512]{1,0:T(8,128)(2,1)S(1)} %pad_maximum_fusion.1.refs_2_, f32[192,128]{1,0:T(8,128)S(1)} %broadcast_in_dim.35.refs_3_.refs_8_, ...), custom_call_target="tpu_custom_call" | custom-call | flops 16199999488 | tf_op jit(solution)/shard_map/edges/pallas_call | solution.py:100
  337.8 2.2 copy-done.17
  340.0 7.9 collective-permute-done.1.refs_3_
  347.9 2.1 copy-done.30
  350.0 36.0 %product.3 = bf16[4,192,96,128]{3,2,1,0:T(8,128)(2,1)} custom-call(s32[1]{0:T(128)} %bitcast.5.refs_0_, bf16[192,96,128]{2,1,0:T(8,128)(2,1)} %copy-done.17, bf16[192,96,128]{2,1,0:T(8,128)(2,1)} %copy-done.15, bf16[192,96,128]{2,1,0:T(8,128)(2,1)} %copy-done.30), custom_call_target="tpu_custom_call" | custom-call | flops 19800000512 | tf_op jit(solution)/shard_map/product/pallas_call | solution.py:157
  386.1 7.6 slice_bitcast_fusion
  393.7 108.5 %all_to_all.40 = bf16[4,48,96,128]{3,2,1,0:T(8,128)(2,1)} all-to-all(bf16[4,48,96,128]{3,2,1,0:T(8,128)(2,1)S(1)} %get-tuple-element.46), channel_id=1, replica_groups={{0,8,16,24},{4,12,20,28},{1,9,17,25},{5,13,21,29},{2,10,18,26},{6,14,22..., dimensions={0} | all-to-all | bytes 9437184 | tf_op jit(solution)/shard_map/all_to_all | solution.py:392
  502.2 36.5 %middle.3 = (bf16[192,96,128]{2,1,0:T(8,128)(2,1)S(1)}, bf16[192,96,128]{2,1,0:T(8,128)(2,1)S(1)}, bf16[192,96,128]{2,1,0:T(8,128)(2,1)S(1)}, f32[128,128]{1,0:T(8,128)S(1)}, f32[2,8,128]{2,1,0:T(8,128)S(1)}) custom-call(bf16[192,96,128]{2,1,0:T(8,128)(2,1)} %bitcast.3.refs_0_, bf16[192,96,128]{2,1,0:T(8,128)(2,1)} %bitcast.75, ...), custom_call_target="tpu_custom_call" | custom-call | flops 24000000000 | tf_op jit(solution)/shard_map/middle/pallas_call | solution.py:217
  538.7 2.1 copy-done.3
  540.7 2.1 copy-done.5
  542.9 2.3 copy-done.20
  545.1 11.1 reduce-scatter.9.cloned.1.call-done
  556.3 110.6 %all_to_all.41 = bf16[4,48,96,128]{3,2,1,0:T(8,128)(2,1)} all-to-all(bf16[4,48,96,128]{3,2,1,0:T(8,128)(2,1)} %get-tuple-element.47), channel_id=1, replica_groups={{0,8,16,24},{4,12,20,28},{1,9,17,25},{5,13,21,29},{2,10,18,26},{6,14,22..., dimensions={0} | all-to-all | bytes 9437184 | tf_op jit(solution)/shard_map/all_to_all | solution.py:392
  666.9 36.4 %middle.2 = (bf16[192,96,128]{2,1,0:T(8,128)(2,1)S(1)}, bf16[192,96,128]{2,1,0:T(8,128)(2,1)S(1)}, bf16[192,96,128]{2,1,0:T(8,128)(2,1)S(1)}, f32[128,128]{1,0:T(8,128)S(1)}, f32[2,8,128]{2,1,0:T(8,128)S(1)}) custom-call(bf16[192,96,128]{2,1,0:T(8,128)(2,1)} %bitcast.4.refs_0_, bf16[192,96,128]{2,1,0:T(8,128)(2,1)} %bitcast.73, ...), custom_call_target="tpu_custom_call" | custom-call | flops 24000000000 | tf_op jit(solution)/shard_map/middle/pallas_call | solution.py:217
  703.4 2.2 copy-done.1
  705.6 2.2 copy-done.2
  707.7 2.1 copy-done.19
  709.9 24.2 %all-gather.5.cloned.1.call-done = bf16[768,96,128]{2,1,0:T(8,128)(2,1)} async-done(((bf16[192,96,128]{2,1,0:T(8,128)(2,1)}), bf16[768,96,128]{2,1,0:T(8,128)(2,1)}) %all-gather.5.cloned.1.call-update) | async-done | bytes 18874384 | tf_op jit(solution)/shard_map/all_gather | solution.py:458
  734.1 5.1 all-to-all-start.5
  739.3 51.7 %edge_grad.2 = (bf16[192,96,128]{2,1,0:T(8,128)(2,1)}, bf16[192,96,128]{2,1,0:T(8,128)(2,1)}, bf16[192,96,128]{2,1,0:T(8,128)(2,1)}) custom-call(s32[1]{0:T(128)} %bitcast.5.refs_0_, bf16[192,96,128]{2,1,0:T(8,128)(2,1)} %copy-done.18, bf16[192,96,128]{2,1,0:T(8,128)(2,1)} %copy-done.16, bf16[192,96,128]{2,1,0:T(8,128)(2,1)} %copy-done.31, ...), custom_call_target="tpu_custom_call" | custom-call | flops 30000001024 | tf_op jit(solution)/shard_map/edge_grad/pallas_call | solution.py:275
  791.0 52.8 %all-to-all-done.5.refs_0_ = bf16[4,48,96,128]{3,2,1,0:T(8,128)(2,1)} async-done(((bf16[4,48,96,128]{3,2,1,0:T(8,128)(2,1)}), bf16[4,48,96,128]{3,2,1,0:T(8,128)(2,1)}, u32[]{:S(2)}, u32[]{:S(2)}) %all-to-all-start.5) | async-done | bytes 4718624 | tf_op jit(solution)/shard_map/all_to_all | solution.py:392
  843.8 5.1 all-to-all-start.4
  849.0 50.3 %input_grad.2 = (bf16[192,96,128]{2,1,0:T(8,128)(2,1)S(1)}, f32[128,640]{1,0:T(8,128)S(1)}, f32[2,8,128]{2,1,0:T(8,128)S(1)}) custom-call(bf16[192,96,128]{2,1,0:T(8,128)(2,1)} %bitcast.3.refs_0_, bf16[192,96,128]{2,1,0:T(8,128)(2,1)} %bitcast.76, bf16[192,96,128]{2,1,0:T(8,128)(2,1)} %get-tuple-element.57.refs_2_, ...), custom_call_target="tpu_custom_call" | custom-call | flops 32399998976 | tf_op jit(solution)/shard_map/input_grad/pallas_call | solution.py:340
  899.4 2.1 copy-done.4
  901.5 10.3 all-gather.7.cloned.1.call-done
  911.8 49.8 %edge_grad.3 = (bf16[192,96,128]{2,1,0:T(8,128)(2,1)}, bf16[192,96,128]{2,1,0:T(8,128)(2,1)}, bf16[192,96,128]{2,1,0:T(8,128)(2,1)}) custom-call(s32[1]{0:T(128)} %bitcast.5.refs_0_, bf16[192,96,128]{2,1,0:T(8,128)(2,1)} %copy-done.17, bf16[192,96,128]{2,1,0:T(8,128)(2,1)} %copy-done.15, bf16[192,96,128]{2,1,0:T(8,128)(2,1)} %copy-done.30, ...), custom_call_target="tpu_custom_call" | custom-call | flops 30000001024 | tf_op jit(solution)/shard_map/edge_grad/pallas_call | solution.py:275
  961.6 5.1 all-to-all-start.7
  966.8 3.1 collective-permute-done.3.refs_4_
  969.9 50.3 %input_grad.3 = (bf16[192,96,128]{2,1,0:T(8,128)(2,1)S(1)}, f32[128,640]{1,0:T(8,128)S(1)}, f32[2,8,128]{2,1,0:T(8,128)S(1)}) custom-call(bf16[192,96,128]{2,1,0:T(8,128)(2,1)} %bitcast.4.refs_0_, bf16[192,96,128]{2,1,0:T(8,128)(2,1)} %bitcast.74, bf16[192,96,128]{2,1,0:T(8,128)(2,1)} %get-tuple-element.65.refs_2_, ...), custom_call_target="tpu_custom_call" | custom-call | flops 32399998976 | tf_op jit(solution)/shard_map/input_grad/pallas_call | solution.py:340
  1020.2 2.1 copy-done
  1022.3 49.8 %all-to-all-done.7.refs_0_ = bf16[4,48,96,128]{3,2,1,0:T(8,128)(2,1)} async-done(((bf16[4,48,96,128]{3,2,1,0:T(8,128)(2,1)}), bf16[4,48,96,128]{3,2,1,0:T(8,128)(2,1)}, u32[]{:S(2)}, u32[]{:S(2)}) %all-to-all-start.7) | async-done | bytes 4718624 | tf_op jit(solution)/shard_map/all_to_all | solution.py:392
  1072.1 4.9 all-to-all-start.6
  1077.1 0.2 copy.43
  1077.3 0.2 copy.44
  1077.5 0.2 copy.45
  1077.6 0.2 copy.46
  1078.0 1.4 collective-permute-done.4
  1079.5 1.5 collective-permute-start.5
  1081.0 5.6 collective-permute-done.5
  1086.6 1.5 collective-permute-start.6
  1088.1 4.8 collective-permute-done.6
  1093.0 2.0 collective-permute-start.7
  1095.0 6.9 place.4.refs_1_
  1101.9 55.6 %collective-permute-done.7 = f32[386,128]{1,0:T(8,128)S(1)} collective-permute-done((f32[386,128]{1,0:T(8,128)S(1)}, f32[386,128]{1,0:T(8,128)S(1)}, u32[]{:S(2)}, u32[]{:S(2)}) %collective-permute-start.7) | collective-permute-done | bytes 197664 | tf_op jit(solution)/shard_map/ppermute | solution.py:416
  1157.5 4.7 collective-permute-start.8
  1162.2 6.9 place.5
  1169.1 21.1 %collective-permute-done.8 = f32[386,128]{1,0:T(8,128)S(1)} collective-permute-done((f32[386,128]{1,0:T(8,128)S(1)}, f32[386,128]{1,0:T(8,128)S(1)}, u32[]{:S(2)}, u32[]{:S(2)}) %collective-permute-start.8) | collective-permute-done | bytes 197664 | tf_op jit(solution)/shard_map/ppermute | solution.py:416
  1190.3 6.9 place.6.refs_1_
  1197.4 0.6 multiply_add_fusion.2
  1198.0 1.1 multiply_add_fusion
  1199.1 6.9 place.7
  (102 shorter events, 1.5 us)
Async XLA Ops:
  16.3 6.5 copy-start.27
  16.3 6.7 copy-start.23
  16.3 111.4 %copy-start.14 = (f32[4,128]{1,0:T(4,128)S(1)}, f32[4,128]{1,0:T(4,128)}, u32[]{:S(2)}) copy-start(f32[4,128]{1,0:T(4,128)} %refs_6_.3) | copy-start | bytes 6148
  16.3 111.2 %all-to-all-start = ((bf16[4,48,96,128]{3,2,1,0:T(8,128)(2,1)}), bf16[4,48,96,128]{3,2,1,0:T(8,128)(2,1)}, u32[]{:S(2)}, u32[]{:S(2)}) async-start(bf16[4,48,96,128]{3,2,1,0:T(8,128)(2,1)} %get-tuple-element.86), calls=%async_computation | async-start | bytes 9437184 | tf_op jit(solution)/shard_map/all_to_all | solution.py:392
  22.8 363.2 %reduce-scatter.7.cloned.1.call-start = ((), (), s32[]{:S(2)}) async-start(), calls=%async_computation.12 | async-start | bytes 23592960
  23.1 130.6 %copy-start.21 = (bf16[6,128,128]{2,1,0:T(8,128)(2,1)}, bf16[6,128,128]{2,1,0:T(8,128)(2,1)S(1)}, u32[]{:S(2)}) copy-start(bf16[6,128,128]{2,1,0:T(8,128)(2,1)S(1)} %convert_element_type.6) | copy-start | bytes 589828
  127.6 26.0 %copy-start.6 = (f32[192,128]{1,0:T(8,128)}, f32[192,128]{1,0:T(8,128)S(1)}, u32[]{:S(2)}) copy-start(f32[192,128]{1,0:T(8,128)S(1)} %broadcast_in_dim.31.refs_3_.refs_8_) | copy-start | bytes 294916
  127.7 25.9 %copy-start.10 = (f32[96,128]{1,0:T(8,128)}, f32[96,128]{1,0:T(8,128)S(1)}, u32[]{:S(2)}) copy-start(f32[96,128]{1,0:T(8,128)S(1)} %broadcast_in_dim.33.refs_4_.refs_9_) | copy-start | bytes 147460
  153.6 2.1 copy-start.18
  155.8 10.1 copy-start.16
  155.8 7.9 collective-permute-start
  163.7 2.2 copy-start.31
  201.7 110.0 %all-to-all-start.1 = ((bf16[4,48,96,128]{3,2,1,0:T(8,128)(2,1)}), bf16[4,48,96,128]{3,2,1,0:T(8,128)(2,1)}, u32[]{:S(2)}, u32[]{:S(2)}) async-start(bf16[4,48,96,128]{3,2,1,0:T(8,128)(2,1)} %get-tuple-element.42), calls=%async_computation.1 | async-start | bytes 9437184 | tf_op jit(solution)/shard_map/all_to_all | solution.py:392
  206.7 349.6 %reduce-scatter.9.cloned.1.call-start = ((), (), s32[]{:S(2)}) async-start(), calls=%async_computation.13 | async-start | bytes 23592960
  311.8 26.0 %copy-start.8 = (f32[192,128]{1,0:T(8,128)}, f32[192,128]{1,0:T(8,128)S(1)}, u32[]{:S(2)}) copy-start(f32[192,128]{1,0:T(8,128)S(1)} %broadcast_in_dim.35.refs_3_.refs_8_) | copy-start | bytes 294916
  311.8 25.9 %copy-start.12 = (f32[96,128]{1,0:T(8,128)}, f32[96,128]{1,0:T(8,128)S(1)}, u32[]{:S(2)}) copy-start(f32[96,128]{1,0:T(8,128)S(1)} %broadcast_in_dim.37.refs_4_.refs_9_) | copy-start | bytes 147460
  337.8 2.2 copy-start.17
  340.0 10.0 copy-start.15
  340.0 7.9 collective-permute-start.1
  347.9 2.1 copy-start.30
  386.0 348.1 %all-gather.5.cloned.1.call-start = ((), (), s32[]{:S(2)}) async-start(), calls=%async_computation.10 | async-start | bytes 23592960 | tf_op jit(solution)/shard_map/all_gather | solution.py:458
  538.6 2.1 copy-start.3
  540.7 2.1 copy-start.5
  542.9 2.3 copy-start.20
  556.3 355.5 %all-gather.7.cloned.1.call-start = ((), (), s32[]{:S(2)}) async-start(), calls=%async_computation.11 | async-start | bytes 23592960 | tf_op jit(solution)/shard_map/all_gather | solution.py:458
  703.4 2.2 copy-start.1
  705.6 2.2 copy-start.2
  707.7 2.1 copy-start.19
  734.1 109.7 %all-to-all-start.5 = ((bf16[4,48,96,128]{3,2,1,0:T(8,128)(2,1)}), bf16[4,48,96,128]{3,2,1,0:T(8,128)(2,1)}, u32[]{:S(2)}, u32[]{:S(2)}) async-start(bf16[4,48,96,128]{3,2,1,0:T(8,128)(2,1)} %bitcast.69), calls=%async_computation.5 | async-start | bytes 9437184 | tf_op jit(solution)/shard_map/all_to_all | solution.py:392
  739.3 51.7 %copy-start.22 = (bf16[6,128,128]{2,1,0:T(8,128)(2,1)S(1)}, bf16[6,128,128]{2,1,0:T(8,128)(2,1)}, u32[]{:S(2)}) copy-start(bf16[6,128,128]{2,1,0:T(8,128)(2,1)} %copy-done.21) | copy-start | bytes 589828
  791.0 58.0 %collective-permute-start.2 = (bf16[192,96,128]{2,1,0:T(8,128)(2,1)}, bf16[192,96,128]{2,1,0:T(8,128)(2,1)}, u32[]{:S(2)}, u32[]{:S(2)}) collective-permute-start(bf16[192,96,128]{2,1,0:T(8,128)(2,1)} %get-tuple-element.59), channel_id=1, source_target_pairs={{0,4},{4,0},{8,12},{12,8},{16,20},{20,16},{24,28},{28,24},{1,5},{5... | collective-permute-start | bytes 14155784 | tf_op jit(solution)/shard_map/ppermute | solution.py:395
  843.8 5.2 copy-start.7
  843.8 5.2 copy-start.11
  843.8 117.8 %all-to-all-start.4 = ((bf16[4,48,96,128]{3,2,1,0:T(8,128)(2,1)}), bf16[4,48,96,128]{3,2,1,0:T(8,128)(2,1)}, u32[]{:S(2)}, u32[]{:S(2)}) async-start(bf16[4,48,96,128]{3,2,1,0:T(8,128)(2,1)} %bitcast.68), calls=%async_computation.4 | async-start | bytes 9437184 | tf_op jit(solution)/shard_map/all_to_all | solution.py:392
  899.3 2.2 copy-start.4
  961.6 8.3 collective-permute-start.3
  961.6 8.2 copy-start.9
  961.6 8.2 copy-start.13
  961.6 110.5 %all-to-all-start.7 = ((bf16[4,48,96,128]{3,2,1,0:T(8,128)(2,1)}), bf16[4,48,96,128]{3,2,1,0:T(8,128)(2,1)}, u32[]{:S(2)}, u32[]{:S(2)}) async-start(bf16[4,48,96,128]{3,2,1,0:T(8,128)(2,1)} %bitcast.70), calls=%async_computation.7 | async-start | bytes 9437184 | tf_op jit(solution)/shard_map/all_to_all | solution.py:392
  1020.2 2.1 copy-start
  1072.1 127.0 %all-to-all-start.6 = ((bf16[4,48,96,128]{3,2,1,0:T(8,128)(2,1)}), bf16[4,48,96,128]{3,2,1,0:T(8,128)(2,1)}, u32[]{:S(2)}, u32[]{:S(2)}) async-start(bf16[4,48,96,128]{3,2,1,0:T(8,128)(2,1)} %bitcast.67), calls=%async_computation.6 | async-start | bytes 9437184 | tf_op jit(solution)/shard_map/all_to_all | solution.py:392
  1077.9 1.5 collective-permute-start.4
  1079.5 7.1 collective-permute-start.5
  1086.6 6.4 collective-permute-start.6
  1093.0 64.5 %collective-permute-start.7 = (f32[386,128]{1,0:T(8,128)S(1)}, f32[386,128]{1,0:T(8,128)S(1)}, u32[]{:S(2)}, u32[]{:S(2)}) collective-permute-start(f32[386,128]{1,0:T(8,128)S(1)} %add.87), channel_id=1, source_target_pairs={{0,8},{4,12},{8,0},{12,4},{16,24},{20,28},{24,16},{28,20},{1,9},{5... | collective-permute-start | bytes 592904 | tf_op jit(solution)/shard_map/ppermute | solution.py:416
  1157.5 32.6 %collective-permute-start.8 = (f32[386,128]{1,0:T(8,128)S(1)}, f32[386,128]{1,0:T(8,128)S(1)}, u32[]{:S(2)}, u32[]{:S(2)}) collective-permute-start(f32[386,128]{1,0:T(8,128)S(1)} %add.88), channel_id=1, source_target_pairs={{0,16},{4,20},{8,24},{12,28},{16,0},{20,4},{24,8},{28,12},{1,17},{... | collective-permute-start | bytes 592904 | tf_op jit(solution)/shard_map/ppermute | solution.py:416
  1190.2 7.2 copy-start.28
  1190.2 7.2 copy-start.29
  1190.2 7.8 copy-start.24
  1190.2 7.8 copy-start.25
  1190.2 7.8 copy-start.26
  1190.2 7.0 collective-permute-start.9
Sparse Core Ops, SparseCore 0:
  201.8 170.0 reduce-scatter.6
  386.1 170.0 reduce-scatter.8
  558.1 175.9 all-gather.4
  735.8 175.9 all-gather.6

commit v3 on v2

--- a/solution.py
+++ b/solution.py
@@ -13,7 +13,7 @@
 LOW = jnp.bfloat16
 F32 = jnp.float32
 MIB = 1 << 20
-SHARE = 600_000_000
+SHARE = 6_000_000_000
 
 
 def sds(shape, dtype):
@@ -103,7 +103,7 @@
         in_specs=[flat] + [whole_spec(v) for v in (norms, proj, rowm, colm)],
         out_specs=[flat, flat],
         out_shape=[sds(z.shape, LOW)] * 2,
-        compiler_params=params(32),
+        compiler_params=params(58),
         cost_estimate=cost(27),
         name="edges",
     )(z, norms, proj, rowm, colm)
@@ -147,7 +147,7 @@
     return steps, inward, outward
 
 
-def product_call(scal, left, own, other, nparts):
+def product_call(scal, left, own, other, nparts, micros):
     ni, nk, chan = left.shape
     nrow = ni // nparts
     nj = 2 * ni
@@ -166,8 +166,8 @@
                             pltpu.VMEM((chan, ni, nj), LOW)],
         ),
         out_shape=sds((nparts, ni, 2 * nrow, chan), LOW),
-        compiler_params=params(56),
-        cost_estimate=cost(33),
+        compiler_params=params(58),
+        cost_estimate=cost(micros),
         name="product",
     )(scal, left, own, other)
 
@@ -221,7 +221,7 @@
         out_specs=[flat] * 3 + [whole_spec(v) for v in sums],
         out_shape=[sds(z.shape, LOW)] * 3 + sums,
         scratch_shapes=[low, low],
-        compiler_params=params(40),
+        compiler_params=params(58),
         cost_estimate=cost(40),
         name="middle",
     )(z, g, x, norms, gate_w, out_w)
@@ -263,7 +263,8 @@
         send[...] = to_minor(rt[:, pl.ds(pl.multiple_of((1 - core) * half + at, rows), rows), :])
 
 
-def edge_grad_call(scal, left, own, other, gx):
+def edge_grad_call(scal, left, own, other, gx, token):
+    tokens = [] if token is None else [token]
     nparts = gx.shape[0]
     ni, nk, chan = left.shape
     nrow = ni // nparts
@@ -273,29 +274,29 @@
     edge = pl.BlockSpec((rows, nk, chan), lambda s, sc: (inward(s), 0, 0))
     back = pl.BlockSpec((rows, nk, chan), lambda s, sc: (outward(s), 0, 0))
     return pl.pallas_call(
-        lambda *refs: edge_grad_kernel(nparts, 4, *refs),
+        lambda *refs: edge_grad_kernel(nparts, 4, *refs[:5], *refs[5 + len(tokens):]),
         grid_spec=pltpu.PrefetchScalarGridSpec(
             num_scalar_prefetch=1,
             grid=(2 * steps,),
             in_specs=[edge] * 3 + [pl.BlockSpec((nparts, rows, 2 * nrow, chan),
-                                                lambda s, sc: (0, inward(s), 0, 0))],
+                                                lambda s, sc: (0, inward(s), 0, 0))]
+            + [pl.BlockSpec(memory_space=pl.ANY)] * len(tokens),
             out_specs=[back] * 3,
             scratch_shapes=[pltpu.VMEM((chan, ni, nk), LOW), pltpu.VMEM((chan, nj, nk), LOW),
                             pltpu.VMEM((chan, ni, nj), LOW)],
         ),
         out_shape=[sds(left.shape, LOW)] * 3,
         compiler_params=params(58),
-        cost_estimate=cost(50),
+        cost_estimate=cost(5),
         name="edge_grad",
-    )(scal, left, own, other, gx)
+    )(scal, left, own, other, gx, *tokens)
 
 
 def input_kernel(sub, z_ref, g_ref, gleft, keep, got, gate_grad, norms, proj, rowm, colm,
                  out, wproj, nin, ulow, plow):
     rows, nk, chan = z_ref.shape
-    base = pl.program_id(0) * rows
-
-    @pl.when(pl.program_id(0) == 0)
+
+    @pl.when((pl.program_id(0) == 0) & (pl.program_id(1) == 0))
     def _():
         wproj[...] = jnp.zeros_like(wproj)
         nin[...] = jnp.zeros_like(nin)
@@ -309,7 +310,7 @@
         u = (hat * norms[0:1] + norms[1:2]).astype(LOW)
         ulow[flat] = u
         p = dot(u, proj[:, :4 * chan])
-        m = row_mask(rowm, colm, base + at, sub)
+        m = row_mask(rowm.at[0], colm, at, sub)
         gl = gleft[rng].astype(F32).reshape(-1, chan) * m
         gr = (keep[rng].astype(F32) + got[rng].astype(F32)).reshape(-1, chan) * m
         for n, grad in ((0, gl), (2, gr)):
@@ -331,43 +332,53 @@
     wproj[...] += dot(ulow[...], plow[...], 0, 0)
 
 
-def input_call(z, g, gleft, keep, got, gate_grad, norms, proj, rowm, colm):
+def input_call(z, g, gleft, keep, got, gate_grad, norms, proj, rowm, colm, nblocks, h, parts,
+               micros):
     ni, nk, chan = z.shape
-    rows = 16
-    flat = pl.BlockSpec((rows, nk, chan), lambda s: (s, 0, 0))
+    nrow = ni // nblocks
+    rows = nrow // 4
+    sub = 4 if rows % 4 == 0 else 2
+    per = 4 // parts
+    flat = pl.BlockSpec((rows, nk, chan), lambda s, r: (s * 4 + h * per + r, 0, 0))
+    mask = pl.BlockSpec((1, rows, chan), lambda s, r: (s * 4 + h * per + r, 0, 0))
+    rowm = rowm.reshape(-1, rows, chan)
     width = proj.shape[1]
     sums = [sds((chan, width), F32), sds((2, 8, chan), F32)]
+    whole = lambda v: pl.BlockSpec(v.shape, lambda s, r: (0,) * len(v.shape))
     return pl.pallas_call(
-        lambda *refs: input_kernel(4, *refs),
-        grid=(ni // rows,),
-        in_specs=[flat] * 6 + [whole_spec(v) for v in (norms, proj, rowm, colm)],
-        out_specs=[flat] + [whole_spec(v) for v in sums],
-        out_shape=[sds(z.shape, LOW)] + sums,
+        lambda *refs: input_kernel(sub, *refs),
+        grid=(nblocks, per),
+        in_specs=[flat] * 6 + [whole(norms), whole(proj), mask, whole(colm)],
+        out_specs=[pl.BlockSpec((rows, nk, chan), lambda s, r: (s * per + r, 0, 0))]
+        + [whole(v) for v in sums],
+        out_shape=[sds((ni // parts, nk, chan), LOW)] + sums,
         scratch_shapes=[pltpu.VMEM((rows * nk, chan), LOW), pltpu.VMEM((rows * nk, width), LOW)],
-        compiler_params=params(40),
-        cost_estimate=cost(54),
+        compiler_params=params(58),
+        cost_estimate=cost(micros),
         name="input_grad",
     )(z, g, gleft, keep, got, gate_grad, norms, proj, rowm, colm)
 
 
-def place_call(blocks, b, batches, whole=None):
-    count, nrow, nk, chan = blocks.shape
-    half = nrow // 2
+def place_call(blocks, b, batches, h, parts, whole=None):
+    count, size, nk, chan = blocks.shape
 
     def kernel(*refs):
-        refs[-1][...] = refs[0][...]
+        refs[-2][...] = refs[0][...]
+        refs[-1][...] = jnp.zeros_like(refs[-1])
 
     args = [blocks] + ([] if whole is None else [whole])
     return pl.pallas_call(
         kernel,
         grid=(count, 2),
-        in_specs=[pl.BlockSpec((1, half, nk, chan), lambda g, r: (g, r, 0, 0))]
+        in_specs=[pl.BlockSpec((1, size // 2, nk, chan), lambda g, r: (g, r, 0, 0))]
         + [pl.BlockSpec(memory_space=pl.ANY)] * (len(args) - 1),
-        out_specs=pl.BlockSpec((1, half, nk, chan), lambda g, r: (g * batches + b, r, 0, 0)),
-        out_shape=sds((count * batches, nrow, nk, chan), LOW),
+        out_specs=[pl.BlockSpec((1, size // 2, nk, chan),
+                                lambda g, r: (g * batches + b, h * 2 + r, 0, 0)),
+                   pl.BlockSpec((8, 128), lambda g, r: (0, 0))],
+        out_shape=[sds((count * batches, size * parts, nk, chan), LOW), sds((8, 128), F32)],
         input_output_aliases={} if whole is None else {1: 0},
-        compiler_params=params(16),
-        cost_estimate=cost(5),
+        compiler_params=params(58),
+        cost_estimate=cost(0.02),
         name="place",
     )(*args)
 
@@ -403,7 +414,7 @@
     def blocked(v):
         return v.reshape(zeds, nrow, ncol, chan)
 
-    def sum_all(term):
+    def sum_all(term, first, second):
         count = term.shape[0] // 2
         mine = lax.dynamic_slice_in_dim(term, core * count, count, 0)
         mine = mine + coreswap(lax.dynamic_slice_in_dim(term, (1 - core) * count, count, 0))
@@ -411,8 +422,11 @@
         while step < cols:
             mine = mine + lax.ppermute(mine, "col", [(q, q ^ step) for q in range(cols)])
             step *= 2
+        mine = after(mine, first)
         step = 2
         while step < rows:
+            if step * 2 >= rows:
+                mine = mine + second[:1]
             mine = mine + lax.ppermute(mine, "row", [(r, r ^ step) for r in range(rows)])
             step *= 2
         got = coreswap(mine)
@@ -435,52 +449,65 @@
         return left, right, coreswap(right)
 
     pairs, cots, kept, reduced = [], [], [], []
+    last = None
     for b in range(batches):
-        block = zswap(after(take(pair, b), pairs[b - 1]) if b else take(pair, b))
-        pairs.append(flat(block))
+        block = take(after(pair, block), b) if b else take(pair, b)
+        last = zswap(after(block, last) if b else block)
+        pairs.append(flat(last))
     for b in range(batches):
-        block = zswap(after(take(cotangent, b), cots[b - 1] if b else pairs[-1]))
-        cots.append(flat(block))
+        last = zswap(take(after(cotangent, last), b))
+        cots.append(flat(last))
     for b in range(batches):
         if b:
             pairs[b] = after(pairs[b], part)
-        kept.append(edges(b))
-        part = product_call(scal, *kept[b], cols)
-        if b:
-            part = after(part, reduced[b - 1])
-        reduced.append(flat(lax.psum_scatter(part, "col", scatter_dimension=0, tiled=True)))
+        left, right, other = edges(b)
+        kept.append((left, right, other))
+        part = product_call(scal, left, right, other, cols, 33 if b else 3)
+        ready = after(part, reduced[b - 1], cots[b - 1]) if b else part
+        reduced.append(flat(lax.psum_scatter(ready, "col", scatter_dimension=0, tiled=True)))
+    def collect(pieces, whole=None):
+        token = None
+        for blocks, b, h, share in pieces:
+            whole, token = place_call(blocks, b, batches, h, share, whole)
+        return whole, token
+
     gathered, news, gates, sums = [], [], [], []
     for b in range(batches):
         new, gx, gate_grad, wout, nout = middle_call(
             pairs[b], cots[b], reduced[b], norm_params, weight_low[4], weight_low[5])
-        news.append(zswap(blocked(new)))
-        gx = after(gx, gathered[b - 1] if b else reduced[-1])
-        gathered.append(lax.all_gather(gx, "col", axis=0))
+        last = zswap(after(blocked(new), last))
+        news.append((last, b, 0, 1))
+        ready = after(gx, (gathered[b - 1], last) if b else reduced[-1])
+        gathered.append(lax.all_gather(ready, "col", axis=0))
         gates.append(gate_grad)
         sums.append((wout, nout))
+    new_pair, placed = collect(news)
     backs, flats = [], []
     for b in range(batches):
-        gx = after(gathered[b], out) if b else gathered[b]
-        gleft, keep, send = edge_grad_call(scal, *kept[b], gx)
+        grad = after(gathered[b], out) if b else gathered[b]
+        gleft, keep, send = edge_grad_call(scal, *kept[b], grad, placed if b else None)
         got = coreswap(send)
-        out = input_call(pairs[b], cots[b], gleft, keep, got, gates[b], norm_params, project_low,
-                         *masks[b])
-        back, wproj, nin = out
-        backs.append(zswap(blocked(back)))
+        if b:
+            got = after(got, last)
+        share = 2 if b == batches - 1 else 1
+        for h in range(share):
+            out = input_call(pairs[b], cots[b], gleft, keep, got, gates[b], norm_params,
+                             project_low, *masks[b], zeds, h, share, 27 if b == batches - 1 else 5)
+            back, wproj, nin = out
+            last = zswap(after(back.reshape(zeds, nrow // share, ncol, chan), last))
+            backs.append((last, b, h, share))
+            grads = (wproj, nin) if h == 0 else (grads[0] + wproj, grads[1] + nin)
+        wproj, nin = grads
         wout, nout = sums[b]
         wproj = jnp.transpose(wproj.reshape(chan, 5, chan), (1, 0, 2)).reshape(5 * chan, chan)
         flats.append(jnp.concatenate(
             [wproj, wout, jnp.sum(nin, axis=1), jnp.sum(nout, axis=1)], axis=0))
 
-    def collect(pieces):
-        whole = None
-        for b in range(batches):
-            whole = place_call(pieces[b], b, batches, whole)
-        return whole
-
-    new_pair = collect(news)
-    pair_grad = collect(backs)
-    grads = sum_all(sum(flats))
+    pair_grad, first = collect(backs[:-2]) if batches > 1 else (None, None)
+    pair_grad, second = collect(backs[-2:-1], pair_grad)
+    pair_grad, _ = collect(backs[-1:], pair_grad)
+    term = sum(flats) if first is None else sum(flats) + first[:1]
+    grads = sum_all(term, backs[-2][0], second)
     grad_weights = grads[: 6 * chan].reshape(weights.shape)
     grad_norms = grads[6 * chan:]
     rate = 0.1 / (length * math.sqrt(crops))

time: 1210 us -> 1140 us (0.942)
  blocking collectives: 219 us -> 110 us
  Pallas kernels: 426 us -> 442 us
    all_to_all x2 -> x1, blocking collectives: 219 us -> 110 us  [zswap(): lax.all_to_all(blocks, 'row', 0, 0, tiled=True, axis_index_groups=same_core)]
    ppermute x2, waiting for transfers between devices: 76.7 us -> 21.1 us  [sum_all(): lax.ppermute(mine, 'row', [(r, r ^ step) for r in range(rows)])]
    unnamed x6, waiting for transfers between devices: 11.2 us -> 50.3 us
    all_gather x2, waiting for transfers between devices: 34.5 us -> 67.5 us  [shards(): gathered.append(lax.all_gather(ready, 'col', axis=0))]
    unnamed x68 -> x46, local copies, waits for them, and re-layouts: 25.9 us -> 1.55 us
    pallas_call x8 -> x10, Pallas kernels: 230 us -> 241 us  [the longest x3 108 us: input_call(): pl.pallas_call(lambda *refs: input_kernel(sub, *refs), grid=(nblocks, per...]
    all_to_all x6 -> x8, starting transfers between devices: 31.7 us -> 39.5 us  [zswap(): lax.all_to_all(blocks, 'row', 0, 0, tiled=True, axis_index_groups=same_core)]
    all_to_all x6 -> x8, waiting for transfers between devices: 312 us -> 308 us  [zswap(): lax.all_to_all(blocks, 'row', 0, 0, tiled=True, axis_index_groups=same_core)]
  transfers between devices with their start and end apart: 20 -> 22, of which waited for: 15 -> 18; matrix products, arithmetic and copies ran while one was open for 1% -> 3% of each run, Pallas kernels for 29% -> 36%
where the time goes in v3:
time: 1140 us; the launch traced here: 1130 us
  waiting for transfers between devices  473 us (41%)
  Pallas kernels  442 us (39%)
  blocking collectives  110 us (10%)
  starting transfers between devices  49.6 us (4%)
  local copies, waits for them, and re-layouts  35.9 us (3%)
  between operations  14.2 us (1%)
    all_to_all x8, waiting for transfers between devices, zswap(): lax.all_to_all(blocks, 'row', 0, 0, tiled=True, axis_index_groups=same_core)  308 us
    all_to_all x1, blocking collectives, zswap(): lax.all_to_all(blocks, 'row', 0, 0, tiled=True, axis_index_groups=same_core)  110 us
    pallas_call x3, Pallas kernels, input_call(): pl.pallas_call(lambda *refs: input_kernel(sub, *refs), grid=(nblocks, per...  108 us
    pallas_call x2, Pallas kernels, edge_grad_call(): pl.pallas_call(lambda *refs: edge_grad_kernel(nparts, 4, *refs[:5], *refs...  101 us
    pallas_call x2, Pallas kernels, middle_call(): pl.pallas_call(lambda *refs: middle_kernel(4, *refs), grid=(ni // rows,),...  75.1 us
    pallas_call x2, Pallas kernels, product_call(): pl.pallas_call(lambda *refs: product_kernel(nparts, 4, *refs), grid_spec=...  71.7 us
    all_gather x2, waiting for transfers between devices, shards(): gathered.append(lax.all_gather(ready, 'col', axis=0))  67.5 us
    pallas_call x2, Pallas kernels, edges_call(): pl.pallas_call(lambda *refs: edges_kernel(4, *refs), grid=(ni // rows,),...  54 us
  transfers between devices with their start and end apart: 22, of which 18 were waited for; matrix products, arithmetic and copies ran while one was open for 3% of the time, Pallas kernels for 36%

profile of v3, /device:TPU:0, one launch (start us, length us, event | category | flops | bytes accessed | tf_op | source)
XLA Modules:
  0.0 1133.1 jit_solution(2837146633887483678)
XLA Ops:
  7.2 5.5 slice_bitcast_fusion.3
  12.7 6.4 all-to-all-start
  20.4 1.2 fusion.2
  23.7 5.5 slice_bitcast_fusion.2
  29.3 94.6 %all-to-all-done = bf16[4,48,96,128]{3,2,1,0:T(8,128)(2,1)} async-done(((bf16[4,48,96,128]{3,2,1,0:T(8,128)(2,1)}), bf16[4,48,96,128]{3,2,1,0:T(8,128)(2,1)}, u32[]{:S(2)}, u32[]{:S(2)}) %all-to-all-start) | async-done | bytes 4718624 | tf_op jit(solution)/shard_map/all_to_all | solution.py:403
  123.9 4.9 all-to-all-start.1
  128.9 0.7 broadcast_in_dim.39.refs_3_
  130.3 27.0 %edges.2 = (bf16[192,96,128]{2,1,0:T(8,128)(2,1)}, bf16[192,96,128]{2,1,0:T(8,128)(2,1)}) custom-call(bf16[192,96,128]{2,1,0:T(8,128)(2,1)} %bitcast.6.refs_0_, f32[4,128]{1,0:T(4,128)} %refs_6_.5, bf16[128,512]{1,0:T(8,128)(2,1)} %pad_maximum_fusion.1.refs_2_, f32[192,128]{1,0:T(8,128)} %broadcast_in_dim.39.refs_3_, f32[96,128]{1,0:T(8,128)} %broadcast_in_dim.41.refs_4_.refs_9_), custom_call_target="tpu_custom_call" | custom-call | flops 161999994880 | tf_op jit(solution)/shard_map/edges/pallas_call | solution.py:100
  157.4 1.2 fusion.1
  158.7 6.9 collective-permute-done.refs_3_
  165.6 35.8 %product.2 = bf16[4,192,96,128]{3,2,1,0:T(8,128)(2,1)} custom-call(s32[1]{0:T(128)} %bitcast.5.refs_0_, bf16[192,96,128]{2,1,0:T(8,128)(2,1)} %get-tuple-element.63.refs_1_, bf16[192,96,128]{2,1,0:T(8,128)(2,1)} %get-tuple-element.64.refs_2_, bf16[192,96,128]{2,1,0:T(8,128)(2,1)} %collective-permute-done.refs_3_), custom_call_target="tpu_custom_call" | custom-call | flops 17999998976 | tf_op jit(solution)/shard_map/product/pallas_call | solution.py:157
  201.4 31.3 %all-to-all-done.1 = bf16[4,48,96,128]{3,2,1,0:T(8,128)(2,1)} async-done(((bf16[4,48,96,128]{3,2,1,0:T(8,128)(2,1)}), bf16[4,48,96,128]{3,2,1,0:T(8,128)(2,1)}, u32[]{:S(2)}, u32[]{:S(2)}) %all-to-all-start.1) | async-done | bytes 4718624 | tf_op jit(solution)/shard_map/all_to_all | solution.py:403
  232.7 0.7 broadcast_in_dim.43.refs_3_
  234.1 27.0 %edges.3 = (bf16[192,96,128]{2,1,0:T(8,128)(2,1)}, bf16[192,96,128]{2,1,0:T(8,128)(2,1)}) custom-call(bf16[192,96,128]{2,1,0:T(8,128)(2,1)} %bitcast.4.refs_0_, f32[4,128]{1,0:T(4,128)} %refs_6_.5, bf16[128,512]{1,0:T(8,128)(2,1)} %pad_maximum_fusion.1.refs_2_, f32[192,128]{1,0:T(8,128)} %broadcast_in_dim.43.refs_3_, f32[96,128]{1,0:T(8,128)} %broadcast_in_dim.45.refs_4_.refs_9_), custom_call_target="tpu_custom_call" | custom-call | flops 161999994880 | tf_op jit(solution)/shard_map/edges/pallas_call | solution.py:100
  261.2 5.5 slice_bitcast_fusion.1
  266.7 5.0 all-to-all-start.2
  271.7 35.9 %product.3 = bf16[4,192,96,128]{3,2,1,0:T(8,128)(2,1)} custom-call(s32[1]{0:T(128)} %bitcast.5.refs_0_, bf16[192,96,128]{2,1,0:T(8,128)(2,1)} %get-tuple-element.68.refs_1_, bf16[192,96,128]{2,1,0:T(8,128)(2,1)} %get-tuple-element.69.refs_2_, bf16[192,96,128]{2,1,0:T(8,128)(2,1)} %collective-permute-done.1.refs_3_), custom_call_target="tpu_custom_call" | custom-call | flops 198000001024 | tf_op jit(solution)/shard_map/product/pallas_call | solution.py:157
  307.6 69.8 %all-to-all-done.2 = bf16[4,48,96,128]{3,2,1,0:T(8,128)(2,1)} async-done(((bf16[4,48,96,128]{3,2,1,0:T(8,128)(2,1)}), bf16[4,48,96,128]{3,2,1,0:T(8,128)(2,1)}, u32[]{:S(2)}, u32[]{:S(2)}) %all-to-all-start.2) | async-done | bytes 4718624 | tf_op jit(solution)/shard_map/all_to_all | solution.py:403
  377.5 5.5 slice_bitcast_fusion
  383.0 5.0 all-to-all-start.3
  388.0 37.5 %middle.3 = (bf16[192,96,128]{2,1,0:T(8,128)(2,1)}, bf16[192,96,128]{2,1,0:T(8,128)(2,1)}, bf16[192,96,128]{2,1,0:T(8,128)(2,1)}, f32[128,128]{1,0:T(8,128)}, f32[2,8,128]{2,1,0:T(8,128)}) custom-call(bf16[192,96,128]{2,1,0:T(8,128)(2,1)} %bitcast.6.refs_0_, bf16[192,96,128]{2,1,0:T(8,128)(2,1)} %bitcast.20.refs_1_, bf16[192,96,128]{2,1,0:T(8,128)(2,1)} %bitcast.94, ...), custom_call_target="tpu_custom_call" | custom-call | flops 240000008192 | tf_op jit(solution)/shard_map/middle/pallas_call | solution.py:217
  425.5 67.4 %all-to-all-done.3 = bf16[4,48,96,128]{3,2,1,0:T(8,128)(2,1)} async-done(((bf16[4,48,96,128]{3,2,1,0:T(8,128)(2,1)}), bf16[4,48,96,128]{3,2,1,0:T(8,128)(2,1)}, u32[]{:S(2)}, u32[]{:S(2)}) %all-to-all-start.3) | async-done | bytes 4718624 | tf_op jit(solution)/shard_map/all_to_all | solution.py:403
  492.9 5.0 all-to-all-start.4
  497.9 50.2 %reduce-scatter.9.cloned.1.call-done = bf16[1,192,96,128]{3,2,1,0:T(8,128)(2,1)} async-done(((bf16[4,192,96,128]{3,2,1,0:T(8,128)(2,1)}), bf16[1,192,96,128]{3,2,1,0:T(8,128)(2,1)}) %reduce-scatter.9.cloned.1.call-update) | async-done | bytes 4718608
  548.2 37.5 %middle.2 = (bf16[192,96,128]{2,1,0:T(8,128)(2,1)}, bf16[192,96,128]{2,1,0:T(8,128)(2,1)}, bf16[192,96,128]{2,1,0:T(8,128)(2,1)}, f32[128,128]{1,0:T(8,128)}, f32[2,8,128]{2,1,0:T(8,128)}) custom-call(bf16[192,96,128]{2,1,0:T(8,128)(2,1)} %bitcast.4.refs_0_, bf16[192,96,128]{2,1,0:T(8,128)(2,1)} %bitcast.16.refs_1_, bf16[192,96,128]{2,1,0:T(8,128)(2,1)} %bitcast.95, ...), custom_call_target="tpu_custom_call" | custom-call | flops 240000008192 | tf_op jit(solution)/shard_map/middle/pallas_call | solution.py:217
  585.7 16.4 %all-to-all-done.4.refs_0_ = bf16[4,48,96,128]{3,2,1,0:T(8,128)(2,1)} async-done(((bf16[4,48,96,128]{3,2,1,0:T(8,128)(2,1)}), bf16[4,48,96,128]{3,2,1,0:T(8,128)(2,1)}, u32[]{:S(2)}, u32[]{:S(2)}) %all-to-all-start.4) | async-done | bytes 4718624 | tf_op jit(solution)/shard_map/all_to_all | solution.py:403
  602.2 110.1 %all_to_all.45.refs_0_ = bf16[4,48,96,128]{3,2,1,0:T(8,128)(2,1)} all-to-all(bf16[4,48,96,128]{3,2,1,0:T(8,128)(2,1)} %bitcast.82), channel_id=1, replica_groups={{0,8,16,24},{4,12,20,28},{1,9,17,25},{5,13,21,29},{2,10,18,26},{6,14,22..., dimensions={0} | all-to-all | bytes 9437184 | tf_op jit(solution)/shard_map/all_to_all | solution.py:403
  712.2 13.8 %all-gather.5.cloned.1.call-done = bf16[768,96,128]{2,1,0:T(8,128)(2,1)} async-done(((bf16[192,96,128]{2,1,0:T(8,128)(2,1)}), bf16[768,96,128]{2,1,0:T(8,128)(2,1)}) %all-gather.5.cloned.1.call-update) | async-done | bytes 18874384 | tf_op jit(solution)/shard_map/all_gather | solution.py:481
  726.1 51.5 %edge_grad.2 = (bf16[192,96,128]{2,1,0:T(8,128)(2,1)}, bf16[192,96,128]{2,1,0:T(8,128)(2,1)}, bf16[192,96,128]{2,1,0:T(8,128)(2,1)}) custom-call(s32[1]{0:T(128)} %bitcast.5.refs_0_, bf16[192,96,128]{2,1,0:T(8,128)(2,1)} %get-tuple-element.63.refs_1_, bf16[192,96,128]{2,1,0:T(8,128)(2,1)} %get-tuple-element.64.refs_2_, ...), custom_call_target="tpu_custom_call" | custom-call | flops 30000001024 | tf_op jit(solution)/shard_map/edge_grad/pallas_call | solution.py:276
  777.8 6.9 place.5
  784.8 6.9 place.6
  791.6 0.8 broadcast_in_dim.47.refs_8_
  792.4 52.7 %input_grad.3 = (bf16[192,96,128]{2,1,0:T(8,128)(2,1)}, f32[128,640]{1,0:T(8,128)}, f32[2,8,128]{2,1,0:T(8,128)}) custom-call(bf16[192,96,128]{2,1,0:T(8,128)(2,1)} %bitcast.6.refs_0_, bf16[192,96,128]{2,1,0:T(8,128)(2,1)} %bitcast.20.refs_1_, bf16[192,96,128]{2,1,0:T(8,128)(2,1)} %get-tuple-element.81.refs_2_, ...), custom_call_target="tpu_custom_call" | custom-call | flops 30000001024 | tf_op jit(solution)/shard_map/input_grad/pallas_call | solution.py:348
  845.1 5.0 all-to-all-start.6
  850.1 53.7 %all-gather.7.cloned.1.call-done = bf16[768,96,128]{2,1,0:T(8,128)(2,1)} async-done(((bf16[192,96,128]{2,1,0:T(8,128)(2,1)}), bf16[768,96,128]{2,1,0:T(8,128)(2,1)}) %all-gather.7.cloned.1.call-update) | async-done | bytes 18874384 | tf_op jit(solution)/shard_map/all_gather | solution.py:481
  903.8 49.4 %edge_grad.3 = (bf16[192,96,128]{2,1,0:T(8,128)(2,1)}, bf16[192,96,128]{2,1,0:T(8,128)(2,1)}, bf16[192,96,128]{2,1,0:T(8,128)(2,1)}) custom-call(s32[1]{0:T(128)} %bitcast.5.refs_0_, bf16[192,96,128]{2,1,0:T(8,128)(2,1)} %get-tuple-element.68.refs_1_, bf16[192,96,128]{2,1,0:T(8,128)(2,1)} %get-tuple-element.69.refs_2_, ...), custom_call_target="tpu_custom_call" | custom-call | flops 30000001024 | tf_op jit(solution)/shard_map/edge_grad/pallas_call | solution.py:276
  953.3 2.2 all-to-all-done.6.refs_0_
  955.5 6.0 collective-permute-done.3.refs_4_
  961.5 0.8 broadcast_in_dim.49.refs_8_
  962.2 27.6 %input_grad.5 = (bf16[96,96,128]{2,1,0:T(8,128)(2,1)}, f32[128,640]{1,0:T(8,128)}, f32[2,8,128]{2,1,0:T(8,128)}) custom-call(bf16[192,96,128]{2,1,0:T(8,128)(2,1)} %bitcast.4.refs_0_, bf16[192,96,128]{2,1,0:T(8,128)(2,1)} %bitcast.16.refs_1_, bf16[192,96,128]{2,1,0:T(8,128)(2,1)} %get-tuple-element.90.refs_2_, ...), custom_call_target="tpu_custom_call" | custom-call | flops 161999994880 | tf_op jit(solution)/shard_map/input_grad/pallas_call | solution.py:348
  989.8 4.6 all-to-all-start.7
  994.4 27.6 %input_grad.4 = (bf16[96,96,128]{2,1,0:T(8,128)(2,1)}, f32[128,640]{1,0:T(8,128)}, f32[2,8,128]{2,1,0:T(8,128)}) custom-call(bf16[192,96,128]{2,1,0:T(8,128)(2,1)} %bitcast.4.refs_0_, bf16[192,96,128]{2,1,0:T(8,128)(2,1)} %bitcast.16.refs_1_, bf16[192,96,128]{2,1,0:T(8,128)(2,1)} %get-tuple-element.90.refs_2_, ...), custom_call_target="tpu_custom_call" | custom-call | flops 161999994880 | tf_op jit(solution)/shard_map/input_grad/pallas_call | solution.py:348
  1022.1 26.7 %all-to-all-done.7.refs_0_ = bf16[4,24,96,128]{3,2,1,0:T(8,128)(2,1)} async-done(((bf16[4,24,96,128]{3,2,1,0:T(8,128)(2,1)}), bf16[4,24,96,128]{3,2,1,0:T(8,128)(2,1)}, u32[]{:S(2)}, u32[]{:S(2)}) %all-to-all-start.7) | async-done | bytes 2359328 | tf_op jit(solution)/shard_map/all_to_all | solution.py:403
  1048.7 3.6 all-to-all-start.8
  1054.0 6.9 place.7
  1060.8 1.2 slice_bitcast_fusion.11
  1062.0 1.1 add.108
  1063.5 0.7 add_reduce_fusion
  1064.2 0.7 fusion
  1065.1 1.4 collective-permute-done.4
  1066.5 1.5 collective-permute-start.5
  1068.1 5.6 collective-permute-done.5
  1073.7 1.5 collective-permute-start.6
  1075.2 4.7 collective-permute-done.6
  1080.0 2.0 collective-permute-start.7
  1082.0 5.9 place.8
  1088.5 5.8 collective-permute-done.7
  1094.4 4.7 collective-permute-start.8
  1099.1 15.3 %collective-permute-done.8 = f32[386,128]{1,0:T(8,128)S(1)} collective-permute-done((f32[386,128]{1,0:T(8,128)S(1)}, f32[386,128]{1,0:T(8,128)S(1)}, u32[]{:S(2)}, u32[]{:S(2)}) %collective-permute-start.8) | collective-permute-done | bytes 197664 | tf_op jit(solution)/shard_map/ppermute | solution.py:430
  1114.5 1.4 collective-permute-done.9
  1116.0 1.3 multiply_add_fusion.2
  1117.3 2.1 multiply_add_fusion
  1119.4 1.4 copy-done
  1120.8 5.8 place.9
  (95 shorter events, 8.4 us)
Async XLA Ops:
  12.7 6.5 copy-start.9
  12.7 9.0 copy-start.3
  12.7 111.2 %all-to-all-start = ((bf16[4,48,96,128]{3,2,1,0:T(8,128)(2,1)}), bf16[4,48,96,128]{3,2,1,0:T(8,128)(2,1)}, u32[]{:S(2)}, u32[]{:S(2)}) async-start(bf16[4,48,96,128]{3,2,1,0:T(8,128)(2,1)} %slice_bitcast_fusion.3), calls=%async_computation | async-start | bytes 9437184 | tf_op jit(solution)/shard_map/all_to_all | solution.py:403
  21.7 7.5 copy-start.1
  123.9 108.8 %all-to-all-start.1 = ((bf16[4,48,96,128]{3,2,1,0:T(8,128)(2,1)}), bf16[4,48,96,128]{3,2,1,0:T(8,128)(2,1)}, u32[]{:S(2)}, u32[]{:S(2)}) async-start(bf16[4,48,96,128]{3,2,1,0:T(8,128)(2,1)} %slice_bitcast_fusion.2), calls=%async_computation.1 | async-start | bytes 9437184 | tf_op jit(solution)/shard_map/all_to_all | solution.py:403
  128.8 248.6 %reduce-scatter.7.cloned.1.call-start = ((), (), s32[]{:S(2)}) async-start(), calls=%async_computation.13 | async-start | bytes 23592960
  130.3 27.0 %copy-start.16 = (f32[384]{0:T(512)S(1)}, f32[384]{0:T(512)}, u32[]{:S(2)}) copy-start(f32[384]{0:T(512)} %get-tuple-element.114) | copy-start | bytes 4612
  157.3 8.3 collective-permute-start
  201.4 32.1 %copy-start.18 = (f32[96]{0:T(128)S(1)}, f32[96]{0:T(128)}, u32[]{:S(2)}) copy-start(f32[96]{0:T(128)} %get-tuple-element.134) | copy-start | bytes 1156
  261.1 10.5 collective-permute-start.1
  266.7 110.8 %all-to-all-start.2 = ((bf16[4,48,96,128]{3,2,1,0:T(8,128)(2,1)}), bf16[4,48,96,128]{3,2,1,0:T(8,128)(2,1)}, u32[]{:S(2)}, u32[]{:S(2)}) async-start(bf16[4,48,96,128]{3,2,1,0:T(8,128)(2,1)} %slice_bitcast_fusion.1), calls=%async_computation.2 | async-start | bytes 9437184 | tf_op jit(solution)/shard_map/all_to_all | solution.py:403
  271.6 276.5 %reduce-scatter.9.cloned.1.call-start = ((), (), s32[]{:S(2)}) async-start(), calls=%async_computation.14 | async-start | bytes 23592960
  383.0 109.9 %all-to-all-start.3 = ((bf16[4,48,96,128]{3,2,1,0:T(8,128)(2,1)}), bf16[4,48,96,128]{3,2,1,0:T(8,128)(2,1)}, u32[]{:S(2)}, u32[]{:S(2)}) async-start(bf16[4,48,96,128]{3,2,1,0:T(8,128)(2,1)} %slice_bitcast_fusion), calls=%async_computation.3 | async-start | bytes 9437184 | tf_op jit(solution)/shard_map/all_to_all | solution.py:403
  492.9 109.3 %all-to-all-start.4 = ((bf16[4,48,96,128]{3,2,1,0:T(8,128)(2,1)}), bf16[4,48,96,128]{3,2,1,0:T(8,128)(2,1)}, u32[]{:S(2)}, u32[]{:S(2)}) async-start(bf16[4,48,96,128]{3,2,1,0:T(8,128)(2,1)} %bitcast.80), calls=%async_computation.4 | async-start | bytes 9437184 | tf_op jit(solution)/shard_map/all_to_all | solution.py:403
  497.9 228.2 %all-gather.5.cloned.1.call-start = ((), (), s32[]{:S(2)}) async-start(), calls=%async_computation.11 | async-start | bytes 23592960 | tf_op jit(solution)/shard_map/all_gather | solution.py:481
  548.1 355.6 %all-gather.7.cloned.1.call-start = ((), (), s32[]{:S(2)}) async-start(), calls=%async_computation.12 | async-start | bytes 23592960 | tf_op jit(solution)/shard_map/all_gather | solution.py:481
  726.1 51.5 %copy-start.10 = (f32[4,1,48]{2,1,0:T(1,128)S(1)}, f32[4,1,48]{2,1,0:T(1,128)}, u32[]{:S(2)}) copy-start(f32[4,1,48]{2,1,0:T(1,128)} %get-tuple-element.125) | copy-start | bytes 2308
  726.1 51.6 %copy-start.2 = (bf16[6,128,128]{2,1,0:T(8,128)(2,1)S(1)}, bf16[6,128,128]{2,1,0:T(8,128)(2,1)}, u32[]{:S(2)}) copy-start(bf16[6,128,128]{2,1,0:T(8,128)(2,1)} %copy-done.1) | copy-start | bytes 589828
  777.6 14.0 %collective-permute-start.2 = (bf16[192,96,128]{2,1,0:T(8,128)(2,1)}, bf16[192,96,128]{2,1,0:T(8,128)(2,1)}, u32[]{:S(2)}, u32[]{:S(2)}) collective-permute-start(bf16[192,96,128]{2,1,0:T(8,128)(2,1)} %get-tuple-element.83), channel_id=1, source_target_pairs={{0,4},{4,0},{8,12},{12,8},{16,20},{20,16},{24,28},{28,24},{1,5},{5... | collective-permute-start | bytes 14155784 | tf_op jit(solution)/shard_map/ppermute | solution.py:406
  777.8 13.8 %copy-start.17 = (bf16[128,640]{1,0:T(8,128)(2,1)}, bf16[128,640]{1,0:T(8,128)(2,1)S(1)}, u32[]{:S(2)}) copy-start(bf16[128,640]{1,0:T(8,128)(2,1)S(1)} %constant_dynamic-update-slice_fusion.refs_7_) | copy-start | bytes 491524
  845.1 110.4 %all-to-all-start.6 = ((bf16[4,48,96,128]{3,2,1,0:T(8,128)(2,1)}), bf16[4,48,96,128]{3,2,1,0:T(8,128)(2,1)}, u32[]{:S(2)}, u32[]{:S(2)}) async-start(bf16[4,48,96,128]{3,2,1,0:T(8,128)(2,1)} %bitcast.81), calls=%async_computation.6 | async-start | bytes 9437184 | tf_op jit(solution)/shard_map/all_to_all | solution.py:403
  903.8 49.4 %copy-start.11 = (f32[4,1,48]{2,1,0:T(1,128)S(1)}, f32[4,1,48]{2,1,0:T(1,128)}, u32[]{:S(2)}) copy-start(f32[4,1,48]{2,1,0:T(1,128)} %get-tuple-element.123) | copy-start | bytes 2308
  953.2 8.3 collective-permute-start.3
  989.8 59.0 %all-to-all-start.7 = ((bf16[4,24,96,128]{3,2,1,0:T(8,128)(2,1)}), bf16[4,24,96,128]{3,2,1,0:T(8,128)(2,1)}, u32[]{:S(2)}, u32[]{:S(2)}) async-start(bf16[4,24,96,128]{3,2,1,0:T(8,128)(2,1)} %bitcast.84), calls=%async_computation.7 | async-start | bytes 4718592 | tf_op jit(solution)/shard_map/all_to_all | solution.py:403
  1022.0 30.4 %copy-start.12 = (f32[2,8,128]{2,1,0:T(8,128)S(1)}, f32[2,8,128]{2,1,0:T(8,128)}, u32[]{:S(2)}) copy-start(f32[2,8,128]{2,1,0:T(8,128)} %get-tuple-element.104) | copy-start | bytes 24580
  1022.0 30.4 %copy-start.13 = (f32[2,8,128]{2,1,0:T(8,128)S(1)}, f32[2,8,128]{2,1,0:T(8,128)}, u32[]{:S(2)}) copy-start(f32[2,8,128]{2,1,0:T(8,128)} %get-tuple-element.110) | copy-start | bytes 24580
  1022.0 31.0 %copy-start.6 = (f32[128,640]{1,0:T(8,128)S(1)}, f32[128,640]{1,0:T(8,128)}, u32[]{:S(2)}) copy-start(f32[128,640]{1,0:T(8,128)} %get-tuple-element.86) | copy-start | bytes 983044
  1022.1 31.2 %copy-start.14 = (f32[2,8,128]{2,1,0:T(8,128)S(1)}, f32[2,8,128]{2,1,0:T(8,128)}, u32[]{:S(2)}) copy-start(f32[2,8,128]{2,1,0:T(8,128)} %get-tuple-element.87) | copy-start | bytes 24580
  1048.7 70.7 %all-to-all-start.8 = ((bf16[4,24,96,128]{3,2,1,0:T(8,128)(2,1)}), bf16[4,24,96,128]{3,2,1,0:T(8,128)(2,1)S(1)}, u32[]{:S(2)}, u32[]{:S(2)}) async-start(bf16[4,24,96,128]{3,2,1,0:T(8,128)(2,1)} %bitcast.83), calls=%async_computation.8 | async-start | bytes 4718592 | tf_op jit(solution)/shard_map/all_to_all | solution.py:403
  1052.4 11.1 copy-start.15
  1052.4 11.8 %copy-start.7 = (f32[128,128]{1,0:T(8,128)S(1)}, f32[128,128]{1,0:T(8,128)}, u32[]{:S(2)}) copy-start(f32[128,128]{1,0:T(8,128)} %get-tuple-element.103) | copy-start | bytes 196612
  1052.4 11.8 %copy-start.8 = (f32[128,128]{1,0:T(8,128)S(1)}, f32[128,128]{1,0:T(8,128)}, u32[]{:S(2)}) copy-start(f32[128,128]{1,0:T(8,128)} %get-tuple-element.107) | copy-start | bytes 196612
  1065.0 1.5 collective-permute-start.4
  1066.5 7.1 collective-permute-start.5
  1073.7 6.3 collective-permute-start.6
  1080.0 14.4 %collective-permute-start.7 = (f32[386,128]{1,0:T(8,128)S(1)}, f32[386,128]{1,0:T(8,128)S(1)}, u32[]{:S(2)}, u32[]{:S(2)}) collective-permute-start(f32[386,128]{1,0:T(8,128)S(1)} %add.118), channel_id=1, source_target_pairs={{0,8},{4,12},{8,0},{12,4},{16,24},{20,28},{24,16},{28,20},{1,9},{5... | collective-permute-start | bytes 592904 | tf_op jit(solution)/shard_map/ppermute | solution.py:430
  1082.0 34.0 %copy-start.19 = (f32[4,128]{1,0:T(4,128)S(1)}, f32[4,128]{1,0:T(4,128)}, u32[]{:S(2)}) copy-start(f32[4,128]{1,0:T(4,128)} %refs_6_.5) | copy-start | bytes 6148
  1082.0 34.0 %copy-start.20 = (f32[4,128]{1,0:T(4,128)S(1)}, f32[4,128]{1,0:T(4,128)}, u32[]{:S(2)}) copy-start(f32[4,128]{1,0:T(4,128)} %param.17) | copy-start | bytes 6148
  1082.0 35.3 %copy-start.4 = (f32[6,128,128]{2,1,0:T(8,128)S(1)}, f32[6,128,128]{2,1,0:T(8,128)}, u32[]{:S(2)}) copy-start(f32[6,128,128]{2,1,0:T(8,128)} %param.12) | copy-start | bytes 1179652
  1082.0 35.3 %copy-start.5 = (f32[6,128,128]{2,1,0:T(8,128)S(1)}, f32[6,128,128]{2,1,0:T(8,128)}, u32[]{:S(2)}) copy-start(f32[6,128,128]{2,1,0:T(8,128)} %param.16) | copy-start | bytes 1179652
  1094.4 20.0 %collective-permute-start.8 = (f32[386,128]{1,0:T(8,128)S(1)}, f32[386,128]{1,0:T(8,128)S(1)}, u32[]{:S(2)}, u32[]{:S(2)}) collective-permute-start(f32[386,128]{1,0:T(8,128)S(1)} %add_add_fusion), channel_id=1, source_target_pairs={{0,16},{4,20},{8,24},{12,28},{16,0},{20,4},{24,8},{28,12},{1,17},{... | collective-permute-start | bytes 592904 | tf_op jit(solution)/shard_map/ppermute | solution.py:430
  1114.4 1.5 collective-permute-start.9
  1119.4 1.4 copy-start
Sparse Core Ops, SparseCore 0:
  201.5 172.2 reduce-scatter.6
  377.6 170.5 reduce-scatter.8
  550.0 176.0 all-gather.4
  727.8 175.9 all-gather.6

commit v4 on v3

--- a/solution.py
+++ b/solution.py
@@ -90,15 +90,15 @@
         right[pl.ds(at, sub)] = rv.astype(LOW).reshape(sub, nk, chan)
         return 0
 
-    lax.fori_loop(0, rows // sub, step, 0)
+    lax.fori_loop(0, rows // sub, step, 0, unroll=rows // sub)
 
 
 def edges_call(z, norms, proj, rowm, colm):
     ni, nk, chan = z.shape
-    rows = 16
+    rows = 32
     flat = pl.BlockSpec((rows, nk, chan), lambda s: (s, 0, 0))
     return pl.pallas_call(
-        lambda *refs: edges_kernel(4, *refs),
+        lambda *refs: edges_kernel(8, *refs),
         grid=(ni // rows,),
         in_specs=[flat] + [whole_spec(v) for v in (norms, proj, rowm, colm)],
         out_specs=[flat, flat],
@@ -155,7 +155,7 @@
     steps, inward, outward = phases(ni, rows)
     edge = pl.BlockSpec((rows, nk, chan), lambda s, sc: (inward(s), 0, 0))
     return pl.pallas_call(
-        lambda *refs: product_kernel(nparts, 4, *refs),
+        lambda *refs: product_kernel(nparts, 16, *refs),
         grid_spec=pltpu.PrefetchScalarGridSpec(
             num_scalar_prefetch=1,
             grid=(2 * steps,),
@@ -204,7 +204,7 @@
         gx[rng] = norm_back(gy * norms[2:3], hat, inverse).astype(LOW).reshape(sub, nk, chan)
         return 0
 
-    lax.fori_loop(0, rows // sub, step, 0)
+    lax.fori_loop(0, rows // sub, step, 0, unroll=rows // sub)
     wout[...] += dot(ylow[...], glow[...], 0, 0)
 
 
@@ -215,7 +215,7 @@
     low = pltpu.VMEM((rows * nk, chan), LOW)
     sums = [sds((chan, chan), F32), sds((2, 8, chan), F32)]
     return pl.pallas_call(
-        lambda *refs: middle_kernel(4, *refs),
+        lambda *refs: middle_kernel(8, *refs),
         grid=(ni // rows,),
         in_specs=[flat] * 3 + [whole_spec(v) for v in (norms, gate_w, out_w)],
         out_specs=[flat] * 3 + [whole_spec(v) for v in sums],
@@ -274,7 +274,7 @@
     edge = pl.BlockSpec((rows, nk, chan), lambda s, sc: (inward(s), 0, 0))
     back = pl.BlockSpec((rows, nk, chan), lambda s, sc: (outward(s), 0, 0))
     return pl.pallas_call(
-        lambda *refs: edge_grad_kernel(nparts, 4, *refs[:5], *refs[5 + len(tokens):]),
+        lambda *refs: edge_grad_kernel(nparts, 16, *refs[:5], *refs[5 + len(tokens):]),
         grid_spec=pltpu.PrefetchScalarGridSpec(
             num_scalar_prefetch=1,
             grid=(2 * steps,),
@@ -328,16 +328,17 @@
         out[rng] = grad_z.astype(LOW).reshape(sub, nk, chan)
         return 0
 
-    lax.fori_loop(0, rows // sub, step, 0)
+    lax.fori_loop(0, rows // sub, step, 0, unroll=rows // sub)
     wproj[...] += dot(ulow[...], plow[...], 0, 0)
 
 
 def input_call(z, g, gleft, keep, got, gate_grad, norms, proj, rowm, colm, nblocks, h, parts,
-               micros):
+               micros, token):
+    tokens = [] if token is None else [token]
     ni, nk, chan = z.shape
     nrow = ni // nblocks
     rows = nrow // 4
-    sub = 4 if rows % 4 == 0 else 2
+    sub = rows // 2
     per = 4 // parts
     flat = pl.BlockSpec((rows, nk, chan), lambda s, r: (s * 4 + h * per + r, 0, 0))
     mask = pl.BlockSpec((1, rows, chan), lambda s, r: (s * 4 + h * per + r, 0, 0))
@@ -346,9 +347,10 @@
     sums = [sds((chan, width), F32), sds((2, 8, chan), F32)]
     whole = lambda v: pl.BlockSpec(v.shape, lambda s, r: (0,) * len(v.shape))
     return pl.pallas_call(
-        lambda *refs: input_kernel(sub, *refs),
+        lambda *refs: input_kernel(sub, *refs[:10], *refs[10 + len(tokens):]),
         grid=(nblocks, per),
-        in_specs=[flat] * 6 + [whole(norms), whole(proj), mask, whole(colm)],
+        in_specs=[flat] * 6 + [whole(norms), whole(proj), mask, whole(colm)]
+        + [pl.BlockSpec(memory_space=pl.ANY)] * len(tokens),
         out_specs=[pl.BlockSpec((rows, nk, chan), lambda s, r: (s * per + r, 0, 0))]
         + [whole(v) for v in sums],
         out_shape=[sds((ni // parts, nk, chan), LOW)] + sums,
@@ -356,7 +358,7 @@
         compiler_params=params(58),
         cost_estimate=cost(micros),
         name="input_grad",
-    )(z, g, gleft, keep, got, gate_grad, norms, proj, rowm, colm)
+    )(z, g, gleft, keep, got, gate_grad, norms, proj, rowm, colm, *tokens)
 
 
 def place_call(blocks, b, batches, h, parts, whole=None):
@@ -373,7 +375,7 @@
         in_specs=[pl.BlockSpec((1, size // 2, nk, chan), lambda g, r: (g, r, 0, 0))]
         + [pl.BlockSpec(memory_space=pl.ANY)] * (len(args) - 1),
         out_specs=[pl.BlockSpec((1, size // 2, nk, chan),
-                                lambda g, r: (g * batches + b, h * 2 + r, 0, 0)),
+                                lambda g, r: (b * count + g, h * 2 + r, 0, 0)),
                    pl.BlockSpec((8, 128), lambda g, r: (0, 0))],
         out_shape=[sds((count * batches, size * parts, nk, chan), LOW), sds((8, 128), F32)],
         input_output_aliases={} if whole is None else {1: 0},
@@ -414,7 +416,7 @@
     def blocked(v):
         return v.reshape(zeds, nrow, ncol, chan)
 
-    def sum_all(term, first, second):
+    def sum_col(term):
         count = term.shape[0] // 2
         mine = lax.dynamic_slice_in_dim(term, core * count, count, 0)
         mine = mine + coreswap(lax.dynamic_slice_in_dim(term, (1 - core) * count, count, 0))
@@ -422,19 +424,22 @@
         while step < cols:
             mine = mine + lax.ppermute(mine, "col", [(q, q ^ step) for q in range(cols)])
             step *= 2
-        mine = after(mine, first)
+        return mine
+
+    def sum_zed(mine, second, third):
         step = 2
         while step < rows:
             if step * 2 >= rows:
                 mine = mine + second[:1]
             mine = mine + lax.ppermute(mine, "row", [(r, r ^ step) for r in range(rows)])
             step *= 2
+        mine = mine + third[:1]
         got = coreswap(mine)
         return jnp.concatenate([jnp.where(core == 0, mine, got), jnp.where(core == 0, got, mine)])
 
     masks = []
     for b in range(batches):
-        crop_mask = lax.dynamic_index_in_dim(mask_float, zed * batches + b, 0, keepdims=False)
+        crop_mask = lax.dynamic_index_in_dim(mask_float, b * zeds + zed, 0, keepdims=False)
         by_block = crop_mask.reshape(zeds, 2, nrow)
         rowm = lax.dynamic_index_in_dim(by_block, core, 1, keepdims=False).reshape(-1)
         colm = lax.dynamic_slice_in_dim(crop_mask, col * ncol, ncol, 0)
@@ -442,7 +447,7 @@
                       jnp.broadcast_to(colm[:, None], (ncol, chan))))
 
     def take(whole, b):
-        return whole.reshape(zeds, batches, nrow, ncol, chan)[:, b]
+        return whole[b * zeds:(b + 1) * zeds]
 
     def edges(b):
         left, right = edges_call(pairs[b], norm_params, project_low[:, :4 * chan], *masks[b])
@@ -454,8 +459,10 @@
         block = take(after(pair, block), b) if b else take(pair, b)
         last = zswap(after(block, last) if b else block)
         pairs.append(flat(last))
+    sliced = [take(cotangent, b) for b in range(batches)]
+    pairs[0] = after(pairs[0], sliced)
     for b in range(batches):
-        last = zswap(take(after(cotangent, last), b))
+        last = zswap(after(sliced[b], last))
         cots.append(flat(last))
     for b in range(batches):
         if b:
@@ -482,32 +489,37 @@
         gates.append(gate_grad)
         sums.append((wout, nout))
     new_pair, placed = collect(news)
-    backs, flats = [], []
+    term, pair_grad, placed_back = 0.0, None, None
     for b in range(batches):
+        final = b == batches - 1
+        wout, nout = sums[b]
         grad = after(gathered[b], out) if b else gathered[b]
         gleft, keep, send = edge_grad_call(scal, *kept[b], grad, placed if b else None)
         got = coreswap(send)
         if b:
             got = after(got, last)
-        share = 2 if b == batches - 1 else 1
+        share = 2 if final else 1
+        backs = []
         for h in range(share):
             out = input_call(pairs[b], cots[b], gleft, keep, got, gates[b], norm_params,
-                             project_low, *masks[b], zeds, h, share, 27 if b == batches - 1 else 5)
+                             project_low, *masks[b], zeds, h, share, 27 if final else 5,
+                             placed_back)
             back, wproj, nin = out
-            last = zswap(after(back.reshape(zeds, nrow // share, ncol, chan), last))
+            wproj = jnp.transpose(wproj.reshape(chan, 5, chan), (1, 0, 2)).reshape(5 * chan, chan)
+            part = [wproj, jnp.zeros_like(wout) if h else wout, jnp.sum(nin, axis=1),
+                    jnp.zeros((2, chan), F32) if h else jnp.sum(nout, axis=1)]
+            term = term + jnp.concatenate(part, axis=0)
+            back = back.reshape(zeds, nrow // share, ncol, chan)
+            if final and h == share - 1:
+                term = sum_col(term)
+                back = after(back, term)
+            last = zswap(after(back, last))
             backs.append((last, b, h, share))
-            grads = (wproj, nin) if h == 0 else (grads[0] + wproj, grads[1] + nin)
-        wproj, nin = grads
-        wout, nout = sums[b]
-        wproj = jnp.transpose(wproj.reshape(chan, 5, chan), (1, 0, 2)).reshape(5 * chan, chan)
-        flats.append(jnp.concatenate(
-            [wproj, wout, jnp.sum(nin, axis=1), jnp.sum(nout, axis=1)], axis=0))
-
-    pair_grad, first = collect(backs[:-2]) if batches > 1 else (None, None)
-    pair_grad, second = collect(backs[-2:-1], pair_grad)
-    pair_grad, _ = collect(backs[-1:], pair_grad)
-    term = sum(flats) if first is None else sum(flats) + first[:1]
-    grads = sum_all(term, backs[-2][0], second)
+        if not final:
+            pair_grad, placed_back = collect(backs, pair_grad)
+    pair_grad, second = collect(backs[:1], pair_grad)
+    pair_grad, third = collect(backs[1:], pair_grad)
+    grads = sum_zed(after(term, backs[0][0]), second, third)
     grad_weights = grads[: 6 * chan].reshape(weights.shape)
     grad_norms = grads[6 * chan:]
     rate = 0.1 / (length * math.sqrt(crops))

time: 1140 us -> 1110 us (0.974)
  Pallas kernels: 442 us -> 329 us
  waiting for transfers between devices: 473 us -> 557 us
    pallas_call x11, Pallas kernels: 410 us -> 297 us  [the longest x2 94 us: edge_grad_call(): pl.pallas_call(lambda *refs: edge_grad_kernel(nparts, 16, *refs[:5], *ref...]
    all_gather x2, waiting for transfers between devices: 67.5 us -> 102 us  [shards(): gathered.append(lax.all_gather(ready, 'col', axis=0))]
    all_to_all x8, waiting for transfers between devices: 308 us -> 339 us  [zswap(): lax.all_to_all(blocks, 'row', 0, 0, tiled=True, axis_index_groups=same_core)]
    squeeze x4 -> x0, local copies, waits for them, and re-layouts: 22 us -> none  [take(): return whole.reshape(zeds, batches, nrow, ncol, chan)[:, b]]
    slice x0 -> x3, local copies, waits for them, and re-layouts: none -> 20.3 us  [take(): return whole[b * zeds:(b + 1) * zeds]]
    ppermute x4, waiting for transfers between devices: 31.4 us -> 45 us  [the longest x2 34.1 us: sum_zed(): lax.ppermute(mine, 'row', [(r, r ^ step) for r in range(rows)])]
  transfers between devices with their start and end apart: 22 -> 22, of which waited for: 18 -> 17; matrix products, arithmetic and copies ran while one was open for 3% -> 3% of each run, Pallas kernels for 36% -> 28%
where the time goes in v4:
time: 1110 us; the launch traced here: 1100 us
  waiting for transfers between devices  557 us (50%)
  Pallas kernels  329 us (30%)
  blocking collectives  110 us (10%)
  starting transfers between devices  50.4 us (5%)
  local copies, waits for them, and re-layouts  36.9 us (3%)
  between operations  14.2 us (1%)
    all_to_all x8, waiting for transfers between devices, zswap(): lax.all_to_all(blocks, 'row', 0, 0, tiled=True, axis_index_groups=same_core)  339 us
    all_to_all x1, blocking collectives, zswap(): lax.all_to_all(blocks, 'row', 0, 0, tiled=True, axis_index_groups=same_core)  110 us
    all_gather x2, waiting for transfers between devices, shards(): gathered.append(lax.all_gather(ready, 'col', axis=0))  102 us
    pallas_call x2, Pallas kernels, edge_grad_call(): pl.pallas_call(lambda *refs: edge_grad_kernel(nparts, 16, *refs[:5], *ref...  94 us
    pallas_call x2, Pallas kernels, product_call(): pl.pallas_call(lambda *refs: product_kernel(nparts, 16, *refs), grid_spec...  64.3 us
    pallas_call x3, Pallas kernels, input_call(): pl.pallas_call(lambda *refs: input_kernel(sub, *refs[:10], *refs[10 + len...  62.7 us
    unnamed x6, waiting for transfers between devices  58.3 us
    pallas_call x2, Pallas kernels, middle_call(): pl.pallas_call(lambda *refs: middle_kernel(8, *refs), grid=(ni // rows,),...  44.2 us
  transfers between devices with their start and end apart: 22, of which 17 were waited for; matrix products, arithmetic and copies ran while one was open for 3% of the time, Pallas kernels for 28%

profile of v4, /device:TPU:0, one launch (start us, length us, event | category | flops | bytes accessed | tf_op | source)
XLA Modules:
  0.0 1104.6 jit_solution(11501018040774273201)
XLA Ops:
  7.2 5.5 slice.48
  12.7 6.4 all-to-all-start
  20.4 1.2 fusion.2
  21.7 5.6 slice.49
  29.3 9.2 fusion.3
  38.5 85.4 %all-to-all-done = bf16[4,48,96,128]{3,2,1,0:T(8,128)(2,1)} async-done(((bf16[4,48,96,128]{3,2,1,0:T(8,128)(2,1)}), bf16[4,48,96,128]{3,2,1,0:T(8,128)(2,1)}, u32[]{:S(2)}, u32[]{:S(2)}) %all-to-all-start) | async-done | bytes 4718624 | tf_op jit(solution)/shard_map/all_to_all | solution.py:405
  123.9 4.9 all-to-all-start.1
  128.9 0.7 broadcast_in_dim.45.refs_3_
  129.6 0.7 broadcast_in_dim.47.refs_4_.refs_9_
  130.3 15.9 %edges.2 = (bf16[192,96,128]{2,1,0:T(8,128)(2,1)}, bf16[192,96,128]{2,1,0:T(8,128)(2,1)}) custom-call(bf16[192,96,128]{2,1,0:T(8,128)(2,1)} %bitcast.2.refs_0_, f32[4,128]{1,0:T(4,128)} %refs_6_.5, bf16[128,512]{1,0:T(8,128)(2,1)} %pad_maximum_fusion.1.refs_2_, f32[192,128]{1,0:T(8,128)} %broadcast_in_dim.45.refs_3_, f32[96,128]{1,0:T(8,128)} %broadcast_in_dim.47.refs_4_.refs_9_), custom_call_target="tpu_custom_call" | custom-call | flops 161999994880 | tf_op jit(solution)/shard_map/edges/pallas_call | solution.py:100
  146.3 1.2 fusion.1
  147.6 6.8 collective-permute-done.refs_3_
  154.4 32.0 %product.2 = bf16[4,192,96,128]{3,2,1,0:T(8,128)(2,1)} custom-call(s32[1]{0:T(128)} %bitcast.1.refs_0_, bf16[192,96,128]{2,1,0:T(8,128)(2,1)} %get-tuple-element.67.refs_1_, bf16[192,96,128]{2,1,0:T(8,128)(2,1)} %get-tuple-element.68.refs_2_, bf16[192,96,128]{2,1,0:T(8,128)(2,1)} %collective-permute-done.refs_3_), custom_call_target="tpu_custom_call" | custom-call | flops 17999998976 | tf_op jit(solution)/shard_map/product/pallas_call | solution.py:157
  186.4 46.3 %all-to-all-done.1 = bf16[4,48,96,128]{3,2,1,0:T(8,128)(2,1)} async-done(((bf16[4,48,96,128]{3,2,1,0:T(8,128)(2,1)}), bf16[4,48,96,128]{3,2,1,0:T(8,128)(2,1)}, u32[]{:S(2)}, u32[]{:S(2)}) %all-to-all-start.1) | async-done | bytes 4718624 | tf_op jit(solution)/shard_map/all_to_all | solution.py:405
  232.7 0.7 broadcast_in_dim.49.refs_3_
  234.1 15.9 %edges.3 = (bf16[192,96,128]{2,1,0:T(8,128)(2,1)}, bf16[192,96,128]{2,1,0:T(8,128)(2,1)}) custom-call(bf16[192,96,128]{2,1,0:T(8,128)(2,1)} %bitcast.refs_0_, f32[4,128]{1,0:T(4,128)} %refs_6_.5, bf16[128,512]{1,0:T(8,128)(2,1)} %pad_maximum_fusion.1.refs_2_, f32[192,128]{1,0:T(8,128)} %broadcast_in_dim.49.refs_3_, f32[96,128]{1,0:T(8,128)} %broadcast_in_dim.51.refs_4_.refs_9_), custom_call_target="tpu_custom_call" | custom-call | flops 161999994880 | tf_op jit(solution)/shard_map/edges/pallas_call | solution.py:100
  250.0 5.0 all-to-all-start.2
  255.3 3.0 collective-permute-done.1.refs_3_
  258.2 32.3 %product.3 = bf16[4,192,96,128]{3,2,1,0:T(8,128)(2,1)} custom-call(s32[1]{0:T(128)} %bitcast.1.refs_0_, bf16[192,96,128]{2,1,0:T(8,128)(2,1)} %get-tuple-element.72.refs_1_, bf16[192,96,128]{2,1,0:T(8,128)(2,1)} %get-tuple-element.73.refs_2_, bf16[192,96,128]{2,1,0:T(8,128)(2,1)} %collective-permute-done.1.refs_3_), custom_call_target="tpu_custom_call" | custom-call | flops 198000001024 | tf_op jit(solution)/shard_map/product/pallas_call | solution.py:157
  290.5 69.8 %all-to-all-done.2 = bf16[4,48,96,128]{3,2,1,0:T(8,128)(2,1)} async-done(((bf16[4,48,96,128]{3,2,1,0:T(8,128)(2,1)}), bf16[4,48,96,128]{3,2,1,0:T(8,128)(2,1)}, u32[]{:S(2)}, u32[]{:S(2)}) %all-to-all-start.2) | async-done | bytes 4718624 | tf_op jit(solution)/shard_map/all_to_all | solution.py:405
  360.4 5.0 all-to-all-start.3
  365.4 22.0 %middle.3 = (bf16[192,96,128]{2,1,0:T(8,128)(2,1)}, bf16[192,96,128]{2,1,0:T(8,128)(2,1)}, bf16[192,96,128]{2,1,0:T(8,128)(2,1)}, f32[128,128]{1,0:T(8,128)}, f32[2,8,128]{2,1,0:T(8,128)}) custom-call(bf16[192,96,128]{2,1,0:T(8,128)(2,1)} %bitcast.2.refs_0_, bf16[192,96,128]{2,1,0:T(8,128)(2,1)} %bitcast.12.refs_1_, bf16[192,96,128]{2,1,0:T(8,128)(2,1)} %bitcast.76, ...), custom_call_target="tpu_custom_call" | custom-call | flops 240000008192 | tf_op jit(solution)/shard_map/middle/pallas_call | solution.py:217
  387.4 82.5 %all-to-all-done.3 = bf16[4,48,96,128]{3,2,1,0:T(8,128)(2,1)} async-done(((bf16[4,48,96,128]{3,2,1,0:T(8,128)(2,1)}), bf16[4,48,96,128]{3,2,1,0:T(8,128)(2,1)}, u32[]{:S(2)}, u32[]{:S(2)}) %all-to-all-start.3) | async-done | bytes 4718624 | tf_op jit(solution)/shard_map/all_to_all | solution.py:405
  469.9 5.0 all-to-all-start.4
  474.9 58.3 %reduce-scatter.9.cloned.1.call-done = bf16[1,192,96,128]{3,2,1,0:T(8,128)(2,1)} async-done(((bf16[4,192,96,128]{3,2,1,0:T(8,128)(2,1)}), bf16[1,192,96,128]{3,2,1,0:T(8,128)(2,1)}) %reduce-scatter.9.cloned.1.call-update) | async-done | bytes 4718608
  533.3 22.3 %middle.2 = (bf16[192,96,128]{2,1,0:T(8,128)(2,1)}, bf16[192,96,128]{2,1,0:T(8,128)(2,1)}, bf16[192,96,128]{2,1,0:T(8,128)(2,1)}, f32[128,128]{1,0:T(8,128)}, f32[2,8,128]{2,1,0:T(8,128)}) custom-call(bf16[192,96,128]{2,1,0:T(8,128)(2,1)} %bitcast.refs_0_, bf16[192,96,128]{2,1,0:T(8,128)(2,1)} %bitcast.8.refs_1_, bf16[192,96,128]{2,1,0:T(8,128)(2,1)} %bitcast.77, ...), custom_call_target="tpu_custom_call" | custom-call | flops 240000008192 | tf_op jit(solution)/shard_map/middle/pallas_call | solution.py:217
  555.5 23.3 %all-to-all-done.4.refs_0_ = bf16[4,48,96,128]{3,2,1,0:T(8,128)(2,1)} async-done(((bf16[4,48,96,128]{3,2,1,0:T(8,128)(2,1)}), bf16[4,48,96,128]{3,2,1,0:T(8,128)(2,1)}, u32[]{:S(2)}, u32[]{:S(2)}) %all-to-all-start.4) | async-done | bytes 4718624 | tf_op jit(solution)/shard_map/all_to_all | solution.py:405
  578.8 110.1 %all_to_all.45.refs_0_ = bf16[4,48,96,128]{3,2,1,0:T(8,128)(2,1)} all-to-all(bf16[4,48,96,128]{3,2,1,0:T(8,128)(2,1)} %bitcast.62), channel_id=1, replica_groups={{0,8,16,24},{4,12,20,28},{1,9,17,25},{5,13,21,29},{2,10,18,26},{6,14,22..., dimensions={0} | all-to-all | bytes 9437184 | tf_op jit(solution)/shard_map/all_to_all | solution.py:405
  688.9 22.2 %all-gather.5.cloned.1.call-done = bf16[768,96,128]{2,1,0:T(8,128)(2,1)} async-done(((bf16[192,96,128]{2,1,0:T(8,128)(2,1)}), bf16[768,96,128]{2,1,0:T(8,128)(2,1)}) %all-gather.5.cloned.1.call-update) | async-done | bytes 18874384 | tf_op jit(solution)/shard_map/all_gather | solution.py:488
  711.1 48.1 %edge_grad.2 = (bf16[192,96,128]{2,1,0:T(8,128)(2,1)}, bf16[192,96,128]{2,1,0:T(8,128)(2,1)}, bf16[192,96,128]{2,1,0:T(8,128)(2,1)}) custom-call(s32[1]{0:T(128)} %bitcast.1.refs_0_, bf16[192,96,128]{2,1,0:T(8,128)(2,1)} %get-tuple-element.67.refs_1_, bf16[192,96,128]{2,1,0:T(8,128)(2,1)} %get-tuple-element.68.refs_2_, ...), custom_call_target="tpu_custom_call" | custom-call | flops 30000001024 | tf_op jit(solution)/shard_map/edge_grad/pallas_call | solution.py:276
  759.3 6.9 place.5
  766.3 6.9 place.6
  773.1 0.8 broadcast_in_dim.53.refs_8_
  773.9 30.3 %input_grad.3 = (bf16[192,96,128]{2,1,0:T(8,128)(2,1)}, f32[128,640]{1,0:T(8,128)}, f32[2,8,128]{2,1,0:T(8,128)}) custom-call(bf16[192,96,128]{2,1,0:T(8,128)(2,1)} %bitcast.2.refs_0_, bf16[192,96,128]{2,1,0:T(8,128)(2,1)} %bitcast.12.refs_1_, bf16[192,96,128]{2,1,0:T(8,128)(2,1)} %get-tuple-element.85.refs_2_, ...), custom_call_target="tpu_custom_call" | custom-call | flops 30000001024 | tf_op jit(solution)/shard_map/input_grad/pallas_call | solution.py:349
  804.2 5.0 all-to-all-start.6
  809.2 79.6 %all-gather.7.cloned.1.call-done = bf16[768,96,128]{2,1,0:T(8,128)(2,1)} async-done(((bf16[192,96,128]{2,1,0:T(8,128)(2,1)}), bf16[768,96,128]{2,1,0:T(8,128)(2,1)}) %all-gather.7.cloned.1.call-update) | async-done | bytes 18874384 | tf_op jit(solution)/shard_map/all_gather | solution.py:488
  888.8 45.9 %edge_grad.3 = (bf16[192,96,128]{2,1,0:T(8,128)(2,1)}, bf16[192,96,128]{2,1,0:T(8,128)(2,1)}, bf16[192,96,128]{2,1,0:T(8,128)(2,1)}) custom-call(s32[1]{0:T(128)} %bitcast.1.refs_0_, bf16[192,96,128]{2,1,0:T(8,128)(2,1)} %get-tuple-element.72.refs_1_, bf16[192,96,128]{2,1,0:T(8,128)(2,1)} %get-tuple-element.73.refs_2_, ...), custom_call_target="tpu_custom_call" | custom-call | flops 30000001024 | tf_op jit(solution)/shard_map/edge_grad/pallas_call | solution.py:276
  937.9 0.9 copy.33
  938.8 6.8 place.7
  945.7 0.8 broadcast_in_dim.55.refs_8_
  946.4 16.1 %input_grad.5 = (bf16[96,96,128]{2,1,0:T(8,128)(2,1)}, f32[128,640]{1,0:T(8,128)}, f32[2,8,128]{2,1,0:T(8,128)}) custom-call(bf16[192,96,128]{2,1,0:T(8,128)(2,1)} %bitcast.refs_0_, bf16[192,96,128]{2,1,0:T(8,128)(2,1)} %bitcast.8.refs_1_, bf16[192,96,128]{2,1,0:T(8,128)(2,1)} %get-tuple-element.94.refs_2_, bf16[192,96,128]{2,1,0:T(8,128)(2,1)} %get-tuple-element.95.refs_3_, ...), custom_call_target="tpu_custom_call" | custom-call | flops 161999994880 | tf_op jit(solution)/shard_map/input_grad/pallas_call | solution.py:349
  962.6 4.7 all-to-all-start.7
  967.5 16.3 %input_grad.4 = (bf16[96,96,128]{2,1,0:T(8,128)(2,1)}, f32[128,640]{1,0:T(8,128)}, f32[2,8,128]{2,1,0:T(8,128)}) custom-call(bf16[192,96,128]{2,1,0:T(8,128)(2,1)} %bitcast.refs_0_, bf16[192,96,128]{2,1,0:T(8,128)(2,1)} %bitcast.8.refs_1_, bf16[192,96,128]{2,1,0:T(8,128)(2,1)} %get-tuple-element.94.refs_2_, bf16[192,96,128]{2,1,0:T(8,128)(2,1)} %get-tuple-element.95.refs_3_, ...), custom_call_target="tpu_custom_call" | custom-call | flops 161999994880 | tf_op jit(solution)/shard_map/input_grad/pallas_call | solution.py:349
  984.1 1.1 copy.36
  985.4 0.7 reduce_sum.49
  987.1 1.1 collective-permute-done.4
  988.2 1.5 collective-permute-start.5
  989.7 5.8 collective-permute-done.5
  995.5 1.5 collective-permute-start.6
  997.1 5.1 collective-permute-done.6
  1002.2 20.0 %all-to-all-done.7.refs_0_ = bf16[4,24,96,128]{3,2,1,0:T(8,128)(2,1)} async-done(((bf16[4,24,96,128]{3,2,1,0:T(8,128)(2,1)}), bf16[4,24,96,128]{3,2,1,0:T(8,128)(2,1)}, u32[]{:S(2)}, u32[]{:S(2)}) %all-to-all-start.7) | async-done | bytes 2359328 | tf_op jit(solution)/shard_map/all_to_all | solution.py:405
  1022.2 3.6 all-to-all-start.8
  1025.8 2.0 collective-permute-start.7
  1027.8 5.8 place.8
  1033.6 0.7 slice_bitcast_fusion.7
  1034.2 34.1 %collective-permute-done.7 = f32[386,128]{1,0:T(8,128)S(1)} collective-permute-done((f32[386,128]{1,0:T(8,128)S(1)}, f32[386,128]{1,0:T(8,128)S(1)}, u32[]{:S(2)}, u32[]{:S(2)}) %collective-permute-start.7) | collective-permute-done | bytes 197664 | tf_op jit(solution)/shard_map/ppermute | solution.py:434
  1068.4 4.7 collective-permute-start.8
  1073.1 12.0 %all-to-all-done.8.refs_0_ = bf16[4,24,96,128]{3,2,1,0:T(8,128)(2,1)S(1)} async-done(((bf16[4,24,96,128]{3,2,1,0:T(8,128)(2,1)}), bf16[4,24,96,128]{3,2,1,0:T(8,128)(2,1)S(1)}, u32[]{:S(2)}, u32[]{:S(2)}) %all-to-all-start.8) | async-done | bytes 2359328 | tf_op jit(solution)/shard_map/all_to_all | solution.py:405
  1085.1 1.4 copy-done
  1086.5 5.9 place.9
  1092.4 0.7 slice_bitcast_fusion.6
  1093.2 1.4 collective-permute-done.9
  1094.7 1.3 multiply_add_fusion.2
  1096.0 2.1 multiply_add_fusion
  (114 shorter events, 9.7 us)
Async XLA Ops:
  12.7 6.5 copy-start.13
  12.7 9.0 copy-start.3
  12.7 111.2 %all-to-all-start = ((bf16[4,48,96,128]{3,2,1,0:T(8,128)(2,1)}), bf16[4,48,96,128]{3,2,1,0:T(8,128)(2,1)}, u32[]{:S(2)}, u32[]{:S(2)}) async-start(bf16[4,48,96,128]{3,2,1,0:T(8,128)(2,1)} %slice.48), calls=%async_computation | async-start | bytes 9437184 | tf_op jit(solution)/shard_map/all_to_all | solution.py:405
  21.7 6.2 copy-start.1
  123.9 108.8 %all-to-all-start.1 = ((bf16[4,48,96,128]{3,2,1,0:T(8,128)(2,1)}), bf16[4,48,96,128]{3,2,1,0:T(8,128)(2,1)}, u32[]{:S(2)}, u32[]{:S(2)}) async-start(bf16[4,48,96,128]{3,2,1,0:T(8,128)(2,1)} %slice.49), calls=%async_computation.1 | async-start | bytes 9437184 | tf_op jit(solution)/shard_map/all_to_all | solution.py:405
  128.8 231.5 %reduce-scatter.7.cloned.1.call-start = ((), (), s32[]{:S(2)}) async-start(), calls=%async_computation.13 | async-start | bytes 23592960
  130.3 15.9 %copy-start.20 = (f32[384]{0:T(512)S(1)}, f32[384]{0:T(512)}, u32[]{:S(2)}) copy-start(f32[384]{0:T(512)} %get-tuple-element.120) | copy-start | bytes 4612
  146.2 8.3 collective-permute-start
  186.4 47.0 %copy-start.25 = (f32[96]{0:T(128)S(1)}, f32[96]{0:T(128)}, u32[]{:S(2)}) copy-start(f32[96]{0:T(128)} %get-tuple-element.142) | copy-start | bytes 1156
  250.0 8.3 collective-permute-start.1
  250.0 110.4 %all-to-all-start.2 = ((bf16[4,48,96,128]{3,2,1,0:T(8,128)(2,1)}), bf16[4,48,96,128]{3,2,1,0:T(8,128)(2,1)}, u32[]{:S(2)}, u32[]{:S(2)}) async-start(bf16[4,48,96,128]{3,2,1,0:T(8,128)(2,1)} %get-tuple-element.70), calls=%async_computation.2 | async-start | bytes 9437184 | tf_op jit(solution)/shard_map/all_to_all | solution.py:405
  255.0 278.2 %reduce-scatter.9.cloned.1.call-start = ((), (), s32[]{:S(2)}) async-start(), calls=%async_computation.14 | async-start | bytes 23592960
  360.4 109.5 %all-to-all-start.3 = ((bf16[4,48,96,128]{3,2,1,0:T(8,128)(2,1)}), bf16[4,48,96,128]{3,2,1,0:T(8,128)(2,1)}, u32[]{:S(2)}, u32[]{:S(2)}) async-start(bf16[4,48,96,128]{3,2,1,0:T(8,128)(2,1)} %get-tuple-element.71), calls=%async_computation.3 | async-start | bytes 9437184 | tf_op jit(solution)/shard_map/all_to_all | solution.py:405
  469.9 108.9 %all-to-all-start.4 = ((bf16[4,48,96,128]{3,2,1,0:T(8,128)(2,1)}), bf16[4,48,96,128]{3,2,1,0:T(8,128)(2,1)}, u32[]{:S(2)}, u32[]{:S(2)}) async-start(bf16[4,48,96,128]{3,2,1,0:T(8,128)(2,1)} %bitcast.61), calls=%async_computation.4 | async-start | bytes 9437184 | tf_op jit(solution)/shard_map/all_to_all | solution.py:405
  474.9 236.2 %all-gather.5.cloned.1.call-start = ((), (), s32[]{:S(2)}) async-start(), calls=%async_computation.11 | async-start | bytes 23592960 | tf_op jit(solution)/shard_map/all_gather | solution.py:488
  533.2 355.5 %all-gather.7.cloned.1.call-start = ((), (), s32[]{:S(2)}) async-start(), calls=%async_computation.12 | async-start | bytes 23592960 | tf_op jit(solution)/shard_map/all_gather | solution.py:488
  711.1 48.1 %copy-start.14 = (f32[4,1,48]{2,1,0:T(1,128)S(1)}, f32[4,1,48]{2,1,0:T(1,128)}, u32[]{:S(2)}) copy-start(f32[4,1,48]{2,1,0:T(1,128)} %get-tuple-element.131) | copy-start | bytes 2308
  711.1 48.2 %copy-start.2 = (bf16[6,128,128]{2,1,0:T(8,128)(2,1)S(1)}, bf16[6,128,128]{2,1,0:T(8,128)(2,1)}, u32[]{:S(2)}) copy-start(bf16[6,128,128]{2,1,0:T(8,128)(2,1)} %copy-done.1) | copy-start | bytes 589828
  759.2 14.0 %collective-permute-start.2 = (bf16[192,96,128]{2,1,0:T(8,128)(2,1)}, bf16[192,96,128]{2,1,0:T(8,128)(2,1)}, u32[]{:S(2)}, u32[]{:S(2)}) collective-permute-start(bf16[192,96,128]{2,1,0:T(8,128)(2,1)} %get-tuple-element.87), channel_id=1, source_target_pairs={{0,4},{4,0},{8,12},{12,8},{16,20},{20,16},{24,28},{28,24},{1,5},{5... | collective-permute-start | bytes 14155784 | tf_op jit(solution)/shard_map/ppermute | solution.py:408
  759.3 13.8 %copy-start.21 = (bf16[128,640]{1,0:T(8,128)(2,1)}, bf16[128,640]{1,0:T(8,128)(2,1)S(1)}, u32[]{:S(2)}) copy-start(bf16[128,640]{1,0:T(8,128)(2,1)S(1)} %constant_dynamic-update-slice_fusion.refs_7_) | copy-start | bytes 491524
  804.2 134.6 %all-to-all-start.6 = ((bf16[4,48,96,128]{3,2,1,0:T(8,128)(2,1)}), bf16[4,48,96,128]{3,2,1,0:T(8,128)(2,1)}, u32[]{:S(2)}, u32[]{:S(2)}) async-start(bf16[4,48,96,128]{3,2,1,0:T(8,128)(2,1)} %bitcast.60), calls=%async_computation.6 | async-start | bytes 9437184 | tf_op jit(solution)/shard_map/all_to_all | solution.py:405
  888.8 45.9 %copy-start.15 = (f32[4,1,48]{2,1,0:T(1,128)S(1)}, f32[4,1,48]{2,1,0:T(1,128)}, u32[]{:S(2)}) copy-start(f32[4,1,48]{2,1,0:T(1,128)} %get-tuple-element.129) | copy-start | bytes 2308
  888.8 47.3 %copy-start.16 = (f32[2,8,128]{2,1,0:T(8,128)S(1)}, f32[2,8,128]{2,1,0:T(8,128)}, u32[]{:S(2)}) copy-start(f32[2,8,128]{2,1,0:T(8,128)} %get-tuple-element.103) | copy-start | bytes 24580
  888.8 47.9 %copy-start.17 = (f32[2,8,128]{2,1,0:T(8,128)S(1)}, f32[2,8,128]{2,1,0:T(8,128)}, u32[]{:S(2)}) copy-start(f32[2,8,128]{2,1,0:T(8,128)} %get-tuple-element.107) | copy-start | bytes 24580
  888.8 48.4 %copy-start.7 = (f32[128,640]{1,0:T(8,128)S(1)}, f32[128,640]{1,0:T(8,128)}, u32[]{:S(2)}) copy-start(f32[128,640]{1,0:T(8,128)} %get-tuple-element.90) | copy-start | bytes 983044
  888.8 48.6 %copy-start.18 = (f32[2,8,128]{2,1,0:T(8,128)S(1)}, f32[2,8,128]{2,1,0:T(8,128)}, u32[]{:S(2)}) copy-start(f32[2,8,128]{2,1,0:T(8,128)} %get-tuple-element.91) | copy-start | bytes 24580
  934.7 11.0 collective-permute-start.3
  962.6 59.6 %all-to-all-start.7 = ((bf16[4,24,96,128]{3,2,1,0:T(8,128)(2,1)}), bf16[4,24,96,128]{3,2,1,0:T(8,128)(2,1)}, u32[]{:S(2)}, u32[]{:S(2)}) async-start(bf16[4,24,96,128]{3,2,1,0:T(8,128)(2,1)} %bitcast.64), calls=%async_computation.7 | async-start | bytes 4718592 | tf_op jit(solution)/shard_map/all_to_all | solution.py:405
  967.3 16.4 %copy-start.8 = (f32[128,640]{1,0:T(8,128)S(1)}, f32[128,640]{1,0:T(8,128)}, u32[]{:S(2)}) copy-start(f32[128,640]{1,0:T(8,128)} %get-tuple-element.104) | copy-start | bytes 983044
  967.4 16.7 %copy-start.19 = (f32[2,8,128]{2,1,0:T(8,128)S(1)}, f32[2,8,128]{2,1,0:T(8,128)}, u32[]{:S(2)}) copy-start(f32[2,8,128]{2,1,0:T(8,128)} %get-tuple-element.106) | copy-start | bytes 24580
  967.4 18.8 %copy-start.5 = (f32[5,128,128]{2,1,0:T(8,128)S(1)}, f32[5,128,128]{2,1,0:T(8,128)}, u32[]{:S(2)}) copy-start(f32[5,128,128]{2,1,0:T(8,128)} %copy.33) | copy-start | bytes 983044
  967.4 18.7 %copy-start.9 = (f32[128,128]{1,0:T(8,128)S(1)}, f32[128,128]{1,0:T(8,128)}, u32[]{:S(2)}) copy-start(f32[128,128]{1,0:T(8,128)} %get-tuple-element.102) | copy-start | bytes 196612
  967.4 18.7 %copy-start.10 = (f32[128,128]{1,0:T(8,128)S(1)}, f32[128,128]{1,0:T(8,128)}, u32[]{:S(2)}) copy-start(f32[128,128]{1,0:T(8,128)} %get-tuple-element.105) | copy-start | bytes 196612
  967.4 18.7 %copy-start.11 = (f32[772]{0:T(1024)S(1)}, f32[772]{0:T(1024)}, u32[]{:S(2)}) copy-start(f32[772]{0:T(1024)} %pad.3.clone) | copy-start | bytes 9268
  967.4 18.7 %copy-start.12 = (f32[772]{0:T(1024)S(1)}, f32[772]{0:T(1024)}, u32[]{:S(2)}) copy-start(f32[772]{0:T(1024)} %pad.5.clone) | copy-start | bytes 9268
  967.4 18.7 %copy-start.22 = (f32[2,128]{1,0:T(2,128)S(1)}, f32[2,128]{1,0:T(2,128)}, u32[]{:S(2)}) copy-start(f32[2,128]{1,0:T(2,128)} %reduce_sum.46) | copy-start | bytes 3076
  967.4 18.7 %copy-start.23 = (f32[2,128]{1,0:T(2,128)S(1)}, f32[2,128]{1,0:T(2,128)}, u32[]{:S(2)}) copy-start(f32[2,128]{1,0:T(2,128)} %reduce_sum.48) | copy-start | bytes 3076
  967.4 18.7 %copy-start.24 = (f32[2,128]{1,0:T(2,128)S(1)}, f32[2,128]{1,0:T(2,128)}, u32[]{:S(2)}) copy-start(f32[2,128]{1,0:T(2,128)} %reduce_sum.45) | copy-start | bytes 3076
  986.5 1.7 collective-permute-start.4
  988.2 7.3 collective-permute-start.5
  995.5 6.6 collective-permute-start.6
  1022.2 62.9 %all-to-all-start.8 = ((bf16[4,24,96,128]{3,2,1,0:T(8,128)(2,1)}), bf16[4,24,96,128]{3,2,1,0:T(8,128)(2,1)S(1)}, u32[]{:S(2)}, u32[]{:S(2)}) async-start(bf16[4,24,96,128]{3,2,1,0:T(8,128)(2,1)} %bitcast.63), calls=%async_computation.8 | async-start | bytes 4718592 | tf_op jit(solution)/shard_map/all_to_all | solution.py:405
  1025.8 42.6 %collective-permute-start.7 = (f32[386,128]{1,0:T(8,128)S(1)}, f32[386,128]{1,0:T(8,128)S(1)}, u32[]{:S(2)}, u32[]{:S(2)}) collective-permute-start(f32[386,128]{1,0:T(8,128)S(1)} %add.107), channel_id=1, source_target_pairs={{0,8},{4,12},{8,0},{12,4},{16,24},{20,28},{24,16},{28,20},{1,9},{5... | collective-permute-start | bytes 592904 | tf_op jit(solution)/shard_map/ppermute | solution.py:434
  1068.4 24.7 %collective-permute-start.8 = (f32[386,128]{1,0:T(8,128)S(1)}, f32[386,128]{1,0:T(8,128)S(1)}, u32[]{:S(2)}, u32[]{:S(2)}) collective-permute-start(f32[386,128]{1,0:T(8,128)S(1)} %add_add_fusion.1), channel_id=1, source_target_pairs={{0,16},{4,20},{8,24},{12,28},{16,0},{20,4},{24,8},{28,12},{1,17},{... | collective-permute-start | bytes 592904 | tf_op jit(solution)/shard_map/ppermute | solution.py:434
  1085.1 1.4 copy-start
  1086.5 8.2 copy-start.26
  1086.5 8.2 copy-start.27
  1086.5 9.5 copy-start.4
  1086.5 9.5 copy-start.6
  1093.1 1.5 collective-permute-start.9
Sparse Core Ops, SparseCore 0:
  186.6 172.2 reduce-scatter.6
  362.3 170.8 reduce-scatter.8
  535.1 175.9 all-gather.4
  712.8 175.9 all-gather.6

commit v5 on v4

--- a/solution.py
+++ b/solution.py
@@ -227,11 +227,13 @@
     )(z, g, x, norms, gate_w, out_w)
 
 
-def edge_grad_kernel(nparts, unroll, sc, left, own, other, gx, gleft, keep, send, lt, rt, gt):
+def edge_grad_kernel(nparts, unroll, sc, left, own, other, gxs, gleft, keep, send, lt, rt, gt,
+                     gtile):
     s = pl.program_id(0)
     steps = pl.num_programs(0) // 2
     rows, nk, chan = left.shape
-    nrow = gx.shape[2] // 2
+    nrow = gtile.shape[1] // 2
+    gxs = [v.at[0] for v in gxs]
     half = nparts * nrow
     core = sc[0]
 
@@ -241,8 +243,15 @@
         lt[:, pl.ds(at, rows), :] = to_major(left[...])
         rt[:, pl.ds(pl.multiple_of(core * half + at, rows), rows), :] = to_major(own[...])
         rt[:, pl.ds(pl.multiple_of((1 - core) * half + at, rows), rows), :] = to_major(other[...])
+        tiles = gxs
+        if len(gxs) > nparts:
+            for h in range(2):
+                @pl.when((s >= steps // 2) if h else (s < steps // 2))
+                def _(h=h):
+                    gtile[...] = gxs[nparts - 1 + h][...]
+            tiles = gxs[:nparts - 1] + [gtile]
         g = jnp.concatenate([
-            gx[q, :, c * nrow:(c + 1) * nrow] for c in range(2) for q in range(nparts)
+            tiles[q][:, c * nrow:(c + 1) * nrow] for c in range(2) for q in range(nparts)
         ], axis=1)
         gt[:, pl.ds(at, rows), :] = to_major(g)
 
@@ -263,33 +272,48 @@
         send[...] = to_minor(rt[:, pl.ds(pl.multiple_of((1 - core) * half + at, rows), rows), :])
 
 
-def edge_grad_call(scal, left, own, other, gx, token):
+def edge_grad_call(scal, left, own, other, gxs, token):
     tokens = [] if token is None else [token]
-    nparts = gx.shape[0]
     ni, nk, chan = left.shape
+    nj = 2 * ni
+    nparts = nj // gxs[0].shape[-2]
     nrow = ni // nparts
-    nj = 2 * ni
     rows = pick_rows(nrow)
+    per = nrow // rows
     steps, inward, outward = phases(ni, rows)
     edge = pl.BlockSpec((rows, nk, chan), lambda s, sc: (inward(s), 0, 0))
+    part = lambda way: pl.BlockSpec(
+        (rows, nk, chan), lambda s, sc: (sc[1 + way(s) // per] * per + way(s) % per, 0, 0))
     back = pl.BlockSpec((rows, nk, chan), lambda s, sc: (outward(s), 0, 0))
+    block = (1, rows, 2 * nrow, chan)
+    if len(gxs) == 1:
+        specs = [pl.BlockSpec(block, lambda s, sc, q=q: (q, inward(s), 0, 0))
+                 for q in range(nparts)]
+        gxs = gxs * nparts
+    else:
+        gxs = [v[None] for v in gxs]
+        specs = [pl.BlockSpec(block, lambda s, sc: (0, inward(s), 0, 0))] * (nparts - 1)
+        specs += [pl.BlockSpec(block, lambda s, sc, h=h: (
+            0, jnp.clip(s - h * (steps // 2), 0, steps // 2 - 1), 0, 0)) for h in range(2)]
+    count = len(gxs)
     return pl.pallas_call(
-        lambda *refs: edge_grad_kernel(nparts, 16, *refs[:5], *refs[5 + len(tokens):]),
+        lambda *refs: edge_grad_kernel(nparts, 16, *refs[:4], refs[4:4 + count],
+                                       *refs[4 + count + len(tokens):]),
         grid_spec=pltpu.PrefetchScalarGridSpec(
             num_scalar_prefetch=1,
             grid=(2 * steps,),
-            in_specs=[edge] * 3 + [pl.BlockSpec((nparts, rows, 2 * nrow, chan),
-                                                lambda s, sc: (0, inward(s), 0, 0))]
+            in_specs=[edge, part(inward), part(inward)] + specs
             + [pl.BlockSpec(memory_space=pl.ANY)] * len(tokens),
-            out_specs=[back] * 3,
+            out_specs=[back, part(outward), part(outward)],
             scratch_shapes=[pltpu.VMEM((chan, ni, nk), LOW), pltpu.VMEM((chan, nj, nk), LOW),
-                            pltpu.VMEM((chan, ni, nj), LOW)],
+                            pltpu.VMEM((chan, ni, nj), LOW),
+                            pltpu.VMEM((rows, 2 * nrow, chan), LOW)],
         ),
         out_shape=[sds(left.shape, LOW)] * 3,
         compiler_params=params(58),
         cost_estimate=cost(5),
         name="edge_grad",
-    )(scal, left, own, other, gx, *tokens)
+    )(scal, left, own, other, *gxs, *tokens)
 
 
 def input_kernel(sub, z_ref, g_ref, gleft, keep, got, gate_grad, norms, proj, rowm, colm,
@@ -398,7 +422,9 @@
     weight_low = weights.astype(LOW)
     project_low = jnp.concatenate([weight_low[n] for n in range(5)], axis=1)
     mask_float = residue_mask.astype(F32)
-    scal = jnp.stack([core]).astype(jnp.int32)
+    by_column = jnp.stack([core] + list(range(cols))).astype(jnp.int32)
+    by_distance = jnp.stack([core] + [col ^ e for e in range(cols)]).astype(jnp.int32)
+    near = [b for b in range(batches - 1) if cols == 4]
     same_core = [[2 * q + c for q in range(zeds)] for c in range(2)]
 
     def zswap(blocks):
@@ -415,6 +441,17 @@
 
     def blocked(v):
         return v.reshape(zeds, nrow, ncol, chan)
+
+    def col_move(v, e):
+        return lax.ppermute(v, "col", [(q, q ^ e) for q in range(cols)])
+
+    def gather_near(own):
+        return [own, col_move(own, 1), col_move(own, 2)]
+
+    def gather_far(near):
+        own, from_x, from_y = near
+        half = own.shape[0] // 2
+        return near + [col_move(from_y[:half], 1), col_move(from_x[half:], 2)]
 
     def sum_col(term):
         count = term.shape[0] // 2
@@ -469,7 +506,7 @@
             pairs[b] = after(pairs[b], part)
         left, right, other = edges(b)
         kept.append((left, right, other))
-        part = product_call(scal, left, right, other, cols, 33 if b else 3)
+        part = product_call(by_column, left, right, other, cols, 33 if b else 3)
         ready = after(part, reduced[b - 1], cots[b - 1]) if b else part
         reduced.append(flat(lax.psum_scatter(ready, "col", scatter_dimension=0, tiled=True)))
     def collect(pieces, whole=None):
@@ -485,7 +522,13 @@
         last = zswap(after(blocked(new), last))
         news.append((last, b, 0, 1))
         ready = after(gx, (gathered[b - 1], last) if b else reduced[-1])
-        gathered.append(lax.all_gather(ready, "col", axis=0))
+        if b - 1 in near:
+            gathered[b - 1] = gather_far(after(gathered[b - 1], gx, news[b - 1][0]))
+            ready = after(gx, gathered[b - 1], last)
+        if b in near:
+            gathered.append(gather_near(ready))
+        else:
+            gathered.append([lax.all_gather(ready, "col", axis=0)])
         gates.append(gate_grad)
         sums.append((wout, nout))
     new_pair, placed = collect(news)
@@ -494,7 +537,9 @@
         final = b == batches - 1
         wout, nout = sums[b]
         grad = after(gathered[b], out) if b else gathered[b]
-        gleft, keep, send = edge_grad_call(scal, *kept[b], grad, placed if b else None)
+        if b in near and final:
+            grad = gather_far(grad)
+        gleft, keep, send = edge_grad_call(by_distance if b in near else by_column, *kept[b], grad, placed if b else None)
         got = coreswap(send)
         if b:
             got = after(got, last)

time: 1110 us -> 1090 us (0.982)
  blocking collectives: 110 us -> 0 us
  waiting for transfers between devices: 557 us -> 631 us
    all_to_all x1 -> x0, blocking collectives: 110 us -> none  [zswap(): lax.all_to_all(blocks, 'row', 0, 0, tiled=True, axis_index_groups=same_core)]
    ppermute x0 -> x4, waiting for transfers between devices: none -> 105 us  [col_move(): return lax.ppermute(v, 'col', [(q, q ^ e) for q in range(cols)])]
    all_gather x2 -> x1, waiting for transfers between devices: 102 us -> 74.1 us  [shards(): gathered.append([lax.all_gather(ready, 'col', axis=0)])]
    all_to_all x8 -> x9, starting transfers between devices: 39.7 us -> 44.8 us  [zswap(): lax.all_to_all(blocks, 'row', 0, 0, tiled=True, axis_index_groups=same_core)]
    all_to_all x8 -> x9, waiting for transfers between devices: 339 us -> 336 us  [zswap(): lax.all_to_all(blocks, 'row', 0, 0, tiled=True, axis_index_groups=same_core)]
    unnamed x6 -> x5, waiting for transfers between devices: 58.3 us -> 59.2 us
  transfers between devices with their start and end apart: 22 -> 26, of which waited for: 17 -> 20; matrix products, arithmetic and copies ran while one was open for 3% -> 3% of each run, Pallas kernels for 28% -> 29%
where the time goes in v5:
time: 1090 us
  waiting for transfers between devices  631 us (58%)
  Pallas kernels  334 us (31%)
  starting transfers between devices  59.6 us (5%)
  local copies, waits for them, and re-layouts  41.6 us (4%)
  between operations  14.2 us (1%)
    all_to_all x9, waiting for transfers between devices, zswap(): lax.all_to_all(blocks, 'row', 0, 0, tiled=True, axis_index_groups=same_core)  336 us
    ppermute x4, waiting for transfers between devices, col_move(): return lax.ppermute(v, 'col', [(q, q ^ e) for q in range(cols)])  105 us
    pallas_call x2, Pallas kernels, edge_grad_call(): pl.pallas_call(lambda *refs: edge_grad_kernel(nparts, 16, *refs[:4], refs...  98.1 us
    all_gather x1, waiting for transfers between devices, shards(): gathered.append([lax.all_gather(ready, 'col', axis=0)])  74.1 us
    pallas_call x2, Pallas kernels, product_call(): pl.pallas_call(lambda *refs: product_kernel(nparts, 16, *refs), grid_spec...  65.8 us
    pallas_call x3, Pallas kernels, input_call(): pl.pallas_call(lambda *refs: input_kernel(sub, *refs[:10], *refs[10 + len...  62.8 us
    unnamed x5, waiting for transfers between devices  59.2 us
    all_to_all x9, starting transfers between devices, zswap(): lax.all_to_all(blocks, 'row', 0, 0, tiled=True, axis_index_groups=same_core)  44.8 us
  transfers between devices with their start and end apart: 26, of which 20 were waited for; matrix products, arithmetic and copies ran while one was open for 3% of the time, Pallas kernels for 29%

profile of v5, /device:TPU:0, one launch (start us, length us, event | category | flops | bytes accessed | tf_op | source)
XLA Modules:
  0.0 1087.5 jit_solution(14793576087534202856)
XLA Ops:
  7.2 5.4 slice.54
  12.6 6.4 all-to-all-start
  20.3 1.2 fusion.2
  21.6 5.6 slice.55
  29.2 9.1 fusion.3
  38.3 85.5 %all-to-all-done = bf16[4,48,96,128]{3,2,1,0:T(8,128)(2,1)} async-done(((bf16[4,48,96,128]{3,2,1,0:T(8,128)(2,1)}), bf16[4,48,96,128]{3,2,1,0:T(8,128)(2,1)}, u32[]{:S(2)}, u32[]{:S(2)}) %all-to-all-start) | async-done | bytes 4718624 | tf_op jit(solution)/shard_map/all_to_all | solution.py:431
  123.8 4.9 all-to-all-start.1
  130.2 15.9 %edges.2 = (bf16[192,96,128]{2,1,0:T(8,128)(2,1)}, bf16[192,96,128]{2,1,0:T(8,128)(2,1)}) custom-call(bf16[192,96,128]{2,1,0:T(8,128)(2,1)} %bitcast.2.refs_0_, f32[4,128]{1,0:T(4,128)} %refs_6_.5, bf16[128,512]{1,0:T(8,128)(2,1)} %pad_maximum_fusion.1.refs_2_, f32[192,128]{1,0:T(8,128)} %broadcast_in_dim.60.refs_3_, f32[96,128]{1,0:T(8,128)} %broadcast_in_dim.62.refs_4_.refs_9_), custom_call_target="tpu_custom_call" | custom-call | flops 161999994880 | tf_op jit(solution)/shard_map/edges/pallas_call | solution.py:100
  146.2 1.2 fusion.1
  148.1 6.2 collective-permute-done.refs_3_
  154.4 32.7 %product.2 = bf16[4,192,96,128]{3,2,1,0:T(8,128)(2,1)} custom-call(s32[5]{0:T(128)} %stack.23.refs_0_, bf16[192,96,128]{2,1,0:T(8,128)(2,1)} %get-tuple-element.70.refs_1_, bf16[192,96,128]{2,1,0:T(8,128)(2,1)} %get-tuple-element.71.refs_2_, bf16[192,96,128]{2,1,0:T(8,128)(2,1)} %collective-permute-done.refs_3_), custom_call_target="tpu_custom_call" | custom-call | flops 17999998976 | tf_op jit(solution)/shard_map/product/pallas_call | solution.py:157
  187.1 45.5 %all-to-all-done.1 = bf16[4,48,96,128]{3,2,1,0:T(8,128)(2,1)} async-done(((bf16[4,48,96,128]{3,2,1,0:T(8,128)(2,1)}), bf16[4,48,96,128]{3,2,1,0:T(8,128)(2,1)}, u32[]{:S(2)}, u32[]{:S(2)}) %all-to-all-start.1) | async-done | bytes 4718624 | tf_op jit(solution)/shard_map/all_to_all | solution.py:431
  234.0 15.9 %edges.3 = (bf16[192,96,128]{2,1,0:T(8,128)(2,1)}, bf16[192,96,128]{2,1,0:T(8,128)(2,1)}) custom-call(bf16[192,96,128]{2,1,0:T(8,128)(2,1)} %bitcast.refs_0_, f32[4,128]{1,0:T(4,128)} %refs_6_.5, bf16[128,512]{1,0:T(8,128)(2,1)} %pad_maximum_fusion.1.refs_2_, f32[192,128]{1,0:T(8,128)} %broadcast_in_dim.64.refs_3_, f32[96,128]{1,0:T(8,128)} %broadcast_in_dim.66.refs_4_.refs_9_), custom_call_target="tpu_custom_call" | custom-call | flops 161999994880 | tf_op jit(solution)/shard_map/edges/pallas_call | solution.py:100
  249.9 5.1 all-to-all-start.2
  255.2 2.9 collective-permute-done.1.refs_3_
  258.2 33.1 %product.3 = bf16[4,192,96,128]{3,2,1,0:T(8,128)(2,1)} custom-call(s32[5]{0:T(128)} %stack.23.refs_0_, bf16[192,96,128]{2,1,0:T(8,128)(2,1)} %get-tuple-element.75.refs_1_, bf16[192,96,128]{2,1,0:T(8,128)(2,1)} %get-tuple-element.76.refs_2_, bf16[192,96,128]{2,1,0:T(8,128)(2,1)} %collective-permute-done.1.refs_3_), custom_call_target="tpu_custom_call" | custom-call | flops 198000001024 | tf_op jit(solution)/shard_map/product/pallas_call | solution.py:157
  291.3 69.0 %all-to-all-done.2 = bf16[4,48,96,128]{3,2,1,0:T(8,128)(2,1)} async-done(((bf16[4,48,96,128]{3,2,1,0:T(8,128)(2,1)}), bf16[4,48,96,128]{3,2,1,0:T(8,128)(2,1)}, u32[]{:S(2)}, u32[]{:S(2)}) %all-to-all-start.2) | async-done | bytes 4718624 | tf_op jit(solution)/shard_map/all_to_all | solution.py:431
  360.3 5.0 all-to-all-start.3
  365.3 21.9 %middle.3 = (bf16[192,96,128]{2,1,0:T(8,128)(2,1)}, bf16[192,96,128]{2,1,0:T(8,128)(2,1)}, bf16[192,96,128]{2,1,0:T(8,128)(2,1)}, f32[128,128]{1,0:T(8,128)}, f32[2,8,128]{2,1,0:T(8,128)}) custom-call(bf16[192,96,128]{2,1,0:T(8,128)(2,1)} %bitcast.2.refs_0_, bf16[192,96,128]{2,1,0:T(8,128)(2,1)} %bitcast.12.refs_1_, bf16[192,96,128]{2,1,0:T(8,128)(2,1)} %bitcast.87, ...), custom_call_target="tpu_custom_call" | custom-call | flops 240000008192 | tf_op jit(solution)/shard_map/middle/pallas_call | solution.py:217
  387.2 82.5 %all-to-all-done.3 = bf16[4,48,96,128]{3,2,1,0:T(8,128)(2,1)} async-done(((bf16[4,48,96,128]{3,2,1,0:T(8,128)(2,1)}), bf16[4,48,96,128]{3,2,1,0:T(8,128)(2,1)}, u32[]{:S(2)}, u32[]{:S(2)}) %all-to-all-start.3) | async-done | bytes 4718624 | tf_op jit(solution)/shard_map/all_to_all | solution.py:431
  469.7 4.9 all-to-all-start.4
  474.6 59.2 %reduce-scatter.9.cloned.1.call-done = bf16[1,192,96,128]{3,2,1,0:T(8,128)(2,1)} async-done(((bf16[4,192,96,128]{3,2,1,0:T(8,128)(2,1)}), bf16[1,192,96,128]{3,2,1,0:T(8,128)(2,1)}) %reduce-scatter.9.cloned.1.call-update) | async-done | bytes 4718608
  533.8 1.4 collective-permute-start.2
  535.8 21.8 %middle.2 = (bf16[192,96,128]{2,1,0:T(8,128)(2,1)}, bf16[192,96,128]{2,1,0:T(8,128)(2,1)}, bf16[192,96,128]{2,1,0:T(8,128)(2,1)}, f32[128,128]{1,0:T(8,128)}, f32[2,8,128]{2,1,0:T(8,128)}) custom-call(bf16[192,96,128]{2,1,0:T(8,128)(2,1)} %bitcast.refs_0_, bf16[192,96,128]{2,1,0:T(8,128)(2,1)} %bitcast.8.refs_1_, bf16[192,96,128]{2,1,0:T(8,128)(2,1)} %bitcast.88, ...), custom_call_target="tpu_custom_call" | custom-call | flops 240000008192 | tf_op jit(solution)/shard_map/middle/pallas_call | solution.py:217
  557.6 21.0 %all-to-all-done.4.refs_0_ = bf16[4,48,96,128]{3,2,1,0:T(8,128)(2,1)} async-done(((bf16[4,48,96,128]{3,2,1,0:T(8,128)(2,1)}), bf16[4,48,96,128]{3,2,1,0:T(8,128)(2,1)}, u32[]{:S(2)}, u32[]{:S(2)}) %all-to-all-start.4) | async-done | bytes 4718624 | tf_op jit(solution)/shard_map/all_to_all | solution.py:431
  578.6 5.0 all-to-all-start.5
  583.6 54.0 %collective-permute-done.2 = bf16[192,96,128]{2,1,0:T(8,128)(2,1)} collective-permute-done((bf16[192,96,128]{2,1,0:T(8,128)(2,1)}, bf16[192,96,128]{2,1,0:T(8,128)(2,1)}, u32[]{:S(2)}, u32[]{:S(2)}) %collective-permute-start.2) | collective-permute-done | bytes 4718624 | tf_op jit(solution)/shard_map/ppermute | solution.py:446
  637.6 1.1 collective-permute-done.3
  638.7 1.8 slice.64
  641.3 1.8 slice.65
  643.1 1.5 collective-permute-start.5
  644.6 47.8 %collective-permute-done.4 = bf16[96,96,128]{2,1,0:T(8,128)(2,1)S(1)} collective-permute-done((bf16[96,96,128]{2,1,0:T(8,128)(2,1)S(1)}, bf16[96,96,128]{2,1,0:T(8,128)(2,1)S(1)}, u32[]{:S(2)}, u32[]{:S(2)}) %collective-permute-start.4) | collective-permute-done | bytes 2359328 | tf_op jit(solution)/shard_map/ppermute | solution.py:446
  692.4 2.4 collective-permute-done.5
  695.5 51.0 %edge_grad.2 = (bf16[192,96,128]{2,1,0:T(8,128)(2,1)}, bf16[192,96,128]{2,1,0:T(8,128)(2,1)}, bf16[192,96,128]{2,1,0:T(8,128)(2,1)}) custom-call(s32[5]{0:T(128)} %stack.28.refs_0_, bf16[192,96,128]{2,1,0:T(8,128)(2,1)} %get-tuple-element.70.refs_1_, bf16[192,96,128]{2,1,0:T(8,128)(2,1)} %get-tuple-element.71.refs_2_, ...), custom_call_target="tpu_custom_call" | custom-call | flops 30000001024 | tf_op jit(solution)/shard_map/edge_grad/pallas_call | solution.py:299
  746.7 6.9 place.5
  753.6 6.9 place.6
  761.2 30.4 %input_grad.3 = (bf16[192,96,128]{2,1,0:T(8,128)(2,1)}, f32[128,640]{1,0:T(8,128)}, f32[2,8,128]{2,1,0:T(8,128)}) custom-call(bf16[192,96,128]{2,1,0:T(8,128)(2,1)} %bitcast.2.refs_0_, bf16[192,96,128]{2,1,0:T(8,128)(2,1)} %bitcast.12.refs_1_, bf16[192,96,128]{2,1,0:T(8,128)(2,1)} %get-tuple-element.91.refs_2_, ...), custom_call_target="tpu_custom_call" | custom-call | flops 30000001024 | tf_op jit(solution)/shard_map/input_grad/pallas_call | solution.py:373
  791.6 5.2 all-to-all-start.6
  796.8 74.1 %all-gather.3.cloned.1.call-done = bf16[768,96,128]{2,1,0:T(8,128)(2,1)} async-done(((bf16[192,96,128]{2,1,0:T(8,128)(2,1)}), bf16[768,96,128]{2,1,0:T(8,128)(2,1)}) %all-gather.3.cloned.1.call-update) | async-done | bytes 18874384 | tf_op jit(solution)/shard_map/all_gather | solution.py:531
  870.9 47.1 %edge_grad.3 = (bf16[192,96,128]{2,1,0:T(8,128)(2,1)}, bf16[192,96,128]{2,1,0:T(8,128)(2,1)}, bf16[192,96,128]{2,1,0:T(8,128)(2,1)}) custom-call(s32[5]{0:T(128)} %stack.23.refs_0_, bf16[192,96,128]{2,1,0:T(8,128)(2,1)} %get-tuple-element.75.refs_1_, bf16[192,96,128]{2,1,0:T(8,128)(2,1)} %get-tuple-element.76.refs_2_, ...), custom_call_target="tpu_custom_call" | custom-call | flops 30000001024 | tf_op jit(solution)/shard_map/edge_grad/pallas_call | solution.py:299
  921.2 0.9 copy.33
  922.1 6.8 place.7
  929.0 0.8 broadcast_in_dim.75.refs_8_
  929.7 16.1 %input_grad.5 = (bf16[96,96,128]{2,1,0:T(8,128)(2,1)}, f32[128,640]{1,0:T(8,128)}, f32[2,8,128]{2,1,0:T(8,128)}) custom-call(bf16[192,96,128]{2,1,0:T(8,128)(2,1)} %bitcast.refs_0_, bf16[192,96,128]{2,1,0:T(8,128)(2,1)} %bitcast.8.refs_1_, bf16[192,96,128]{2,1,0:T(8,128)(2,1)} %get-tuple-element.100.refs_2_, ...), custom_call_target="tpu_custom_call" | custom-call | flops 161999994880 | tf_op jit(solution)/shard_map/input_grad/pallas_call | solution.py:373
  945.9 4.6 all-to-all-start.7
  950.6 16.3 %input_grad.4 = (bf16[96,96,128]{2,1,0:T(8,128)(2,1)}, f32[128,640]{1,0:T(8,128)}, f32[2,8,128]{2,1,0:T(8,128)}) custom-call(bf16[192,96,128]{2,1,0:T(8,128)(2,1)} %bitcast.refs_0_, bf16[192,96,128]{2,1,0:T(8,128)(2,1)} %bitcast.8.refs_1_, bf16[192,96,128]{2,1,0:T(8,128)(2,1)} %get-tuple-element.100.refs_2_, ...), custom_call_target="tpu_custom_call" | custom-call | flops 161999994880 | tf_op jit(solution)/shard_map/input_grad/pallas_call | solution.py:373
  967.2 1.1 copy.36
  970.1 1.1 collective-permute-done.8
  971.3 1.5 collective-permute-start.9
  972.8 5.8 collective-permute-done.9
  978.6 1.5 collective-permute-start.10
  980.1 5.1 collective-permute-done.10
  985.3 20.0 %all-to-all-done.7.refs_0_ = bf16[4,24,96,128]{3,2,1,0:T(8,128)(2,1)} async-done(((bf16[4,24,96,128]{3,2,1,0:T(8,128)(2,1)}), bf16[4,24,96,128]{3,2,1,0:T(8,128)(2,1)}, u32[]{:S(2)}, u32[]{:S(2)}) %all-to-all-start.7) | async-done | bytes 2359328 | tf_op jit(solution)/shard_map/all_to_all | solution.py:431
  1005.2 3.6 all-to-all-start.8
  1008.9 2.0 collective-permute-start.11
  1010.9 5.8 place.8
  1017.3 34.0 %collective-permute-done.11 = f32[386,128]{1,0:T(8,128)S(1)} collective-permute-done((f32[386,128]{1,0:T(8,128)S(1)}, f32[386,128]{1,0:T(8,128)S(1)}, u32[]{:S(2)}, u32[]{:S(2)}) %collective-permute-start.11) | collective-permute-done | bytes 197664 | tf_op jit(solution)/shard_map/ppermute | solution.py:471
  1051.3 4.7 collective-permute-start.12
  1056.0 12.0 %all-to-all-done.8.refs_0_ = bf16[4,24,96,128]{3,2,1,0:T(8,128)(2,1)S(1)} async-done(((bf16[4,24,96,128]{3,2,1,0:T(8,128)(2,1)}), bf16[4,24,96,128]{3,2,1,0:T(8,128)(2,1)S(1)}, u32[]{:S(2)}, u32[]{:S(2)}) %all-to-all-start.8) | async-done | bytes 2359328 | tf_op jit(solution)/shard_map/all_to_all | solution.py:431
  1068.0 1.4 copy-done
  1069.4 5.9 place.9
  1076.1 1.4 collective-permute-done.13
  1077.6 1.3 multiply_add_fusion.2
  1078.9 2.1 multiply_add_fusion
  (126 shorter events, 17.2 us)
Async XLA Ops:
  12.6 6.5 copy-start.13
  12.6 9.0 copy-start.3
  12.6 111.2 %all-to-all-start = ((bf16[4,48,96,128]{3,2,1,0:T(8,128)(2,1)}), bf16[4,48,96,128]{3,2,1,0:T(8,128)(2,1)}, u32[]{:S(2)}, u32[]{:S(2)}) async-start(bf16[4,48,96,128]{3,2,1,0:T(8,128)(2,1)} %slice.54), calls=%async_computation | async-start | bytes 9437184 | tf_op jit(solution)/shard_map/all_to_all | solution.py:431
  21.6 6.2 copy-start.1
  123.8 108.8 %all-to-all-start.1 = ((bf16[4,48,96,128]{3,2,1,0:T(8,128)(2,1)}), bf16[4,48,96,128]{3,2,1,0:T(8,128)(2,1)}, u32[]{:S(2)}, u32[]{:S(2)}) async-start(bf16[4,48,96,128]{3,2,1,0:T(8,128)(2,1)} %slice.55), calls=%async_computation.1 | async-start | bytes 9437184 | tf_op jit(solution)/shard_map/all_to_all | solution.py:431
  128.7 231.5 %reduce-scatter.7.cloned.1.call-start = ((), (), s32[]{:S(2)}) async-start(), calls=%async_computation.12 | async-start | bytes 23592960
  130.2 15.9 %copy-start.20 = (f32[384]{0:T(512)S(1)}, f32[384]{0:T(512)}, u32[]{:S(2)}) copy-start(f32[384]{0:T(512)} %get-tuple-element.126) | copy-start | bytes 4612
  146.1 8.3 collective-permute-start
  187.1 46.3 %copy-start.25 = (f32[96]{0:T(128)S(1)}, f32[96]{0:T(128)}, u32[]{:S(2)}) copy-start(f32[96]{0:T(128)} %get-tuple-element.148) | copy-start | bytes 1156
  249.9 8.3 collective-permute-start.1
  249.9 110.4 %all-to-all-start.2 = ((bf16[4,48,96,128]{3,2,1,0:T(8,128)(2,1)}), bf16[4,48,96,128]{3,2,1,0:T(8,128)(2,1)}, u32[]{:S(2)}, u32[]{:S(2)}) async-start(bf16[4,48,96,128]{3,2,1,0:T(8,128)(2,1)} %get-tuple-element.73), calls=%async_computation.2 | async-start | bytes 9437184 | tf_op jit(solution)/shard_map/all_to_all | solution.py:431
  255.0 278.8 %reduce-scatter.9.cloned.1.call-start = ((), (), s32[]{:S(2)}) async-start(), calls=%async_computation.13 | async-start | bytes 23592960
  360.3 109.4 %all-to-all-start.3 = ((bf16[4,48,96,128]{3,2,1,0:T(8,128)(2,1)}), bf16[4,48,96,128]{3,2,1,0:T(8,128)(2,1)}, u32[]{:S(2)}, u32[]{:S(2)}) async-start(bf16[4,48,96,128]{3,2,1,0:T(8,128)(2,1)} %get-tuple-element.74), calls=%async_computation.3 | async-start | bytes 9437184 | tf_op jit(solution)/shard_map/all_to_all | solution.py:431
  469.7 108.9 %all-to-all-start.4 = ((bf16[4,48,96,128]{3,2,1,0:T(8,128)(2,1)}), bf16[4,48,96,128]{3,2,1,0:T(8,128)(2,1)}, u32[]{:S(2)}, u32[]{:S(2)}) async-start(bf16[4,48,96,128]{3,2,1,0:T(8,128)(2,1)} %bitcast.70), calls=%async_computation.4 | async-start | bytes 9437184 | tf_op jit(solution)/shard_map/all_to_all | solution.py:431
  533.8 103.8 %collective-permute-start.2 = (bf16[192,96,128]{2,1,0:T(8,128)(2,1)}, bf16[192,96,128]{2,1,0:T(8,128)(2,1)}, u32[]{:S(2)}, u32[]{:S(2)}) collective-permute-start(bf16[192,96,128]{2,1,0:T(8,128)(2,1)} %get-tuple-element.87), channel_id=1, source_target_pairs={{0,1},{1,0},{2,3},{3,2},{4,5},{5,4},{6,7},{7,6},{8,9},{9,8},{10,11... | collective-permute-start | bytes 14155784 | tf_op jit(solution)/shard_map/ppermute | solution.py:446
  535.2 103.5 %collective-permute-start.3 = (bf16[192,96,128]{2,1,0:T(8,128)(2,1)}, bf16[192,96,128]{2,1,0:T(8,128)(2,1)}, u32[]{:S(2)}, u32[]{:S(2)}) collective-permute-start(bf16[192,96,128]{2,1,0:T(8,128)(2,1)} %get-tuple-element.87), channel_id=1, source_target_pairs={{0,2},{1,3},{2,0},{3,1},{4,6},{5,7},{6,4},{7,5},{8,10},{9,11},{10,... | collective-permute-start | bytes 14155784 | tf_op jit(solution)/shard_map/ppermute | solution.py:446
  578.6 116.2 %all-to-all-start.5 = ((bf16[4,48,96,128]{3,2,1,0:T(8,128)(2,1)}), bf16[4,48,96,128]{3,2,1,0:T(8,128)(2,1)}, u32[]{:S(2)}, u32[]{:S(2)}) async-start(bf16[4,48,96,128]{3,2,1,0:T(8,128)(2,1)} %bitcast.69), calls=%async_computation.5 | async-start | bytes 9437184 | tf_op jit(solution)/shard_map/all_to_all | solution.py:431
  583.6 287.3 %all-gather.3.cloned.1.call-start = ((), (), s32[]{:S(2)}) async-start(), calls=%async_computation.11 | async-start | bytes 23592960 | tf_op jit(solution)/shard_map/all_gather | solution.py:531
  640.6 51.8 %collective-permute-start.4 = (bf16[96,96,128]{2,1,0:T(8,128)(2,1)S(1)}, bf16[96,96,128]{2,1,0:T(8,128)(2,1)S(1)}, u32[]{:S(2)}, u32[]{:S(2)}) collective-permute-start(bf16[96,96,128]{2,1,0:T(8,128)(2,1)S(1)} %slice.64), channel_id=1, source_target_pairs={{0,1},{1,0},{2,3},{3,2},{4,5},{5,4},{6,7},{7,6},{8,9},{9,8},{10,11... | collective-permute-start | bytes 7077896 | tf_op jit(solution)/shard_map/ppermute | solution.py:446
  643.1 51.6 %collective-permute-start.5 = (bf16[96,96,128]{2,1,0:T(8,128)(2,1)S(1)}, bf16[96,96,128]{2,1,0:T(8,128)(2,1)}, u32[]{:S(2)}, u32[]{:S(2)}) collective-permute-start(bf16[96,96,128]{2,1,0:T(8,128)(2,1)S(1)} %slice.65), channel_id=1, source_target_pairs={{0,2},{1,3},{2,0},{3,1},{4,6},{5,7},{6,4},{7,5},{8,10},{9,11},{10,... | collective-permute-start | bytes 7077896 | tf_op jit(solution)/shard_map/ppermute | solution.py:446
  692.4 3.1 copy-start.28
  695.5 51.0 %copy-start.14 = (f32[4,1,48]{2,1,0:T(1,128)S(1)}, f32[4,1,48]{2,1,0:T(1,128)}, u32[]{:S(2)}) copy-start(f32[4,1,48]{2,1,0:T(1,128)} %get-tuple-element.137) | copy-start | bytes 2308
  695.5 51.1 %copy-start.2 = (bf16[6,128,128]{2,1,0:T(8,128)(2,1)S(1)}, bf16[6,128,128]{2,1,0:T(8,128)(2,1)}, u32[]{:S(2)}) copy-start(bf16[6,128,128]{2,1,0:T(8,128)(2,1)} %copy-done.1) | copy-start | bytes 589828
  746.5 14.0 %collective-permute-start.6 = (bf16[192,96,128]{2,1,0:T(8,128)(2,1)}, bf16[192,96,128]{2,1,0:T(8,128)(2,1)}, u32[]{:S(2)}, u32[]{:S(2)}) collective-permute-start(bf16[192,96,128]{2,1,0:T(8,128)(2,1)} %get-tuple-element.93), channel_id=1, source_target_pairs={{0,4},{4,0},{8,12},{12,8},{16,20},{20,16},{24,28},{28,24},{1,5},{5... | collective-permute-start | bytes 14155784 | tf_op jit(solution)/shard_map/ppermute | solution.py:434
  746.7 13.8 %copy-start.21 = (bf16[128,640]{1,0:T(8,128)(2,1)}, bf16[128,640]{1,0:T(8,128)(2,1)S(1)}, u32[]{:S(2)}) copy-start(bf16[128,640]{1,0:T(8,128)(2,1)S(1)} %constant_dynamic-update-slice_fusion.refs_7_) | copy-start | bytes 491524
  791.6 130.5 %all-to-all-start.6 = ((bf16[4,48,96,128]{3,2,1,0:T(8,128)(2,1)}), bf16[4,48,96,128]{3,2,1,0:T(8,128)(2,1)}, u32[]{:S(2)}, u32[]{:S(2)}) async-start(bf16[4,48,96,128]{3,2,1,0:T(8,128)(2,1)} %bitcast.68), calls=%async_computation.6 | async-start | bytes 9437184 | tf_op jit(solution)/shard_map/all_to_all | solution.py:431
  870.9 47.1 %copy-start.15 = (f32[4,1,48]{2,1,0:T(1,128)S(1)}, f32[4,1,48]{2,1,0:T(1,128)}, u32[]{:S(2)}) copy-start(f32[4,1,48]{2,1,0:T(1,128)} %get-tuple-element.135) | copy-start | bytes 2308
  870.9 48.4 %copy-start.16 = (f32[2,8,128]{2,1,0:T(8,128)S(1)}, f32[2,8,128]{2,1,0:T(8,128)}, u32[]{:S(2)}) copy-start(f32[2,8,128]{2,1,0:T(8,128)} %get-tuple-element.109) | copy-start | bytes 24580
  870.9 49.0 %copy-start.17 = (f32[2,8,128]{2,1,0:T(8,128)S(1)}, f32[2,8,128]{2,1,0:T(8,128)}, u32[]{:S(2)}) copy-start(f32[2,8,128]{2,1,0:T(8,128)} %get-tuple-element.113) | copy-start | bytes 24580
  870.9 49.6 %copy-start.7 = (f32[128,640]{1,0:T(8,128)S(1)}, f32[128,640]{1,0:T(8,128)}, u32[]{:S(2)}) copy-start(f32[128,640]{1,0:T(8,128)} %get-tuple-element.96) | copy-start | bytes 983044
  870.9 49.8 %copy-start.18 = (f32[2,8,128]{2,1,0:T(8,128)S(1)}, f32[2,8,128]{2,1,0:T(8,128)}, u32[]{:S(2)}) copy-start(f32[2,8,128]{2,1,0:T(8,128)} %get-tuple-element.97) | copy-start | bytes 24580
  918.0 11.0 %collective-permute-start.7 = (bf16[192,96,128]{2,1,0:T(8,128)(2,1)}, bf16[192,96,128]{2,1,0:T(8,128)(2,1)}, u32[]{:S(2)}, u32[]{:S(2)}) collective-permute-start(bf16[192,96,128]{2,1,0:T(8,128)(2,1)} %get-tuple-element.102), channel_id=1, source_target_pairs={{0,4},{4,0},{8,12},{12,8},{16,20},{20,16},{24,28},{28,24},{1,5},{5... | collective-permute-start | bytes 14155784 | tf_op jit(solution)/shard_map/ppermute | solution.py:434
  945.9 59.3 %all-to-all-start.7 = ((bf16[4,24,96,128]{3,2,1,0:T(8,128)(2,1)}), bf16[4,24,96,128]{3,2,1,0:T(8,128)(2,1)}, u32[]{:S(2)}, u32[]{:S(2)}) async-start(bf16[4,24,96,128]{3,2,1,0:T(8,128)(2,1)} %bitcast.72), calls=%async_computation.7 | async-start | bytes 4718592 | tf_op jit(solution)/shard_map/all_to_all | solution.py:431
  950.5 16.4 %copy-start.8 = (f32[128,640]{1,0:T(8,128)S(1)}, f32[128,640]{1,0:T(8,128)}, u32[]{:S(2)}) copy-start(f32[128,640]{1,0:T(8,128)} %get-tuple-element.110) | copy-start | bytes 983044
  950.5 16.7 %copy-start.19 = (f32[2,8,128]{2,1,0:T(8,128)S(1)}, f32[2,8,128]{2,1,0:T(8,128)}, u32[]{:S(2)}) copy-start(f32[2,8,128]{2,1,0:T(8,128)} %get-tuple-element.112) | copy-start | bytes 24580
  950.5 18.7 %copy-start.5 = (f32[5,128,128]{2,1,0:T(8,128)S(1)}, f32[5,128,128]{2,1,0:T(8,128)}, u32[]{:S(2)}) copy-start(f32[5,128,128]{2,1,0:T(8,128)} %copy.33) | copy-start | bytes 983044
  950.5 18.7 %copy-start.9 = (f32[128,128]{1,0:T(8,128)S(1)}, f32[128,128]{1,0:T(8,128)}, u32[]{:S(2)}) copy-start(f32[128,128]{1,0:T(8,128)} %get-tuple-element.108) | copy-start | bytes 196612
  950.5 18.7 %copy-start.10 = (f32[128,128]{1,0:T(8,128)S(1)}, f32[128,128]{1,0:T(8,128)}, u32[]{:S(2)}) copy-start(f32[128,128]{1,0:T(8,128)} %get-tuple-element.111) | copy-start | bytes 196612
  950.5 18.7 %copy-start.11 = (f32[772]{0:T(1024)S(1)}, f32[772]{0:T(1024)}, u32[]{:S(2)}) copy-start(f32[772]{0:T(1024)} %pad.3.clone) | copy-start | bytes 9268
  950.5 18.7 %copy-start.12 = (f32[772]{0:T(1024)S(1)}, f32[772]{0:T(1024)}, u32[]{:S(2)}) copy-start(f32[772]{0:T(1024)} %pad.5.clone) | copy-start | bytes 9268
  950.6 18.7 %copy-start.22 = (f32[2,128]{1,0:T(2,128)S(1)}, f32[2,128]{1,0:T(2,128)}, u32[]{:S(2)}) copy-start(f32[2,128]{1,0:T(2,128)} %reduce_sum.46) | copy-start | bytes 3076
  950.6 18.7 %copy-start.23 = (f32[2,128]{1,0:T(2,128)S(1)}, f32[2,128]{1,0:T(2,128)}, u32[]{:S(2)}) copy-start(f32[2,128]{1,0:T(2,128)} %reduce_sum.48) | copy-start | bytes 3076
  950.6 18.7 %copy-start.24 = (f32[2,128]{1,0:T(2,128)S(1)}, f32[2,128]{1,0:T(2,128)}, u32[]{:S(2)}) copy-start(f32[2,128]{1,0:T(2,128)} %reduce_sum.45) | copy-start | bytes 3076
  969.6 1.6 collective-permute-start.8
  971.3 7.3 collective-permute-start.9
  978.6 6.6 collective-permute-start.10
  1005.2 62.8 %all-to-all-start.8 = ((bf16[4,24,96,128]{3,2,1,0:T(8,128)(2,1)}), bf16[4,24,96,128]{3,2,1,0:T(8,128)(2,1)S(1)}, u32[]{:S(2)}, u32[]{:S(2)}) async-start(bf16[4,24,96,128]{3,2,1,0:T(8,128)(2,1)} %bitcast.71), calls=%async_computation.8 | async-start | bytes 4718592 | tf_op jit(solution)/shard_map/all_to_all | solution.py:431
  1008.9 42.4 %collective-permute-start.11 = (f32[386,128]{1,0:T(8,128)S(1)}, f32[386,128]{1,0:T(8,128)S(1)}, u32[]{:S(2)}, u32[]{:S(2)}) collective-permute-start(f32[386,128]{1,0:T(8,128)S(1)} %add.107), channel_id=1, source_target_pairs={{0,8},{4,12},{8,0},{12,4},{16,24},{20,28},{24,16},{28,20},{1,9},{5... | collective-permute-start | bytes 592904 | tf_op jit(solution)/shard_map/ppermute | solution.py:471
  1051.3 24.7 %collective-permute-start.12 = (f32[386,128]{1,0:T(8,128)S(1)}, f32[386,128]{1,0:T(8,128)S(1)}, u32[]{:S(2)}, u32[]{:S(2)}) collective-permute-start(f32[386,128]{1,0:T(8,128)S(1)} %add_add_fusion.1), channel_id=1, source_target_pairs={{0,16},{4,20},{8,24},{12,28},{16,0},{20,4},{24,8},{28,12},{1,17},{... | collective-permute-start | bytes 592904 | tf_op jit(solution)/shard_map/ppermute | solution.py:471
  1068.0 1.4 copy-start
  1069.4 8.2 copy-start.26
  1069.4 8.2 copy-start.27
  1069.4 9.5 copy-start.4
  1069.4 9.5 copy-start.6
  1076.0 1.5 collective-permute-start.13
Sparse Core Ops, SparseCore 0:
  187.2 172.2 reduce-scatter.6
  362.9 170.8 reduce-scatter.8
  694.9 175.9 all-gather.2

commit v6 on v5

--- a/solution.py
+++ b/solution.py
@@ -532,7 +532,7 @@
         gates.append(gate_grad)
         sums.append((wout, nout))
     new_pair, placed = collect(news)
-    term, pair_grad, placed_back = 0.0, None, None
+    term, earlier = 0.0, []
     for b in range(batches):
         final = b == batches - 1
         wout, nout = sums[b]
@@ -548,7 +548,7 @@
         for h in range(share):
             out = input_call(pairs[b], cots[b], gleft, keep, got, gates[b], norm_params,
                              project_low, *masks[b], zeds, h, share, 27 if final else 5,
-                             placed_back)
+                             None)
             back, wproj, nin = out
             wproj = jnp.transpose(wproj.reshape(chan, 5, chan), (1, 0, 2)).reshape(5 * chan, chan)
             part = [wproj, jnp.zeros_like(wout) if h else wout, jnp.sum(nin, axis=1),
@@ -561,8 +561,8 @@
             last = zswap(after(back, last))
             backs.append((last, b, h, share))
         if not final:
-            pair_grad, placed_back = collect(backs, pair_grad)
-    pair_grad, second = collect(backs[:1], pair_grad)
+            earlier += backs
+    pair_grad, second = collect(earlier + backs[:1])
     pair_grad, third = collect(backs[1:], pair_grad)
     grads = sum_zed(after(term, backs[0][0]), second, third)
     grad_weights = grads[: 6 * chan].reshape(weights.shape)

time: 1090 us -> 1090 us (level)
  transfers between devices with their start and end apart: 26 -> 26, of which waited for: 20 -> 21; matrix products, arithmetic and copies ran while one was open for 3% -> 3% of each run, Pallas kernels for 29% -> 29%
where the time goes in v6:
time: 1090 us; the launch traced here: 1080 us
  waiting for transfers between devices  628 us (58%)
  Pallas kernels  334 us (31%)
  starting transfers between devices  59.2 us (5%)
  local copies, waits for them, and re-layouts  41.6 us (4%)
  between operations  14.2 us (1%)
    all_to_all x9, waiting for transfers between devices, zswap(): lax.all_to_all(blocks, 'row', 0, 0, tiled=True, axis_index_groups=same_core)  336 us
    ppermute x4, waiting for transfers between devices, col_move(): return lax.ppermute(v, 'col', [(q, q ^ e) for q in range(cols)])  105 us
    pallas_call x2, Pallas kernels, edge_grad_call(): pl.pallas_call(lambda *refs: edge_grad_kernel(nparts, 16, *refs[:4], refs...  98.1 us
    all_gather x1, waiting for transfers between devices, shards(): gathered.append([lax.all_gather(ready, 'col', axis=0)])  74.1 us
    pallas_call x2, Pallas kernels, product_call(): pl.pallas_call(lambda *refs: product_kernel(nparts, 16, *refs), grid_spec...  65.8 us
    pallas_call x3, Pallas kernels, input_call(): pl.pallas_call(lambda *refs: input_kernel(sub, *refs[:10], *refs[10 + len...  62.7 us
    unnamed x5, waiting for transfers between devices  59.2 us
    all_to_all x9, starting transfers between devices, zswap(): lax.all_to_all(blocks, 'row', 0, 0, tiled=True, axis_index_groups=same_core)  44.8 us
  transfers between devices with their start and end apart: 26, of which 21 were waited for; matrix products, arithmetic and copies ran while one was open for 3% of the time, Pallas kernels for 29%

profile of v6, /device:TPU:0, one launch (start us, length us, event | category | flops | bytes accessed | tf_op | source)
XLA Modules:
  0.0 1084.0 jit_solution(10700838182742999442)
XLA Ops:
  7.2 5.4 slice.54
  12.6 6.4 all-to-all-start
  20.3 1.2 fusion.2
  21.6 5.6 slice.55
  29.2 9.1 fusion.3
  38.3 85.5 %all-to-all-done = bf16[4,48,96,128]{3,2,1,0:T(8,128)(2,1)} async-done(((bf16[4,48,96,128]{3,2,1,0:T(8,128)(2,1)}), bf16[4,48,96,128]{3,2,1,0:T(8,128)(2,1)}, u32[]{:S(2)}, u32[]{:S(2)}) %all-to-all-start) | async-done | bytes 4718624 | tf_op jit(solution)/shard_map/all_to_all | solution.py:431
  123.8 4.9 all-to-all-start.1
  130.2 15.9 %edges.2 = (bf16[192,96,128]{2,1,0:T(8,128)(2,1)}, bf16[192,96,128]{2,1,0:T(8,128)(2,1)}) custom-call(bf16[192,96,128]{2,1,0:T(8,128)(2,1)} %bitcast.2.refs_0_, f32[4,128]{1,0:T(4,128)} %refs_6_.5, bf16[128,512]{1,0:T(8,128)(2,1)} %pad_maximum_fusion.1.refs_2_, f32[192,128]{1,0:T(8,128)} %broadcast_in_dim.60.refs_3_, f32[96,128]{1,0:T(8,128)} %broadcast_in_dim.62.refs_4_.refs_9_), custom_call_target="tpu_custom_call" | custom-call | flops 161999994880 | tf_op jit(solution)/shard_map/edges/pallas_call | solution.py:100
  146.2 1.2 fusion.1
  148.1 6.2 collective-permute-done.refs_3_
  154.4 32.7 %product.2 = bf16[4,192,96,128]{3,2,1,0:T(8,128)(2,1)} custom-call(s32[5]{0:T(128)} %stack.23.refs_0_, bf16[192,96,128]{2,1,0:T(8,128)(2,1)} %get-tuple-element.69.refs_1_, bf16[192,96,128]{2,1,0:T(8,128)(2,1)} %get-tuple-element.70.refs_2_, bf16[192,96,128]{2,1,0:T(8,128)(2,1)} %collective-permute-done.refs_3_), custom_call_target="tpu_custom_call" | custom-call | flops 17999998976 | tf_op jit(solution)/shard_map/product/pallas_call | solution.py:157
  187.1 45.5 %all-to-all-done.1 = bf16[4,48,96,128]{3,2,1,0:T(8,128)(2,1)} async-done(((bf16[4,48,96,128]{3,2,1,0:T(8,128)(2,1)}), bf16[4,48,96,128]{3,2,1,0:T(8,128)(2,1)}, u32[]{:S(2)}, u32[]{:S(2)}) %all-to-all-start.1) | async-done | bytes 4718624 | tf_op jit(solution)/shard_map/all_to_all | solution.py:431
  234.0 15.9 %edges.3 = (bf16[192,96,128]{2,1,0:T(8,128)(2,1)}, bf16[192,96,128]{2,1,0:T(8,128)(2,1)}) custom-call(bf16[192,96,128]{2,1,0:T(8,128)(2,1)} %bitcast.refs_0_, f32[4,128]{1,0:T(4,128)} %refs_6_.5, bf16[128,512]{1,0:T(8,128)(2,1)} %pad_maximum_fusion.1.refs_2_, f32[192,128]{1,0:T(8,128)} %broadcast_in_dim.64.refs_3_, f32[96,128]{1,0:T(8,128)} %broadcast_in_dim.66.refs_4_.refs_9_), custom_call_target="tpu_custom_call" | custom-call | flops 161999994880 | tf_op jit(solution)/shard_map/edges/pallas_call | solution.py:100
  249.9 5.1 all-to-all-start.2
  255.2 2.9 collective-permute-done.1.refs_3_
  258.2 33.1 %product.3 = bf16[4,192,96,128]{3,2,1,0:T(8,128)(2,1)} custom-call(s32[5]{0:T(128)} %stack.23.refs_0_, bf16[192,96,128]{2,1,0:T(8,128)(2,1)} %get-tuple-element.74.refs_1_, bf16[192,96,128]{2,1,0:T(8,128)(2,1)} %get-tuple-element.75.refs_2_, bf16[192,96,128]{2,1,0:T(8,128)(2,1)} %collective-permute-done.1.refs_3_), custom_call_target="tpu_custom_call" | custom-call | flops 198000001024 | tf_op jit(solution)/shard_map/product/pallas_call | solution.py:157
  291.3 69.0 %all-to-all-done.2 = bf16[4,48,96,128]{3,2,1,0:T(8,128)(2,1)} async-done(((bf16[4,48,96,128]{3,2,1,0:T(8,128)(2,1)}), bf16[4,48,96,128]{3,2,1,0:T(8,128)(2,1)}, u32[]{:S(2)}, u32[]{:S(2)}) %all-to-all-start.2) | async-done | bytes 4718624 | tf_op jit(solution)/shard_map/all_to_all | solution.py:431
  360.3 5.0 all-to-all-start.3
  365.3 21.9 %middle.3 = (bf16[192,96,128]{2,1,0:T(8,128)(2,1)}, bf16[192,96,128]{2,1,0:T(8,128)(2,1)}, bf16[192,96,128]{2,1,0:T(8,128)(2,1)}, f32[128,128]{1,0:T(8,128)}, f32[2,8,128]{2,1,0:T(8,128)}) custom-call(bf16[192,96,128]{2,1,0:T(8,128)(2,1)} %bitcast.2.refs_0_, bf16[192,96,128]{2,1,0:T(8,128)(2,1)} %bitcast.12.refs_1_, bf16[192,96,128]{2,1,0:T(8,128)(2,1)} %bitcast.87, ...), custom_call_target="tpu_custom_call" | custom-call | flops 240000008192 | tf_op jit(solution)/shard_map/middle/pallas_call | solution.py:217
  387.2 82.5 %all-to-all-done.3 = bf16[4,48,96,128]{3,2,1,0:T(8,128)(2,1)} async-done(((bf16[4,48,96,128]{3,2,1,0:T(8,128)(2,1)}), bf16[4,48,96,128]{3,2,1,0:T(8,128)(2,1)}, u32[]{:S(2)}, u32[]{:S(2)}) %all-to-all-start.3) | async-done | bytes 4718624 | tf_op jit(solution)/shard_map/all_to_all | solution.py:431
  469.7 4.9 all-to-all-start.4
  474.6 59.2 %reduce-scatter.9.cloned.1.call-done = bf16[1,192,96,128]{3,2,1,0:T(8,128)(2,1)} async-done(((bf16[4,192,96,128]{3,2,1,0:T(8,128)(2,1)}), bf16[1,192,96,128]{3,2,1,0:T(8,128)(2,1)}) %reduce-scatter.9.cloned.1.call-update) | async-done | bytes 4718608
  533.8 1.4 collective-permute-start.2
  535.8 21.8 %middle.2 = (bf16[192,96,128]{2,1,0:T(8,128)(2,1)}, bf16[192,96,128]{2,1,0:T(8,128)(2,1)}, bf16[192,96,128]{2,1,0:T(8,128)(2,1)}, f32[128,128]{1,0:T(8,128)}, f32[2,8,128]{2,1,0:T(8,128)}) custom-call(bf16[192,96,128]{2,1,0:T(8,128)(2,1)} %bitcast.refs_0_, bf16[192,96,128]{2,1,0:T(8,128)(2,1)} %bitcast.8.refs_1_, bf16[192,96,128]{2,1,0:T(8,128)(2,1)} %bitcast.88, ...), custom_call_target="tpu_custom_call" | custom-call | flops 240000008192 | tf_op jit(solution)/shard_map/middle/pallas_call | solution.py:217
  557.6 21.0 %all-to-all-done.4.refs_0_ = bf16[4,48,96,128]{3,2,1,0:T(8,128)(2,1)} async-done(((bf16[4,48,96,128]{3,2,1,0:T(8,128)(2,1)}), bf16[4,48,96,128]{3,2,1,0:T(8,128)(2,1)}, u32[]{:S(2)}, u32[]{:S(2)}) %all-to-all-start.4) | async-done | bytes 4718624 | tf_op jit(solution)/shard_map/all_to_all | solution.py:431
  578.6 5.0 all-to-all-start.5
  583.6 54.0 %collective-permute-done.2 = bf16[192,96,128]{2,1,0:T(8,128)(2,1)} collective-permute-done((bf16[192,96,128]{2,1,0:T(8,128)(2,1)}, bf16[192,96,128]{2,1,0:T(8,128)(2,1)}, u32[]{:S(2)}, u32[]{:S(2)}) %collective-permute-start.2) | collective-permute-done | bytes 4718624 | tf_op jit(solution)/shard_map/ppermute | solution.py:446
  637.6 1.1 collective-permute-done.3
  638.7 1.8 slice.64
  641.3 1.8 slice.65
  643.1 1.5 collective-permute-start.5
  644.6 47.8 %collective-permute-done.4 = bf16[96,96,128]{2,1,0:T(8,128)(2,1)S(1)} collective-permute-done((bf16[96,96,128]{2,1,0:T(8,128)(2,1)S(1)}, bf16[96,96,128]{2,1,0:T(8,128)(2,1)S(1)}, u32[]{:S(2)}, u32[]{:S(2)}) %collective-permute-start.4) | collective-permute-done | bytes 2359328 | tf_op jit(solution)/shard_map/ppermute | solution.py:446
  692.4 2.4 collective-permute-done.5
  695.5 51.0 %edge_grad.2 = (bf16[192,96,128]{2,1,0:T(8,128)(2,1)}, bf16[192,96,128]{2,1,0:T(8,128)(2,1)}, bf16[192,96,128]{2,1,0:T(8,128)(2,1)}) custom-call(s32[5]{0:T(128)} %stack.28.refs_0_, bf16[192,96,128]{2,1,0:T(8,128)(2,1)} %get-tuple-element.69.refs_1_, bf16[192,96,128]{2,1,0:T(8,128)(2,1)} %get-tuple-element.70.refs_2_, ...), custom_call_target="tpu_custom_call" | custom-call | flops 30000001024 | tf_op jit(solution)/shard_map/edge_grad/pallas_call | solution.py:299
  746.7 6.9 place.5
  753.6 6.9 place.6
  761.2 30.3 %input_grad.3 = (bf16[192,96,128]{2,1,0:T(8,128)(2,1)}, f32[128,640]{1,0:T(8,128)}, f32[2,8,128]{2,1,0:T(8,128)}) custom-call(bf16[192,96,128]{2,1,0:T(8,128)(2,1)} %bitcast.2.refs_0_, bf16[192,96,128]{2,1,0:T(8,128)(2,1)} %bitcast.12.refs_1_, bf16[192,96,128]{2,1,0:T(8,128)(2,1)} %get-tuple-element.90.refs_2_, ...), custom_call_target="tpu_custom_call" | custom-call | flops 30000001024 | tf_op jit(solution)/shard_map/input_grad/pallas_call | solution.py:373
  791.5 5.2 all-to-all-start.6
  796.8 74.1 %all-gather.3.cloned.1.call-done = bf16[768,96,128]{2,1,0:T(8,128)(2,1)} async-done(((bf16[192,96,128]{2,1,0:T(8,128)(2,1)}), bf16[768,96,128]{2,1,0:T(8,128)(2,1)}) %all-gather.3.cloned.1.call-update) | async-done | bytes 18874384 | tf_op jit(solution)/shard_map/all_gather | solution.py:531
  870.9 47.1 %edge_grad.3 = (bf16[192,96,128]{2,1,0:T(8,128)(2,1)}, bf16[192,96,128]{2,1,0:T(8,128)(2,1)}, bf16[192,96,128]{2,1,0:T(8,128)(2,1)}) custom-call(s32[5]{0:T(128)} %stack.23.refs_0_, bf16[192,96,128]{2,1,0:T(8,128)(2,1)} %get-tuple-element.74.refs_1_, bf16[192,96,128]{2,1,0:T(8,128)(2,1)} %get-tuple-element.75.refs_2_, ...), custom_call_target="tpu_custom_call" | custom-call | flops 30000001024 | tf_op jit(solution)/shard_map/edge_grad/pallas_call | solution.py:299
  921.2 0.9 copy.33
  922.1 4.1 collective-permute-done.7.refs_4_
  927.0 16.1 %input_grad.5 = (bf16[96,96,128]{2,1,0:T(8,128)(2,1)}, f32[128,640]{1,0:T(8,128)}, f32[2,8,128]{2,1,0:T(8,128)}) custom-call(bf16[192,96,128]{2,1,0:T(8,128)(2,1)} %bitcast.refs_0_, bf16[192,96,128]{2,1,0:T(8,128)(2,1)} %bitcast.8.refs_1_, bf16[192,96,128]{2,1,0:T(8,128)(2,1)} %get-tuple-element.99.refs_2_, ...), custom_call_target="tpu_custom_call" | custom-call | flops 161999994880 | tf_op jit(solution)/shard_map/input_grad/pallas_call | solution.py:373
  943.1 4.6 all-to-all-start.7
  947.8 16.3 %input_grad.4 = (bf16[96,96,128]{2,1,0:T(8,128)(2,1)}, f32[128,640]{1,0:T(8,128)}, f32[2,8,128]{2,1,0:T(8,128)}) custom-call(bf16[192,96,128]{2,1,0:T(8,128)(2,1)} %bitcast.refs_0_, bf16[192,96,128]{2,1,0:T(8,128)(2,1)} %bitcast.8.refs_1_, bf16[192,96,128]{2,1,0:T(8,128)(2,1)} %get-tuple-element.99.refs_2_, ...), custom_call_target="tpu_custom_call" | custom-call | flops 161999994880 | tf_op jit(solution)/shard_map/input_grad/pallas_call | solution.py:373
  964.4 1.1 copy.36
  967.0 1.4 collective-permute-done.8
  968.4 1.5 collective-permute-start.9
  969.9 5.6 collective-permute-done.9
  975.5 1.5 collective-permute-start.10
  977.0 4.8 collective-permute-done.10
  981.9 20.2 %all-to-all-done.7.refs_0_ = bf16[4,24,96,128]{3,2,1,0:T(8,128)(2,1)} async-done(((bf16[4,24,96,128]{3,2,1,0:T(8,128)(2,1)}), bf16[4,24,96,128]{3,2,1,0:T(8,128)(2,1)}, u32[]{:S(2)}, u32[]{:S(2)}) %all-to-all-start.7) | async-done | bytes 2359328 | tf_op jit(solution)/shard_map/all_to_all | solution.py:431
  1002.1 3.6 all-to-all-start.8
  1005.7 6.9 place.7
  1012.6 2.0 collective-permute-start.11
  1014.6 5.8 place.8
  1021.0 26.7 %collective-permute-done.11 = f32[386,128]{1,0:T(8,128)S(1)} collective-permute-done((f32[386,128]{1,0:T(8,128)S(1)}, f32[386,128]{1,0:T(8,128)S(1)}, u32[]{:S(2)}, u32[]{:S(2)}) %collective-permute-start.11) | collective-permute-done | bytes 197664 | tf_op jit(solution)/shard_map/ppermute | solution.py:471
  1047.8 4.7 collective-permute-start.12
  1052.4 12.1 %all-to-all-done.8.refs_0_ = bf16[4,24,96,128]{3,2,1,0:T(8,128)(2,1)S(1)} async-done(((bf16[4,24,96,128]{3,2,1,0:T(8,128)(2,1)}), bf16[4,24,96,128]{3,2,1,0:T(8,128)(2,1)S(1)}, u32[]{:S(2)}, u32[]{:S(2)}) %all-to-all-start.8) | async-done | bytes 2359328 | tf_op jit(solution)/shard_map/all_to_all | solution.py:431
  1064.5 1.4 copy-done
  1065.9 5.9 place.9
  1072.6 1.4 collective-permute-done.13
  1074.1 1.3 multiply_add_fusion.2
  1075.4 2.1 multiply_add_fusion
  (126 shorter events, 17.6 us)
Async XLA Ops:
  12.6 6.5 copy-start.13
  12.6 9.0 copy-start.3
  12.6 111.2 %all-to-all-start = ((bf16[4,48,96,128]{3,2,1,0:T(8,128)(2,1)}), bf16[4,48,96,128]{3,2,1,0:T(8,128)(2,1)}, u32[]{:S(2)}, u32[]{:S(2)}) async-start(bf16[4,48,96,128]{3,2,1,0:T(8,128)(2,1)} %slice.54), calls=%async_computation | async-start | bytes 9437184 | tf_op jit(solution)/shard_map/all_to_all | solution.py:431
  21.6 6.2 copy-start.1
  123.8 108.8 %all-to-all-start.1 = ((bf16[4,48,96,128]{3,2,1,0:T(8,128)(2,1)}), bf16[4,48,96,128]{3,2,1,0:T(8,128)(2,1)}, u32[]{:S(2)}, u32[]{:S(2)}) async-start(bf16[4,48,96,128]{3,2,1,0:T(8,128)(2,1)} %slice.55), calls=%async_computation.1 | async-start | bytes 9437184 | tf_op jit(solution)/shard_map/all_to_all | solution.py:431
  128.7 231.5 %reduce-scatter.7.cloned.1.call-start = ((), (), s32[]{:S(2)}) async-start(), calls=%async_computation.12 | async-start | bytes 23592960
  130.2 15.9 %copy-start.20 = (f32[384]{0:T(512)S(1)}, f32[384]{0:T(512)}, u32[]{:S(2)}) copy-start(f32[384]{0:T(512)} %get-tuple-element.124) | copy-start | bytes 4612
  146.1 8.3 collective-permute-start
  187.1 46.3 %copy-start.25 = (f32[96]{0:T(128)S(1)}, f32[96]{0:T(128)}, u32[]{:S(2)}) copy-start(f32[96]{0:T(128)} %get-tuple-element.146) | copy-start | bytes 1156
  249.9 8.3 collective-permute-start.1
  249.9 110.4 %all-to-all-start.2 = ((bf16[4,48,96,128]{3,2,1,0:T(8,128)(2,1)}), bf16[4,48,96,128]{3,2,1,0:T(8,128)(2,1)}, u32[]{:S(2)}, u32[]{:S(2)}) async-start(bf16[4,48,96,128]{3,2,1,0:T(8,128)(2,1)} %get-tuple-element.72), calls=%async_computation.2 | async-start | bytes 9437184 | tf_op jit(solution)/shard_map/all_to_all | solution.py:431
  255.0 278.8 %reduce-scatter.9.cloned.1.call-start = ((), (), s32[]{:S(2)}) async-start(), calls=%async_computation.13 | async-start | bytes 23592960
  360.3 109.4 %all-to-all-start.3 = ((bf16[4,48,96,128]{3,2,1,0:T(8,128)(2,1)}), bf16[4,48,96,128]{3,2,1,0:T(8,128)(2,1)}, u32[]{:S(2)}, u32[]{:S(2)}) async-start(bf16[4,48,96,128]{3,2,1,0:T(8,128)(2,1)} %get-tuple-element.73), calls=%async_computation.3 | async-start | bytes 9437184 | tf_op jit(solution)/shard_map/all_to_all | solution.py:431
  469.7 108.9 %all-to-all-start.4 = ((bf16[4,48,96,128]{3,2,1,0:T(8,128)(2,1)}), bf16[4,48,96,128]{3,2,1,0:T(8,128)(2,1)}, u32[]{:S(2)}, u32[]{:S(2)}) async-start(bf16[4,48,96,128]{3,2,1,0:T(8,128)(2,1)} %bitcast.70), calls=%async_computation.4 | async-start | bytes 9437184 | tf_op jit(solution)/shard_map/all_to_all | solution.py:431
  533.8 103.8 %collective-permute-start.2 = (bf16[192,96,128]{2,1,0:T(8,128)(2,1)}, bf16[192,96,128]{2,1,0:T(8,128)(2,1)}, u32[]{:S(2)}, u32[]{:S(2)}) collective-permute-start(bf16[192,96,128]{2,1,0:T(8,128)(2,1)} %get-tuple-element.86), channel_id=1, source_target_pairs={{0,1},{1,0},{2,3},{3,2},{4,5},{5,4},{6,7},{7,6},{8,9},{9,8},{10,11... | collective-permute-start | bytes 14155784 | tf_op jit(solution)/shard_map/ppermute | solution.py:446
  535.2 103.5 %collective-permute-start.3 = (bf16[192,96,128]{2,1,0:T(8,128)(2,1)}, bf16[192,96,128]{2,1,0:T(8,128)(2,1)}, u32[]{:S(2)}, u32[]{:S(2)}) collective-permute-start(bf16[192,96,128]{2,1,0:T(8,128)(2,1)} %get-tuple-element.86), channel_id=1, source_target_pairs={{0,2},{1,3},{2,0},{3,1},{4,6},{5,7},{6,4},{7,5},{8,10},{9,11},{10,... | collective-permute-start | bytes 14155784 | tf_op jit(solution)/shard_map/ppermute | solution.py:446
  578.6 116.2 %all-to-all-start.5 = ((bf16[4,48,96,128]{3,2,1,0:T(8,128)(2,1)}), bf16[4,48,96,128]{3,2,1,0:T(8,128)(2,1)}, u32[]{:S(2)}, u32[]{:S(2)}) async-start(bf16[4,48,96,128]{3,2,1,0:T(8,128)(2,1)} %bitcast.69), calls=%async_computation.5 | async-start | bytes 9437184 | tf_op jit(solution)/shard_map/all_to_all | solution.py:431
  583.6 287.3 %all-gather.3.cloned.1.call-start = ((), (), s32[]{:S(2)}) async-start(), calls=%async_computation.11 | async-start | bytes 23592960 | tf_op jit(solution)/shard_map/all_gather | solution.py:531
  640.6 51.8 %collective-permute-start.4 = (bf16[96,96,128]{2,1,0:T(8,128)(2,1)S(1)}, bf16[96,96,128]{2,1,0:T(8,128)(2,1)S(1)}, u32[]{:S(2)}, u32[]{:S(2)}) collective-permute-start(bf16[96,96,128]{2,1,0:T(8,128)(2,1)S(1)} %slice.64), channel_id=1, source_target_pairs={{0,1},{1,0},{2,3},{3,2},{4,5},{5,4},{6,7},{7,6},{8,9},{9,8},{10,11... | collective-permute-start | bytes 7077896 | tf_op jit(solution)/shard_map/ppermute | solution.py:446
  643.1 51.6 %collective-permute-start.5 = (bf16[96,96,128]{2,1,0:T(8,128)(2,1)S(1)}, bf16[96,96,128]{2,1,0:T(8,128)(2,1)}, u32[]{:S(2)}, u32[]{:S(2)}) collective-permute-start(bf16[96,96,128]{2,1,0:T(8,128)(2,1)S(1)} %slice.65), channel_id=1, source_target_pairs={{0,2},{1,3},{2,0},{3,1},{4,6},{5,7},{6,4},{7,5},{8,10},{9,11},{10,... | collective-permute-start | bytes 7077896 | tf_op jit(solution)/shard_map/ppermute | solution.py:446
  692.4 3.1 copy-start.28
  695.5 51.0 %copy-start.14 = (f32[4,1,48]{2,1,0:T(1,128)S(1)}, f32[4,1,48]{2,1,0:T(1,128)}, u32[]{:S(2)}) copy-start(f32[4,1,48]{2,1,0:T(1,128)} %get-tuple-element.135) | copy-start | bytes 2308
  695.5 51.1 %copy-start.2 = (bf16[6,128,128]{2,1,0:T(8,128)(2,1)S(1)}, bf16[6,128,128]{2,1,0:T(8,128)(2,1)}, u32[]{:S(2)}) copy-start(bf16[6,128,128]{2,1,0:T(8,128)(2,1)} %copy-done.1) | copy-start | bytes 589828
  746.5 14.0 %collective-permute-start.6 = (bf16[192,96,128]{2,1,0:T(8,128)(2,1)}, bf16[192,96,128]{2,1,0:T(8,128)(2,1)}, u32[]{:S(2)}, u32[]{:S(2)}) collective-permute-start(bf16[192,96,128]{2,1,0:T(8,128)(2,1)} %get-tuple-element.92), channel_id=1, source_target_pairs={{0,4},{4,0},{8,12},{12,8},{16,20},{20,16},{24,28},{28,24},{1,5},{5... | collective-permute-start | bytes 14155784 | tf_op jit(solution)/shard_map/ppermute | solution.py:434
  746.7 13.8 %copy-start.21 = (bf16[128,640]{1,0:T(8,128)(2,1)}, bf16[128,640]{1,0:T(8,128)(2,1)S(1)}, u32[]{:S(2)}) copy-start(bf16[128,640]{1,0:T(8,128)(2,1)S(1)} %constant_dynamic-update-slice_fusion.refs_7_) | copy-start | bytes 491524
  791.5 130.6 %all-to-all-start.6 = ((bf16[4,48,96,128]{3,2,1,0:T(8,128)(2,1)}), bf16[4,48,96,128]{3,2,1,0:T(8,128)(2,1)}, u32[]{:S(2)}, u32[]{:S(2)}) async-start(bf16[4,48,96,128]{3,2,1,0:T(8,128)(2,1)} %bitcast.68), calls=%async_computation.6 | async-start | bytes 9437184 | tf_op jit(solution)/shard_map/all_to_all | solution.py:431
  870.9 47.1 %copy-start.15 = (f32[4,1,48]{2,1,0:T(1,128)S(1)}, f32[4,1,48]{2,1,0:T(1,128)}, u32[]{:S(2)}) copy-start(f32[4,1,48]{2,1,0:T(1,128)} %get-tuple-element.133) | copy-start | bytes 2308
  870.9 48.4 %copy-start.16 = (f32[2,8,128]{2,1,0:T(8,128)S(1)}, f32[2,8,128]{2,1,0:T(8,128)}, u32[]{:S(2)}) copy-start(f32[2,8,128]{2,1,0:T(8,128)} %get-tuple-element.107) | copy-start | bytes 24580
  870.9 49.0 %copy-start.17 = (f32[2,8,128]{2,1,0:T(8,128)S(1)}, f32[2,8,128]{2,1,0:T(8,128)}, u32[]{:S(2)}) copy-start(f32[2,8,128]{2,1,0:T(8,128)} %get-tuple-element.111) | copy-start | bytes 24580
  870.9 49.6 %copy-start.7 = (f32[128,640]{1,0:T(8,128)S(1)}, f32[128,640]{1,0:T(8,128)}, u32[]{:S(2)}) copy-start(f32[128,640]{1,0:T(8,128)} %get-tuple-element.95) | copy-start | bytes 983044
  870.9 49.8 %copy-start.18 = (f32[2,8,128]{2,1,0:T(8,128)S(1)}, f32[2,8,128]{2,1,0:T(8,128)}, u32[]{:S(2)}) copy-start(f32[2,8,128]{2,1,0:T(8,128)} %get-tuple-element.96) | copy-start | bytes 24580
  918.0 8.3 collective-permute-start.7
  943.1 59.0 %all-to-all-start.7 = ((bf16[4,24,96,128]{3,2,1,0:T(8,128)(2,1)}), bf16[4,24,96,128]{3,2,1,0:T(8,128)(2,1)}, u32[]{:S(2)}, u32[]{:S(2)}) async-start(bf16[4,24,96,128]{3,2,1,0:T(8,128)(2,1)} %bitcast.72), calls=%async_computation.7 | async-start | bytes 4718592 | tf_op jit(solution)/shard_map/all_to_all | solution.py:431
  947.7 16.4 %copy-start.8 = (f32[128,640]{1,0:T(8,128)S(1)}, f32[128,640]{1,0:T(8,128)}, u32[]{:S(2)}) copy-start(f32[128,640]{1,0:T(8,128)} %get-tuple-element.108) | copy-start | bytes 983044
  947.7 16.7 %copy-start.19 = (f32[2,8,128]{2,1,0:T(8,128)S(1)}, f32[2,8,128]{2,1,0:T(8,128)}, u32[]{:S(2)}) copy-start(f32[2,8,128]{2,1,0:T(8,128)} %get-tuple-element.110) | copy-start | bytes 24580
  947.7 18.7 %copy-start.5 = (f32[5,128,128]{2,1,0:T(8,128)S(1)}, f32[5,128,128]{2,1,0:T(8,128)}, u32[]{:S(2)}) copy-start(f32[5,128,128]{2,1,0:T(8,128)} %copy.33) | copy-start | bytes 983044
  947.7 18.7 %copy-start.9 = (f32[128,128]{1,0:T(8,128)S(1)}, f32[128,128]{1,0:T(8,128)}, u32[]{:S(2)}) copy-start(f32[128,128]{1,0:T(8,128)} %get-tuple-element.106) | copy-start | bytes 196612
  947.7 18.7 %copy-start.10 = (f32[128,128]{1,0:T(8,128)S(1)}, f32[128,128]{1,0:T(8,128)}, u32[]{:S(2)}) copy-start(f32[128,128]{1,0:T(8,128)} %get-tuple-element.109) | copy-start | bytes 196612
  947.7 18.7 %copy-start.11 = (f32[772]{0:T(1024)S(1)}, f32[772]{0:T(1024)}, u32[]{:S(2)}) copy-start(f32[772]{0:T(1024)} %pad.3.clone) | copy-start | bytes 9268
  947.8 18.7 %copy-start.12 = (f32[772]{0:T(1024)S(1)}, f32[772]{0:T(1024)}, u32[]{:S(2)}) copy-start(f32[772]{0:T(1024)} %pad.5.clone) | copy-start | bytes 9268
  947.8 18.7 %copy-start.22 = (f32[2,128]{1,0:T(2,128)S(1)}, f32[2,128]{1,0:T(2,128)}, u32[]{:S(2)}) copy-start(f32[2,128]{1,0:T(2,128)} %reduce_sum.46) | copy-start | bytes 3076
  947.8 18.7 %copy-start.23 = (f32[2,128]{1,0:T(2,128)S(1)}, f32[2,128]{1,0:T(2,128)}, u32[]{:S(2)}) copy-start(f32[2,128]{1,0:T(2,128)} %reduce_sum.48) | copy-start | bytes 3076
  947.8 18.7 %copy-start.24 = (f32[2,128]{1,0:T(2,128)S(1)}, f32[2,128]{1,0:T(2,128)}, u32[]{:S(2)}) copy-start(f32[2,128]{1,0:T(2,128)} %reduce_sum.45) | copy-start | bytes 3076
  966.8 1.5 collective-permute-start.8
  968.4 7.1 collective-permute-start.9
  975.5 6.4 collective-permute-start.10
  1002.1 62.4 %all-to-all-start.8 = ((bf16[4,24,96,128]{3,2,1,0:T(8,128)(2,1)}), bf16[4,24,96,128]{3,2,1,0:T(8,128)(2,1)S(1)}, u32[]{:S(2)}, u32[]{:S(2)}) async-start(bf16[4,24,96,128]{3,2,1,0:T(8,128)(2,1)} %bitcast.71), calls=%async_computation.8 | async-start | bytes 4718592 | tf_op jit(solution)/shard_map/all_to_all | solution.py:431
  1012.6 35.2 %collective-permute-start.11 = (f32[386,128]{1,0:T(8,128)S(1)}, f32[386,128]{1,0:T(8,128)S(1)}, u32[]{:S(2)}, u32[]{:S(2)}) collective-permute-start(f32[386,128]{1,0:T(8,128)S(1)} %add.107), channel_id=1, source_target_pairs={{0,8},{4,12},{8,0},{12,4},{16,24},{20,28},{24,16},{28,20},{1,9},{5... | collective-permute-start | bytes 592904 | tf_op jit(solution)/shard_map/ppermute | solution.py:471
  1047.8 24.7 %collective-permute-start.12 = (f32[386,128]{1,0:T(8,128)S(1)}, f32[386,128]{1,0:T(8,128)S(1)}, u32[]{:S(2)}, u32[]{:S(2)}) collective-permute-start(f32[386,128]{1,0:T(8,128)S(1)} %add_add_fusion.1), channel_id=1, source_target_pairs={{0,16},{4,20},{8,24},{12,28},{16,0},{20,4},{24,8},{28,12},{1,17},{... | collective-permute-start | bytes 592904 | tf_op jit(solution)/shard_map/ppermute | solution.py:471
  1064.5 1.4 copy-start
  1065.9 8.2 copy-start.26
  1065.9 8.2 copy-start.27
  1065.9 9.5 copy-start.4
  1065.9 9.5 copy-start.6
  1072.5 1.5 collective-permute-start.13
Sparse Core Ops, SparseCore 0:
  187.2 172.2 reduce-scatter.6
  362.9 170.8 reduce-scatter.8
  694.9 175.9 all-gather.2
